TPU v7x, 32 devices: a whole 2x2x4 slice. The times are simulated.
32 devices in a mesh: dp: 4 (over x, core), row: 4 (over z), col: 2 (over y).
Axes of the slice: x: 2, y: 2, z: 4, core: 2. Of those that a mesh axis runs over, the one named last changes fastest.
Arguments:
- tokens: bfloat16 [2, 10240, 2048], P(None, ('dp', 'row'), 'col'), may hold values from -6 to 6
- out_grad: bfloat16 [2, 10240, 2048], P(None, ('dp', 'row'), 'col'), may hold values from -6 to 6
- path: int32 [2, 10240, 3], P(None, 'dp'), may hold values from 0 to 103, as said below
- positions: int32 [2, 10240], P(None, 'dp'), may hold values from 0 to 1343, as said below
- w_query: bfloat16 [2048, 2048], P('col', 'row'), may hold values from -0.125 to 0.125
- w_key: bfloat16 [2048, 1024], P('col', 'row'), may hold values from -0.125 to 0.125
- w_value: bfloat16 [2048, 1024], P('col', 'row'), may hold values from -0.125 to 0.125
- w_out: bfloat16 [2048, 2048], P('row', 'col'), may hold values from -1.5 to 1.5
- w_gate: bfloat16 [2048, 8192], P('col', 'row'), may hold values from -0.125 to 0.125
- w_up: bfloat16 [2048, 8192], P('col', 'row'), may hold values from -0.125 to 0.125
- w_down: bfloat16 [8192, 2048], P('row', 'col'), may hold values from -0.0625 to 0.0625
- gain_attn: float32 [2048], P('col'), may hold values from 0.25 to 1.75
- gain_ffn: float32 [2048], P('col'), may hold values from 0.25 to 1.75
Outputs:
- output: bfloat16 [2, 10240, 2048], P(None, ('dp', 'row'), 'col')
- token_grad: bfloat16 [2, 10240, 2048], P(None, ('dp', 'row'), 'col')
- w_query_grad: float32 [2048, 2048], P('col', 'row')
- w_key_grad: float32 [2048, 1024], P('col', 'row')
- w_value_grad: float32 [2048, 1024], P('col', 'row')
- w_out_grad: float32 [2048, 2048], P('row', 'col')
- w_gate_grad: float32 [2048, 8192], P('col', 'row')
- w_up_grad: float32 [2048, 8192], P('col', 'row')
- w_down_grad: float32 [8192, 2048], P('row', 'col')
- gain_attn_grad: float32 [2048], P('col')
- gain_ffn_grad: float32 [2048], P('col')
Inputs may be any that keep to these rules, and one draw needn't show every extreme that they name: Each tree fills 2560 consecutive tokens of a micro-batch, one tree for each index of dp: a trunk of 1024 tokens, then 4 branches of 128 tokens, each a child of the trunk, then 8 leaves, leaf j a child of branch j // 2, of 64 to 192 tokens that sum to 1024; leaf 0 has exactly 192 tokens and leaf 4 exactly 64. path holds a token's segment label, its parent's and its grandparent's, repeating the top label where there is none; each of the 13 segments of a tree has its own label, and labels of different trees differ. `positions`: A trunk token's position is its index in the trunk, a branch token's 1024 plus its index in the branch, a leaf token's 1024 + 128 plus its index in the leaf.
All inputs are finite; a program needn't handle non-finite values.
Results may differ from a plain program's by a relative error of at most 0.02.
Values may be sent and summed in bfloat16 or wider, within the bound.
No kernel may reach another device: no remote copies, remote signals or barrier semaphores. Data moves between devices by JAX's collectives and lax.ppermute only.
A program may use at most 448 MiB of HBM per device.

v0:
```python
import math

import jax
import jax.numpy as jnp
from jax import lax
from jax.sharding import PartitionSpec as P

D = 2048
HEADS = 16
KV_HEADS = 8
HEAD = 128


EPSILON = 1e-05
THETA = 1000000.0


def contract_rows(left, right):
    return lax.dot_general(
        left, right, (((0,), (0,)), ((), ())), preferred_element_type=jnp.float32
    )


def contract_cols(left, right):
    return lax.dot_general(
        left, right, (((1,), (1,)), ((), ())), preferred_element_type=jnp.float32
    )


def rows_gather(values):
    return lax.all_gather(values, "row", axis=0, tiled=True)


def cols_gather(values):
    return lax.all_gather(values, "col", axis=0, tiled=True)


def cols_reduce(part_fn, rows):
    return lax.psum_scatter(
        part_fn(jnp.int32(0), rows * lax.axis_size("col")), "col", scatter_dimension=0, tiled=True
    )


def rows_reduce(part_fn, rows):
    return lax.psum_scatter(
        part_fn(jnp.int32(0), rows * lax.axis_size("row")).astype(jnp.bfloat16),
        "row",
        scatter_dimension=0,
        tiled=True,
    ).astype(jnp.float32)


def feature_sums(values):
    return lax.psum(jnp.sum(values, axis=1), "col")


def sliced_product(whole, weight, transpose):

    def part_fn(start, count):
        if transpose:
            return contract_cols(whole, weight)
        return jnp.dot(whole, weight, preferred_element_type=jnp.float32)

    return part_fn


def rope_tables(positions):
    half = HEAD // 2
    frequency = jnp.power(THETA, -2.0 * jnp.arange(half, dtype=jnp.float32) / HEAD)
    angles = positions.astype(jnp.float32)[:, None] * frequency[None, :]
    angles = jnp.concatenate([angles, angles], axis=1)
    return (jnp.cos(angles), jnp.sin(angles))


def rotate(values, cosine, sine):
    half = values.shape[-1] // 2
    turned = jnp.concatenate([-values[..., half:], values[..., :half]], axis=-1)
    return values * cosine[:, None, :] + turned * sine[:, None, :]


def rotate_back(grads, cosine, sine):
    half = grads.shape[-1] // 2
    scaled = grads * sine[:, None, :]
    turned = jnp.concatenate([scaled[..., half:], -scaled[..., :half]], axis=-1)
    return grads * cosine[:, None, :] + turned


def norm_forward(values, gain):
    ratio = lax.rsqrt(feature_sums(values * values) / D + EPSILON)[:, None]
    normed = values * ratio
    return (ratio, normed, (normed * gain).astype(jnp.bfloat16))


def norm_backward(grad, ratio, normed, gain):
    scaled = grad * gain
    inner = feature_sums(scaled * normed)[:, None] / D
    return (ratio * (scaled - normed * inner), jnp.sum(grad * normed, axis=0))


def body(
    tokens,
    out_grad,
    path,
    positions,
    w_query,
    w_key,
    w_value,
    w_out,
    w_gate,
    w_up,
    w_down,
    gain_attn,
    gain_ffn,
):
    query_width = w_query.shape[1]
    key_width = w_key.shape[1]
    hidden_width = w_gate.shape[1]
    local_heads = key_width // HEAD
    group = HEADS // KV_HEADS
    scale = 1.0 / math.sqrt(HEAD)
    block_rows = path.shape[1]
    local_rows = tokens.shape[1]
    query_rows = block_rows // lax.axis_size("col")
    first = lax.axis_index("col") * query_rows
    w_project = jnp.concatenate([w_query, w_key, w_value], axis=1)
    w_pair = jnp.concatenate([w_gate, w_up], axis=1)
    project_start = jnp.zeros(w_project.shape, jnp.float32)
    pair_start = jnp.zeros(w_pair.shape, jnp.float32)
    down_start = jnp.zeros(w_down.shape, jnp.float32)

    def micro_step(carry, batch):
        grad_project, grad_out, grad_pair, grad_down, grad_gain_attn, grad_gain_ffn = carry
        block, cotangent, block_path, block_place = batch
        inputs = block.astype(jnp.float32)
        cosine, sine = rope_tables(lax.dynamic_slice_in_dim(block_place, first, query_rows, 0))
        query_path = lax.dynamic_slice_in_dim(block_path, first, query_rows, 0)
        key_labels = block_path[:, 0]
        query_place = first + jnp.arange(query_rows, dtype=jnp.int32)
        key_place = jnp.arange(block_rows, dtype=jnp.int32)
        same_path = (
            (key_labels[None, :] == query_path[:, 0:1])
            | (key_labels[None, :] == query_path[:, 1:2])
            | (key_labels[None, :] == query_path[:, 2:3])
        )
        visible = same_path & (key_place[None, :] <= query_place[:, None])
        ratio_attn, normed_attn, input_attn = norm_forward(inputs, gain_attn)
        gathered_attn = rows_gather(input_attn)
        projected = cols_reduce(sliced_product(gathered_attn, w_project, False), query_rows)
        query = rotate(
            projected[:, :query_width].reshape(query_rows, -1, HEAD), cosine, sine
        ).astype(jnp.bfloat16)
        keys = rotate(
            projected[:, query_width : query_width + key_width].reshape(query_rows, -1, HEAD),
            cosine,
            sine,
        ).astype(jnp.bfloat16)
        values = projected[:, query_width + key_width :].astype(jnp.bfloat16)
        keys_all, values_all = (
            lax.all_gather(keys.reshape(query_rows, key_width), "col", axis=0, tiled=True),
            lax.all_gather(values, "col", axis=0, tiled=True),
        )
        query_groups = query.reshape(query_rows, local_heads, group, HEAD)
        key_heads = keys_all.reshape(block_rows, local_heads, HEAD)
        value_heads = values_all.reshape(block_rows, local_heads, HEAD)
        scores = (
            jnp.einsum(
                "ikgd,jkd->kgij", query_groups, key_heads, preferred_element_type=jnp.float32
            )
            * scale
        )
        scores = jnp.where(visible[None, None], scores, -jnp.inf)
        weights = jax.nn.softmax(scores, axis=-1)
        weights_low = weights.astype(jnp.bfloat16)
        mixed = jnp.einsum(
            "kgij,jkd->ikgd", weights_low, value_heads, preferred_element_type=jnp.float32
        )
        attn_low = mixed.reshape(query_rows, query_width).astype(jnp.bfloat16)
        attn_all = cols_gather(attn_low)
        branch_attn = rows_reduce(sliced_product(attn_all, w_out, False), local_rows)
        middle = inputs + branch_attn
        ratio_ffn, normed_ffn, input_ffn = norm_forward(middle, gain_ffn)
        gathered_ffn = rows_gather(input_ffn)
        pair = cols_reduce(sliced_product(gathered_ffn, w_pair, False), query_rows)
        gate = pair[:, :hidden_width]
        upper = pair[:, hidden_width:]
        sigma = jax.nn.sigmoid(gate)
        silu_value = gate * sigma
        hidden = (silu_value * upper).astype(jnp.bfloat16)
        hidden_all = cols_gather(hidden)
        branch_ffn = rows_reduce(sliced_product(hidden_all, w_down, False), local_rows)
        output = (middle + branch_ffn).astype(jnp.bfloat16)
        cotangent_all = rows_gather(cotangent)
        hidden_grad = cols_reduce(sliced_product(cotangent_all, w_down, True), query_rows)
        grad_down = grad_down + contract_rows(hidden_all, cotangent_all)
        gate_grad = hidden_grad * upper * sigma * (1.0 + gate * (1.0 - sigma))
        upper_grad = hidden_grad * silu_value
        pair_grad = jnp.concatenate([gate_grad, upper_grad], axis=1).astype(jnp.bfloat16)
        pair_all = cols_gather(pair_grad)
        normed_ffn_grad = rows_reduce(sliced_product(pair_all, w_pair, True), local_rows)
        grad_pair = grad_pair + contract_rows(gathered_ffn, pair_all)
        middle_back, gain_ffn_step = norm_backward(normed_ffn_grad, ratio_ffn, normed_ffn, gain_ffn)
        middle_grad = cotangent.astype(jnp.float32) + middle_back
        middle_low = middle_grad.astype(jnp.bfloat16)
        middle_all = rows_gather(middle_low)
        attn_grad = cols_reduce(sliced_product(middle_all, w_out, True), query_rows).astype(
            jnp.bfloat16
        )
        grad_out = grad_out + contract_rows(attn_all, middle_all)
        attn_heads = attn_grad.reshape(query_rows, local_heads, group, HEAD)
        weight_grad = jnp.einsum(
            "ikgd,jkd->kgij", attn_heads, value_heads, preferred_element_type=jnp.float32
        )
        score_grad = (
            weights * (weight_grad - jnp.sum(weights * weight_grad, axis=-1, keepdims=True))
        ).astype(jnp.bfloat16)
        query_grad = (
            jnp.einsum("kgij,jkd->ikgd", score_grad, key_heads, preferred_element_type=jnp.float32)
            * scale
        )
        key_part = (
            jnp.einsum(
                "kgij,ikgd->jkd", score_grad, query_groups, preferred_element_type=jnp.float32
            )
            * scale
        )
        value_part = jnp.einsum(
            "kgij,ikgd->jkd", weights_low, attn_heads, preferred_element_type=jnp.float32
        )
        key_grad, value_grad = (
            lax.psum_scatter(
                key_part.reshape(block_rows, key_width).astype(jnp.bfloat16),
                "col",
                scatter_dimension=0,
                tiled=True,
            ).astype(jnp.float32),
            lax.psum_scatter(
                value_part.reshape(block_rows, key_width).astype(jnp.bfloat16),
                "col",
                scatter_dimension=0,
                tiled=True,
            ).astype(jnp.float32),
        )
        query_back = rotate_back(query_grad.reshape(query_rows, -1, HEAD), cosine, sine).reshape(
            query_rows, query_width
        )
        key_back = rotate_back(key_grad.reshape(query_rows, -1, HEAD), cosine, sine).reshape(
            query_rows, key_width
        )
        projected_grad = jnp.concatenate([query_back, key_back, value_grad], axis=1).astype(
            jnp.bfloat16
        )
        projected_all = cols_gather(projected_grad)
        normed_attn_grad = rows_reduce(sliced_product(projected_all, w_project, True), local_rows)
        grad_project = grad_project + contract_rows(gathered_attn, projected_all)
        input_back, gain_attn_step = norm_backward(
            normed_attn_grad, ratio_attn, normed_attn, gain_attn
        )
        input_grad = (middle_grad + input_back).astype(jnp.bfloat16)
        carry = (
            grad_project,
            grad_out,
            grad_pair,
            grad_down,
            grad_gain_attn + gain_attn_step,
            grad_gain_ffn + gain_ffn_step,
        )
        return (carry, (output, input_grad))

    start = (
        project_start,
        jnp.zeros(w_out.shape, jnp.float32),
        pair_start,
        down_start,
        jnp.zeros(gain_attn.shape, jnp.float32),
        jnp.zeros(gain_ffn.shape, jnp.float32),
    )
    sums, (outputs, input_grads) = lax.scan(micro_step, start, (tokens, out_grad, path, positions))
    grad_project, grad_out, grad_pair, grad_down, grad_gain_attn, grad_gain_ffn = sums
    grad_project, grad_out, grad_pair, grad_down = (
        lax.psum(grad_project.astype(jnp.bfloat16), "dp").astype(jnp.float32),
        lax.psum(grad_out.astype(jnp.bfloat16), "dp").astype(jnp.float32),
        lax.psum(grad_pair.astype(jnp.bfloat16), "dp").astype(jnp.float32),
        lax.psum(grad_down.astype(jnp.bfloat16), "dp").astype(jnp.float32),
    )
    grad_gain_attn, grad_gain_ffn = lax.psum((grad_gain_attn, grad_gain_ffn), ("dp", "row"))
    query_part = grad_project[:, :query_width]
    key_part_grad = grad_project[:, query_width : query_width + key_width]
    value_part_grad = grad_project[:, query_width + key_width :]
    return (
        outputs,
        input_grads,
        query_part,
        key_part_grad,
        value_part_grad,
        grad_out,
        grad_pair[:, :hidden_width],
        grad_pair[:, hidden_width:],
        grad_down,
        grad_gain_attn,
        grad_gain_ffn,
    )


def solution(mesh):
    in_specs = (
        P(None, ("dp", "row"), "col"),
        P(None, ("dp", "row"), "col"),
        P(None, "dp", None),
        P(None, "dp"),
        P("col", "row"),
        P("col", "row"),
        P("col", "row"),
        P("row", "col"),
        P("col", "row"),
        P("col", "row"),
        P("row", "col"),
        P("col"),
        P("col"),
    )
    out_specs = (
        P(None, ("dp", "row"), "col"),
        P(None, ("dp", "row"), "col"),
        P("col", "row"),
        P("col", "row"),
        P("col", "row"),
        P("row", "col"),
        P("col", "row"),
        P("col", "row"),
        P("row", "col"),
        P("col"),
        P("col"),
    )
    return jax.shard_map(body, mesh=mesh, in_specs=in_specs, out_specs=out_specs, check_vma=False)
```

profile of v0, /device:TPU:0, one launch (start us, length us, event | category | flops | bytes accessed | tf_op | source)
XLA Modules:
  0.0 6259.9 jit_solution(6269722309973987769)
XLA Ops:
  20.2 5917.6 %while.28 = (s32[]{:T(128)}, f32[1024,1024]{1,0:T(8,128)}, f32[512,1024]{1,0:T(8,128)}, f32[1024,4096]{1,0:T(8,128)}, f32[2048,1024]{1,0:T(8,128)}, /*index=5*/f...) while((s32[]{:T(128)}, f32[1024,1024]{1,0:T(8,128)}, ...), condition=%wide.region_24.25_spmd.clone, body=%wide.region_0.24_spmd.clone.sunk | while | flops 141314211840 | bytes 1911300864 | solution.py:277
  29.4 99.9 %all-gather.15.cloned.1.call-done = bf16[2560,1024]{1,0:T(8,128)(2,1)} async-done(((bf16[640,1024]{1,0:T(8,128)(2,1)}), bf16[2560,1024]{1,0:T(8,128)(2,1)}) %all-gather.15.cloned.1.call-update) | async-done | bytes 5242896 | tf_op jit(solution)/shard_map/while/body/eval_jaxpr/all_gather | solution.py:31
  148.3 112.5 %reduce-scatter.12.cloned.1.call-done = f32[1280,1024]{1,0:T(8,128)} async-done(((f32[2560,1024]{1,0:T(8,128)}), f32[1280,1024]{1,0:T(8,128)}) %reduce-scatter.12.cloned.1.call-update) | async-done | bytes 5242896 | tf_op jit(solution)/shard_map/while/body/eval_jaxpr/reduce_scatter | solution.py:39
  408.1 91.3 %reduce-scatter.14.cloned.1.call-done = bf16[640,1024]{1,0:T(8,128)(2,1)} async-done(((bf16[2560,1024]{1,0:T(8,128)(2,1)}), bf16[640,1024]{1,0:T(8,128)(2,1)}) %reduce-scatter.14.cloned.1.call-update) | async-done | bytes 1310736 | tf_op jit(solution)/shard_map/while/body/eval_jaxpr/reduce_scatter | solution.py:45
  509.8 89.8 %all-gather.17.cloned.1.call-done = bf16[1,2560,1024]{2,1,0:T(8,128)(2,1)} async-done(((bf16[1,640,1024]{2,1,0:T(8,128)(2,1)}), bf16[1,2560,1024]{2,1,0:T(8,128)(2,1)}) %all-gather.17.cloned.1.call-update) | async-done | bytes 5242896 | tf_op jit(solution)/shard_map/while/body/eval_jaxpr/all_gather | solution.py:31
  618.1 80.2 %all-gather.25.cloned.1.call-done = bf16[2560,1024]{1,0:T(8,128)(2,1)} async-done(((bf16[640,1024]{1,0:T(8,128)(2,1)}), bf16[2560,1024]{1,0:T(8,128)(2,1)}) %all-gather.25.cloned.1.call-update) | async-done | bytes 5242896 | tf_op jit(solution)/shard_map/while/body/eval_jaxpr/all_gather | solution.py:31
  729.7 203.5 %reduce-scatter.10.cloned.1.call-done = f32[1280,2048]{1,0:T(8,128)} async-done(((f32[2560,2048]{1,0:T(8,128)}), f32[1280,2048]{1,0:T(8,128)}) %reduce-scatter.10.cloned.1.call-update) | async-done | bytes 10485776 | tf_op jit(solution)/shard_map/while/body/eval_jaxpr/reduce_scatter | solution.py:39
  933.2 919.8 %all-reduce.10.cloned.1.call-done = f32[2560,4096]{1,0:T(8,128)} async-done(((f32[2560,4096]{1,0:T(8,128)}), f32[2560,4096]{1,0:T(8,128)}) %all-reduce.10.cloned.1.call-update) | async-done | bytes 41943056 | tf_op jit(solution)/shard_map/while
  1873.3 248.2 %all-gather.27.cloned.1.call-done = bf16[2560,4096]{1,0:T(8,128)(2,1)} async-done(((bf16[1280,4096]{1,0:T(8,128)(2,1)}), bf16[2560,4096]{1,0:T(8,128)(2,1)}) %all-gather.27.cloned.1.call-update) | async-done | bytes 20971536 | tf_op jit(solution)/shard_map/while/body/eval_jaxpr/all_gather | solution.py:35
  2150.0 93.9 %reduce-scatter.16.cloned.1.call-done = bf16[640,1024]{1,0:T(8,128)(2,1)} async-done(((bf16[2560,1024]{1,0:T(8,128)(2,1)}), bf16[640,1024]{1,0:T(8,128)(2,1)}) %reduce-scatter.16.cloned.1.call-update) | async-done | bytes 1310736 | tf_op jit(solution)/shard_map/while/body/eval_jaxpr/reduce_scatter | solution.py:45
  2256.4 98.7 %all-gather.29.cloned.1.call-done = bf16[2560,1024]{1,0:T(8,128)(2,1)} async-done(((bf16[640,1024]{1,0:T(8,128)(2,1)}), bf16[2560,1024]{1,0:T(8,128)(2,1)}) %all-gather.29.cloned.1.call-update) | async-done | bytes 5242896 | tf_op jit(solution)/shard_map/while/body/eval_jaxpr/all_gather | solution.py:31
  2363.4 63.9 %reduce-scatter.18.cloned.1.call-done = f32[1280,512]{1,0:T(8,128)} async-done(((f32[2560,512]{1,0:T(8,128)}), f32[1280,512]{1,0:T(8,128)}) %reduce-scatter.18.cloned.1.call-update) | async-done | bytes 2621456 | tf_op jit(solution)/shard_map/while/body/eval_jaxpr/reduce_scatter | solution.py:39
  2464.5 41.5 fusion.218
  2579.3 68.1 %all-gather.31.cloned.1.call-done = bf16[2560,1024]{0,1:T(8,128)(2,1)} async-done(((bf16[1280,1024]{0,1:T(8,128)(2,1)}), bf16[2560,1024]{0,1:T(8,128)(2,1)}) %all-gather.31.cloned.1.call-update) | async-done | bytes 5242896 | tf_op jit(solution)/shard_map/while/body/eval_jaxpr/all_gather | solution.py:35
  2657.6 121.4 %all-gather.33.cloned.1.call-done = bf16[2560,2048]{1,0:T(8,128)(2,1)} async-done(((bf16[1280,2048]{1,0:T(8,128)(2,1)}), bf16[2560,2048]{1,0:T(8,128)(2,1)}) %all-gather.33.cloned.1.call-update) | async-done | bytes 10485776 | tf_op jit(solution)/shard_map/while/body/eval_jaxpr/all_gather | solution.py:35
  2882.5 89.9 %reduce-scatter.26.cloned.1.call-done = bf16[640,1024]{1,0:T(8,128)(2,1)} async-done(((bf16[2560,1024]{1,0:T(8,128)(2,1)}), bf16[640,1024]{1,0:T(8,128)(2,1)}) %reduce-scatter.26.cloned.1.call-update) | async-done | bytes 1310736 | tf_op jit(solution)/shard_map/while/body/eval_jaxpr/reduce_scatter | solution.py:45
  2986.5 98.7 %all-gather.15.cloned.1.call-done = bf16[2560,1024]{1,0:T(8,128)(2,1)} async-done(((bf16[640,1024]{1,0:T(8,128)(2,1)}), bf16[2560,1024]{1,0:T(8,128)(2,1)}) %all-gather.15.cloned.1.call-update) | async-done | bytes 5242896 | tf_op jit(solution)/shard_map/while/body/eval_jaxpr/all_gather | solution.py:31
  3104.1 112.5 %reduce-scatter.12.cloned.1.call-done = f32[1280,1024]{1,0:T(8,128)} async-done(((f32[2560,1024]{1,0:T(8,128)}), f32[1280,1024]{1,0:T(8,128)}) %reduce-scatter.12.cloned.1.call-update) | async-done | bytes 5242896 | tf_op jit(solution)/shard_map/while/body/eval_jaxpr/reduce_scatter | solution.py:39
  3364.0 91.3 %reduce-scatter.14.cloned.1.call-done = bf16[640,1024]{1,0:T(8,128)(2,1)} async-done(((bf16[2560,1024]{1,0:T(8,128)(2,1)}), bf16[640,1024]{1,0:T(8,128)(2,1)}) %reduce-scatter.14.cloned.1.call-update) | async-done | bytes 1310736 | tf_op jit(solution)/shard_map/while/body/eval_jaxpr/reduce_scatter | solution.py:45
  3465.7 89.6 %all-gather.17.cloned.1.call-done = bf16[1,2560,1024]{2,1,0:T(8,128)(2,1)} async-done(((bf16[1,640,1024]{2,1,0:T(8,128)(2,1)}), bf16[1,2560,1024]{2,1,0:T(8,128)(2,1)}) %all-gather.17.cloned.1.call-update) | async-done | bytes 5242896 | tf_op jit(solution)/shard_map/while/body/eval_jaxpr/all_gather | solution.py:31
  3574.0 79.9 %all-gather.25.cloned.1.call-done = bf16[2560,1024]{1,0:T(8,128)(2,1)} async-done(((bf16[640,1024]{1,0:T(8,128)(2,1)}), bf16[2560,1024]{1,0:T(8,128)(2,1)}) %all-gather.25.cloned.1.call-update) | async-done | bytes 5242896 | tf_op jit(solution)/shard_map/while/body/eval_jaxpr/all_gather | solution.py:31
  3685.4 203.5 %reduce-scatter.10.cloned.1.call-done = f32[1280,2048]{1,0:T(8,128)} async-done(((f32[2560,2048]{1,0:T(8,128)}), f32[1280,2048]{1,0:T(8,128)}) %reduce-scatter.10.cloned.1.call-update) | async-done | bytes 10485776 | tf_op jit(solution)/shard_map/while/body/eval_jaxpr/reduce_scatter | solution.py:39
  3888.8 919.8 %all-reduce.10.cloned.1.call-done = f32[2560,4096]{1,0:T(8,128)} async-done(((f32[2560,4096]{1,0:T(8,128)}), f32[2560,4096]{1,0:T(8,128)}) %all-reduce.10.cloned.1.call-update) | async-done | bytes 41943056 | tf_op jit(solution)/shard_map/while
  4828.9 248.3 %all-gather.27.cloned.1.call-done = bf16[2560,4096]{1,0:T(8,128)(2,1)} async-done(((bf16[1280,4096]{1,0:T(8,128)(2,1)}), bf16[2560,4096]{1,0:T(8,128)(2,1)}) %all-gather.27.cloned.1.call-update) | async-done | bytes 20971536 | tf_op jit(solution)/shard_map/while/body/eval_jaxpr/all_gather | solution.py:35
  5105.7 93.9 %reduce-scatter.16.cloned.1.call-done = bf16[640,1024]{1,0:T(8,128)(2,1)} async-done(((bf16[2560,1024]{1,0:T(8,128)(2,1)}), bf16[640,1024]{1,0:T(8,128)(2,1)}) %reduce-scatter.16.cloned.1.call-update) | async-done | bytes 1310736 | tf_op jit(solution)/shard_map/while/body/eval_jaxpr/reduce_scatter | solution.py:45
  5212.1 98.7 %all-gather.29.cloned.1.call-done = bf16[2560,1024]{1,0:T(8,128)(2,1)} async-done(((bf16[640,1024]{1,0:T(8,128)(2,1)}), bf16[2560,1024]{1,0:T(8,128)(2,1)}) %all-gather.29.cloned.1.call-update) | async-done | bytes 5242896 | tf_op jit(solution)/shard_map/while/body/eval_jaxpr/all_gather | solution.py:31
  5319.1 63.9 %reduce-scatter.18.cloned.1.call-done = f32[1280,512]{1,0:T(8,128)} async-done(((f32[2560,512]{1,0:T(8,128)}), f32[1280,512]{1,0:T(8,128)}) %reduce-scatter.18.cloned.1.call-update) | async-done | bytes 2621456 | tf_op jit(solution)/shard_map/while/body/eval_jaxpr/reduce_scatter | solution.py:39
  5420.2 41.5 fusion.218
  5535.2 67.9 %all-gather.31.cloned.1.call-done = bf16[2560,1024]{0,1:T(8,128)(2,1)} async-done(((bf16[1280,1024]{0,1:T(8,128)(2,1)}), bf16[2560,1024]{0,1:T(8,128)(2,1)}) %all-gather.31.cloned.1.call-update) | async-done | bytes 5242896 | tf_op jit(solution)/shard_map/while/body/eval_jaxpr/all_gather | solution.py:35
  5613.3 121.6 %all-gather.33.cloned.1.call-done = bf16[2560,2048]{1,0:T(8,128)(2,1)} async-done(((bf16[1280,2048]{1,0:T(8,128)(2,1)}), bf16[2560,2048]{1,0:T(8,128)(2,1)}) %all-gather.33.cloned.1.call-update) | async-done | bytes 10485776 | tf_op jit(solution)/shard_map/while/body/eval_jaxpr/all_gather | solution.py:35
  5838.2 90.0 %reduce-scatter.26.cloned.1.call-done = bf16[640,1024]{1,0:T(8,128)(2,1)} async-done(((bf16[2560,1024]{1,0:T(8,128)(2,1)}), bf16[640,1024]{1,0:T(8,128)(2,1)}) %reduce-scatter.26.cloned.1.call-update) | async-done | bytes 1310736 | tf_op jit(solution)/shard_map/while/body/eval_jaxpr/reduce_scatter | solution.py:45
  5991.2 237.9 %all-reduce.8.cloned.1.call-done = (bf16[1024,1024]{1,0:T(8,128)(2,1)}, bf16[512,1024]{1,0:T(8,128)(2,1)}, bf16[1024,4096]{1,0:T(8,128)(2,1)}, bf16[2048,1024]{1,0:T(8,128)(2,1)}) async-done(((bf16[1024,1024]{1,0:T(8,128)(2,1)}, bf16[512,1024]{1,0:T(8,128)(2,1)}, bf16[1024,4096]{1,0:T(8,128)(2,1)}, bf16[2048,1024]{1,0:T(8,128)(2,1)}), (bf16[1024,1024]{1,0:T(8,128)(2,1)}, bf16[512,1024]{1,0:T(8,128)(2,1)}, ...) | async-done | bytes 15728656 | tf_op jit(solution)/shard_map/psum | solution.py:280
  (465 shorter events, 1154.8 us)
Async XLA Ops:
  20.4 109.0 %all-gather.15.cloned.1.call-start = ((), (), s32[]{:S(2)}) async-start(), calls=%async_computation.10 | async-start | bytes 6553600 | tf_op jit(solution)/shard_map/while/body/eval_jaxpr/all_gather | solution.py:31
  29.4 231.4 %reduce-scatter.12.cloned.1.call-start = ((), (), s32[]{:S(2)}) async-start(), calls=%async_computation.13 | async-start | bytes 15728640 | tf_op jit(solution)/shard_map/while/body/eval_jaxpr/reduce_scatter | solution.py:39
  140.3 158.9 %all-gather.21.cloned.1.call-start = ((), (), s32[]{:S(2)}) async-start(), calls=%async_computation.15 | async-start | bytes 1966080 | tf_op jit(solution)/shard_map/while/body/eval_jaxpr/all_gather | solution.py:159
  359.0 140.4 %reduce-scatter.14.cloned.1.call-start = ((), (), s32[]{:S(2)}) async-start(), calls=%async_computation.17 | async-start | bytes 6553600 | tf_op jit(solution)/shard_map/while/body/eval_jaxpr/reduce_scatter | solution.py:45
  405.5 194.1 %all-gather.17.cloned.1.call-start = ((), (), s32[]{:S(2)}) async-start(), calls=%async_computation.11 | async-start | bytes 6553600 | tf_op jit(solution)/shard_map/while/body/eval_jaxpr/all_gather | solution.py:31
  408.1 290.2 %all-gather.25.cloned.1.call-start = ((), (), s32[]{:S(2)}) async-start(), calls=%async_computation.18 | async-start | bytes 6553600 | tf_op jit(solution)/shard_map/while/body/eval_jaxpr/all_gather | solution.py:31
  509.8 423.4 %reduce-scatter.10.cloned.1.call-start = ((), (), s32[]{:S(2)}) async-start(), calls=%async_computation.12 | async-start | bytes 31457280 | tf_op jit(solution)/shard_map/while/body/eval_jaxpr/reduce_scatter | solution.py:39
  617.8 1235.1 %all-reduce.10.cloned.1.call-start = ((), (), s32[]{:S(2)}) async-start(), calls=%async_computation.19 | async-start | bytes 83886080 | tf_op jit(solution)/shard_map/while
  727.8 1393.7 %all-gather.27.cloned.1.call-start = ((), (), s32[]{:S(2)}) async-start(), calls=%async_computation.20 | async-start | bytes 31457280 | tf_op jit(solution)/shard_map/while/body/eval_jaxpr/all_gather | solution.py:35
  1873.0 370.9 %reduce-scatter.16.cloned.1.call-start = ((), (), s32[]{:S(2)}) async-start(), calls=%async_computation.21 | async-start | bytes 6553600 | tf_op jit(solution)/shard_map/while/body/eval_jaxpr/reduce_scatter | solution.py:45
  2150.0 205.1 %all-gather.29.cloned.1.call-start = ((), (), s32[]{:S(2)}) async-start(), calls=%async_computation.22 | async-start | bytes 6553600 | tf_op jit(solution)/shard_map/while/body/eval_jaxpr/all_gather | solution.py:31
  2256.4 170.9 %reduce-scatter.18.cloned.1.call-start = ((), (), s32[]{:S(2)}) async-start(), calls=%async_computation.23 | async-start | bytes 7864320 | tf_op jit(solution)/shard_map/while/body/eval_jaxpr/reduce_scatter | solution.py:39
  2363.1 193.0 %reduce-scatter.22.cloned.1.call-start = ((), (), s32[]{:S(2)}) async-start(), calls=%async_computation.25 | async-start | bytes 1966080 | tf_op jit(solution)/shard_map/while/body/eval_jaxpr/reduce_scatter | solution.py:230
  2578.7 200.3 %all-gather.33.cloned.1.call-start = ((), (), s32[]{:S(2)}) async-start(), calls=%async_computation.27 | async-start | bytes 15728640 | tf_op jit(solution)/shard_map/while/body/eval_jaxpr/all_gather | solution.py:35
  2579.3 295.9 %reduce-scatter.24.cloned.1.call-start = ((), (), s32[]{:S(2)}) async-start(), calls=%async_computation.28 | async-start | bytes 6553600 | tf_op jit(solution)/shard_map/while/body/eval_jaxpr/reduce_scatter | solution.py:45
  2657.4 315.0 %reduce-scatter.26.cloned.1.call-start = ((), (), s32[]{:S(2)}) async-start(), calls=%async_computation.29 | async-start | bytes 6553600 | tf_op jit(solution)/shard_map/while/body/eval_jaxpr/reduce_scatter | solution.py:45
  2986.4 230.1 %reduce-scatter.12.cloned.1.call-start = ((), (), s32[]{:S(2)}) async-start(), calls=%async_computation.13 | async-start | bytes 15728640 | tf_op jit(solution)/shard_map/while/body/eval_jaxpr/reduce_scatter | solution.py:39
  3096.2 158.9 %all-gather.21.cloned.1.call-start = ((), (), s32[]{:S(2)}) async-start(), calls=%async_computation.15 | async-start | bytes 1966080 | tf_op jit(solution)/shard_map/while/body/eval_jaxpr/all_gather | solution.py:159
  3314.8 140.4 %reduce-scatter.14.cloned.1.call-start = ((), (), s32[]{:S(2)}) async-start(), calls=%async_computation.17 | async-start | bytes 6553600 | tf_op jit(solution)/shard_map/while/body/eval_jaxpr/reduce_scatter | solution.py:45
  3361.4 193.9 %all-gather.17.cloned.1.call-start = ((), (), s32[]{:S(2)}) async-start(), calls=%async_computation.11 | async-start | bytes 6553600 | tf_op jit(solution)/shard_map/while/body/eval_jaxpr/all_gather | solution.py:31
  3363.9 290.0 %all-gather.25.cloned.1.call-start = ((), (), s32[]{:S(2)}) async-start(), calls=%async_computation.18 | async-start | bytes 6553600 | tf_op jit(solution)/shard_map/while/body/eval_jaxpr/all_gather | solution.py:31
  3465.6 423.2 %reduce-scatter.10.cloned.1.call-start = ((), (), s32[]{:S(2)}) async-start(), calls=%async_computation.12 | async-start | bytes 31457280 | tf_op jit(solution)/shard_map/while/body/eval_jaxpr/reduce_scatter | solution.py:39
  3573.5 1235.1 %all-reduce.10.cloned.1.call-start = ((), (), s32[]{:S(2)}) async-start(), calls=%async_computation.19 | async-start | bytes 83886080 | tf_op jit(solution)/shard_map/while
  3683.5 1393.7 %all-gather.27.cloned.1.call-start = ((), (), s32[]{:S(2)}) async-start(), calls=%async_computation.20 | async-start | bytes 31457280 | tf_op jit(solution)/shard_map/while/body/eval_jaxpr/all_gather | solution.py:35
  4828.7 370.9 %reduce-scatter.16.cloned.1.call-start = ((), (), s32[]{:S(2)}) async-start(), calls=%async_computation.21 | async-start | bytes 6553600 | tf_op jit(solution)/shard_map/while/body/eval_jaxpr/reduce_scatter | solution.py:45
  5105.7 205.2 %all-gather.29.cloned.1.call-start = ((), (), s32[]{:S(2)}) async-start(), calls=%async_computation.22 | async-start | bytes 6553600 | tf_op jit(solution)/shard_map/while/body/eval_jaxpr/all_gather | solution.py:31
  5212.1 171.0 %reduce-scatter.18.cloned.1.call-start = ((), (), s32[]{:S(2)}) async-start(), calls=%async_computation.23 | async-start | bytes 7864320 | tf_op jit(solution)/shard_map/while/body/eval_jaxpr/reduce_scatter | solution.py:39
  5318.8 192.9 %reduce-scatter.22.cloned.1.call-start = ((), (), s32[]{:S(2)}) async-start(), calls=%async_computation.25 | async-start | bytes 1966080 | tf_op jit(solution)/shard_map/while/body/eval_jaxpr/reduce_scatter | solution.py:230
  5534.4 200.5 %all-gather.33.cloned.1.call-start = ((), (), s32[]{:S(2)}) async-start(), calls=%async_computation.27 | async-start | bytes 15728640 | tf_op jit(solution)/shard_map/while/body/eval_jaxpr/all_gather | solution.py:35
  5535.2 295.8 %reduce-scatter.24.cloned.1.call-start = ((), (), s32[]{:S(2)}) async-start(), calls=%async_computation.28 | async-start | bytes 6553600 | tf_op jit(solution)/shard_map/while/body/eval_jaxpr/reduce_scatter | solution.py:45
  5613.1 315.2 %reduce-scatter.26.cloned.1.call-start = ((), (), s32[]{:S(2)}) async-start(), calls=%async_computation.29 | async-start | bytes 6553600 | tf_op jit(solution)/shard_map/while/body/eval_jaxpr/reduce_scatter | solution.py:45
  5937.8 291.4 %all-reduce.8.cloned.1.call-start = ((), (), s32[]{:S(2)}) async-start(), calls=%async_computation.9 | async-start | bytes 31457280 | tf_op jit(solution)/shard_map/psum | solution.py:280
  (102 other events, 4170.4 us)
Sparse Core Ops, SparseCore 0:
  29.5 99.8 all-gather.14
  140.5 120.2 reduce-scatter.11
  359.1 39.0 all-gather.22
  405.6 93.7 reduce-scatter.13
  501.0 98.5 all-gather.16
  601.8 96.4 all-gather.24
  700.5 232.5 reduce-scatter.9
  935.5 917.4 all-reduce.9
  1873.1 248.3 all-gather.26
  2150.1 93.7 reduce-scatter.15
  2256.5 98.5 all-gather.28
  2363.2 64.0 reduce-scatter.17
  2578.8 68.5 all-gather.30
  2649.5 129.5 all-gather.32
  2781.4 93.7 reduce-scatter.23
  2878.1 94.2 reduce-scatter.25
  2986.6 98.5 all-gather.14
  3096.3 120.2 reduce-scatter.11
  3315.0 39.0 all-gather.22
  3361.5 93.7 reduce-scatter.13
  3456.7 98.5 all-gather.16
  3557.4 96.4 all-gather.24
  3656.2 232.5 reduce-scatter.9
  3891.1 917.4 all-reduce.9
  4828.8 248.3 all-gather.26
  5105.8 93.7 reduce-scatter.15
  5212.2 98.5 all-gather.28
  5318.9 64.0 reduce-scatter.17
  5534.6 68.5 all-gather.30
  5605.4 129.5 all-gather.32
  5737.2 93.7 reduce-scatter.23
  5833.9 94.2 reduce-scatter.25
  (8 shorter events, 189.5 us)
Sparse Core Ops, SparseCore 1:
  5955.6 273.4 all-reduce.7
where the time goes:
time: 6260 us
  waiting for transfers between devices  5140 us (82%)
  matrix products  633 us (10%)
  other arithmetic  275 us (4%)
  local copies, waits for them, and re-layouts  107 us (2%)
  blocking collectives  75.4 us (1%)
    while x42, waiting for transfers between devices  1840 us
    all_gather x8, waiting for transfers between devices, cols_gather(): return lax.all_gather(values, 'col', axis=0, tiled=True)  953 us
    reduce_scatter x6, waiting for transfers between devices, cols_reduce(): lax.psum_scatter(part_fn(jnp.int32(0), rows * lax.axis_size('col')), 'col...  760 us
    all_gather x8, waiting for transfers between devices, rows_gather(): return lax.all_gather(values, 'row', axis=0, tiled=True)  736 us
    reduce_scatter x8, waiting for transfers between devices, rows_reduce(): lax.psum_scatter(part_fn(jnp.int32(0), rows * lax.axis_size('row')).astyp...  584 us
    psum x1, waiting for transfers between devices, body(): lax.psum(grad_project.astype(jnp.bfloat16), 'dp').astype(jnp.float32)  238 us
    dot_general x8, matrix products, contract_cols(): lax.dot_general(left, right, (((1,), (1,)), ((), ())), preferred_element_...  129 us
    dot_general x8, matrix products, part_fn(): return jnp.dot(whole, weight, preferred_element_type=jnp.float32)  129 us
  transfers between devices with their start and end apart: 41, of which 37 were waited for; matrix products, arithmetic and copies ran while one was open for 8% of the time, Pallas kernels for 0%

commit v1 on v0

--- a/solution.py
+++ b/solution.py
@@ -1,8 +1,11 @@
+import functools
 import math
 
 import jax
 import jax.numpy as jnp
 from jax import lax
+from jax.experimental import pallas as pl
+from jax.experimental.pallas import tpu as pltpu
 from jax.sharding import PartitionSpec as P
 
 D = 2048
@@ -301,6 +304,739 @@
     )
 
 
+CORE_SWAP = [(0, 1), (1, 0), (2, 3), (3, 2)]
+X_SWAP = [(0, 2), (2, 0), (1, 3), (3, 1)]
+COL_SWAP = [(0, 1), (1, 0)]
+LOG2E = 1.4426950408889634
+TRUNK = 1024
+LEAF_BEGIN = TRUNK + 4 * 128
+VMEM_LIMIT = 58 * 1024 * 1024
+NT = (((1,), (1,)), ((), ()))
+TN = (((0,), (0,)), ((), ()))
+NN = (((1,), (0,)), ((), ()))
+
+
+def swap_core(a):
+    return lax.ppermute(a, "dp", CORE_SWAP)
+
+
+def swap_x(a):
+    return lax.ppermute(a, "dp", X_SWAP)
+
+
+def swap_col(a):
+    return lax.ppermute(a, "col", COL_SWAP)
+
+
+def mxu(a, b, dims):
+    return lax.dot_general(a, b, dims, preferred_element_type=jnp.float32)
+
+
+def low(a):
+    return a.astype(jnp.bfloat16)
+
+
+def wide(a):
+    return a.astype(jnp.float32)
+
+
+def rows_call(fn, block, row_ins, full_ins, outs, flops, name, scratch=()):
+    rows = row_ins[0].shape[0]
+    in_specs = [pl.BlockSpec((block, a.shape[1]), lambda i: (i, 0)) for a in row_ins]
+    for a in full_ins:
+        in_specs.append(
+            pl.BlockSpec(
+                a.shape, lambda i, nd=a.ndim: (0,) * nd, pipeline_mode=pl.Buffered(1)
+            )
+        )
+    moved = sum(a.size * a.dtype.itemsize for a in (*row_ins, *full_ins))
+    moved += sum(rows * w * jnp.dtype(dt).itemsize for w, dt in outs)
+    return pl.pallas_call(
+        fn,
+        grid=(rows // block,),
+        in_specs=in_specs,
+        out_specs=[pl.BlockSpec((block, w), lambda i: (i, 0)) for w, _ in outs],
+        out_shape=[jax.ShapeDtypeStruct((rows, w), dt) for w, dt in outs],
+        scratch_shapes=list(scratch),
+        compiler_params=pltpu.CompilerParams(vmem_limit_bytes=VMEM_LIMIT),
+        cost_estimate=pl.CostEstimate(flops=flops, bytes_accessed=moved, transcendentals=0),
+        name=name,
+    )(*row_ins, *full_ins)
+
+
+def turn(u, cosine, sine_signed):
+    return u * cosine + pltpu.roll(u, HEAD // 2, 1) * sine_signed
+
+
+def turn_back(u, cosine, sine_signed):
+    return u * cosine - pltpu.roll(u, HEAD // 2, 1) * sine_signed
+
+
+def project_kernel(x0, x1, x2, x3, cos_ref, sin_ref, gain_ref, w_ref, xn_ref, qkv_ref, r_ref):
+    pieces = [wide(r[...]) for r in (x0, x1, x2, x3)]
+    width = pieces[0].shape[1]
+    total = sum(jnp.sum(p * p, axis=1, keepdims=True) for p in pieces)
+    ratio = lax.rsqrt(total / (4 * width) + EPSILON)
+    r_ref[...] = ratio
+    for i, p in enumerate(pieces):
+        cols = slice(i * width, (i + 1) * width)
+        xn_ref[:, cols] = low(p * ratio * gain_ref[:, cols])
+    normed = xn_ref[...]
+    cosine = cos_ref[...]
+    sine = sin_ref[...]
+    span = w_ref.shape[2]
+    heads = span // HEAD
+    for g in range(w_ref.shape[0]):
+        acc = mxu(normed, w_ref[g], NN)
+        for h in range(heads):
+            u = acc[:, h * HEAD : (h + 1) * HEAD]
+            if h < heads - 1:
+                u = turn(u, cosine, sine)
+            at = g * span + h * HEAD
+            qkv_ref[:, at : at + HEAD] = low(u)
+
+
+def segments_of(kind, trunk, leaf_begin, block):
+    if kind == "branch":
+        return [(0, trunk, None), (None, block, "own")]
+    if kind == "leaf":
+        return [(0, trunk, None), (trunk, leaf_begin - trunk, "parent"), (None, 2 * block, "own")]
+    return [(0, kind, "causal")]
+
+
+def attention_blocks(qb, block, trunk, leaf_begin, run):
+    half = trunk // 2
+
+    @pl.when(qb < half // block)
+    def _():
+        run(half, 0)
+
+    @pl.when((qb >= half // block) & (qb < trunk // block))
+    def _():
+        run(trunk, 0)
+
+    @pl.when((qb >= trunk // block) & (qb < leaf_begin // block))
+    def _():
+        run("branch", pl.multiple_of(qb * block, block))
+
+    @pl.when(qb >= leaf_begin // block)
+    def _():
+        run("leaf", pl.multiple_of(qb * block - block, block))
+
+
+def key_rows(start, window, length):
+    if start is None:
+        return pl.ds(window, length)
+    return pl.ds(start, length)
+
+
+def score_segment(s, start, window, length, mask, qb, block, lab_ref, own_row, parent_row):
+    if mask is None:
+        return s
+    rows = s.shape[0]
+    cols = s.shape[1]
+    if mask == "parent":
+        return jnp.where(lab_ref[key_rows(start, window, length), :] == parent_row, s, -jnp.inf)
+    base = window if start is None else start
+    key_at = base + lax.broadcasted_iota(jnp.int32, (rows, 1), 0)
+    lane = lax.broadcasted_iota(jnp.int32, (1, cols), 1)
+    query_at = qb * block + jnp.where(lane >= block, lane - block, lane)
+    seen = key_at <= query_at
+    if mask == "own":
+        seen = seen & (lab_ref[key_rows(start, window, length), :] == own_row)
+    return jnp.where(seen, s, -jnp.inf)
+
+
+def attend_kernel(trunk, leaf_begin, block, q_ref, k_ref, v_ref, lab_ref, row_ref, o_ref, lse_ref, vt_ref):
+    qb = pl.program_id(1)
+    factor = LOG2E / math.sqrt(HEAD)
+
+    @pl.when(qb == 0)
+    def _():
+        vt_ref[...] = v_ref[...].T
+
+    queries = jnp.concatenate([q_ref[:, :HEAD], q_ref[:, HEAD:]], axis=0)
+    own = row_ref[0:1, :]
+    parent = row_ref[1:2, :]
+    own_row = jnp.concatenate([own, own], axis=1)
+    parent_row = jnp.concatenate([parent, parent], axis=1)
+
+    def run(kind, window):
+        scores = []
+        segs = segments_of(kind, trunk, leaf_begin, block)
+        for start, length, mask in segs:
+            s = mxu(k_ref[key_rows(start, window, length), :], queries, NT)
+            s = score_segment(
+                s, start, window, length, mask, qb, block, lab_ref, own_row, parent_row
+            )
+            scores.append(s)
+        top = scores[0].max(axis=0, keepdims=True)
+        for s in scores[1:]:
+            top = jnp.maximum(top, s.max(axis=0, keepdims=True))
+        total = jnp.zeros_like(top)
+        mixed = jnp.zeros((HEAD, 2 * block), jnp.float32)
+        shift = top * factor
+        for (start, length, mask), s in zip(segs, scores):
+            p = jnp.exp2(s * factor - shift)
+            total = total + p.sum(axis=0, keepdims=True)
+            mixed = mixed + mxu(vt_ref[:, key_rows(start, window, length)], low(p), NN)
+        lse_ref[...] = shift + jnp.log2(total)
+        mixed = mixed / total
+        o_ref[:, :HEAD] = low(mixed[:, :block].T)
+        o_ref[:, HEAD:] = low(mixed[:, block:].T)
+
+    attention_blocks(qb, block, trunk, leaf_begin, run)
+
+
+def attend_back_kernel(
+    trunk, leaf_begin, block, blocks, q_ref, k_ref, v_ref, o_ref, do_ref, lab_ref, row_ref, lse_ref,
+    cos_ref, sin_ref, out_ref, kt_ref, dk_ref, dv_ref,
+):
+    qb = pl.program_id(1)
+    scale = 1.0 / math.sqrt(HEAD)
+    factor = LOG2E * scale
+
+    @pl.when(qb == 0)
+    def _():
+        kt_ref[...] = k_ref[...].T
+        dk_ref[...] = jnp.zeros_like(dk_ref)
+        dv_ref[...] = jnp.zeros_like(dv_ref)
+
+    queries = jnp.concatenate([q_ref[:, :HEAD], q_ref[:, HEAD:]], axis=0)
+    grads = jnp.concatenate([do_ref[:, :HEAD], do_ref[:, HEAD:]], axis=0)
+    outs = jnp.concatenate([o_ref[:, :HEAD], o_ref[:, HEAD:]], axis=0)
+    inner = (wide(grads) * wide(outs)).T.sum(axis=0, keepdims=True)
+    lse = lse_ref[...]
+    own = row_ref[0:1, :]
+    parent = row_ref[1:2, :]
+    own_row = jnp.concatenate([own, own], axis=1)
+    parent_row = jnp.concatenate([parent, parent], axis=1)
+    q_rows = pl.ds(pl.multiple_of(qb * block, block), block)
+
+    def run(kind, window):
+        dq = jnp.zeros((HEAD, 2 * block), jnp.float32)
+        for start, length, mask in segments_of(kind, trunk, leaf_begin, block):
+            keys = key_rows(start, window, length)
+            s = mxu(k_ref[keys, :], queries, NT)
+            s = score_segment(
+                s, start, window, length, mask, qb, block, lab_ref, own_row, parent_row
+            )
+            p = jnp.exp2(s * factor - lse)
+            dp = mxu(v_ref[keys, :], grads, NT)
+            ds = low(p * (dp - inner))
+            dv_ref[keys, :] += mxu(low(p), grads, NN)
+            dk_ref[keys, :] += mxu(ds, queries, NN)
+            dq = dq + mxu(kt_ref[:, keys], ds, NN)
+        dq = dq * scale
+        cosine = cos_ref[q_rows, :]
+        sine = sin_ref[q_rows, :]
+        for h in range(2):
+            part = dq[:, h * block : (h + 1) * block].T
+            out_ref[q_rows, h * HEAD : (h + 1) * HEAD] = low(turn_back(part, cosine, sine))
+
+    attention_blocks(qb, block, trunk, leaf_begin, run)
+
+    @pl.when(qb == blocks - 1)
+    def _():
+        dk = dk_ref[...] * scale
+        out_ref[:, 2 * HEAD : 3 * HEAD] = low(turn_back(dk, cos_ref[...], sin_ref[...]))
+        out_ref[:, 3 * HEAD :] = low(dv_ref[...])
+
+
+def attention_specs(rows, block, groups):
+    q_spec = pl.BlockSpec((block, 2 * HEAD), lambda g, i: (i, 2 * g))
+    k_spec = pl.BlockSpec((rows, HEAD), lambda g, i: (0, 4 * g + 2))
+    v_spec = pl.BlockSpec((rows, HEAD), lambda g, i: (0, 4 * g + 3))
+    lab_spec = pl.BlockSpec((rows, 1), lambda g, i: (0, 0))
+    row_spec = pl.BlockSpec((8, block), lambda g, i: (0, i))
+    o_spec = pl.BlockSpec((block, 2 * HEAD), lambda g, i: (i, g))
+    lse_spec = pl.BlockSpec((None, None, 1, 2 * block), lambda g, i: (g, i, 0, 0))
+    return q_spec, k_spec, v_spec, lab_spec, row_spec, o_spec, lse_spec
+
+
+def attend(qkv, label_col, label_rows, trunk, leaf_begin, block):
+    rows = qkv.shape[0]
+    groups = qkv.shape[1] // (4 * HEAD)
+    blocks = rows // block
+    q_spec, k_spec, v_spec, lab_spec, row_spec, o_spec, lse_spec = attention_specs(rows, block, groups)
+    pairs = groups * 2 * rows * rows // 2
+    return pl.pallas_call(
+        functools.partial(attend_kernel, trunk, leaf_begin, block),
+        grid=(groups, blocks),
+        in_specs=[q_spec, k_spec, v_spec, lab_spec, row_spec],
+        out_specs=[o_spec, lse_spec],
+        out_shape=[
+            jax.ShapeDtypeStruct((rows, groups * 2 * HEAD), jnp.bfloat16),
+            jax.ShapeDtypeStruct((groups, blocks, 1, 2 * block), jnp.float32),
+        ],
+        scratch_shapes=[pltpu.VMEM((HEAD, rows), jnp.bfloat16)],
+        compiler_params=pltpu.CompilerParams(vmem_limit_bytes=VMEM_LIMIT),
+        cost_estimate=pl.CostEstimate(
+            flops=4 * 4 * pairs * HEAD, bytes_accessed=20 * rows * HEAD * 2, transcendentals=pairs
+        ),
+        name="attend",
+    )(qkv, qkv, qkv, label_col, label_rows)
+
+
+def attend_back(qkv, attn, attn_grad, label_col, label_rows, lse, cosine, sine, trunk, leaf_begin, block):
+    rows = qkv.shape[0]
+    groups = qkv.shape[1] // (4 * HEAD)
+    blocks = rows // block
+    q_spec, k_spec, v_spec, lab_spec, row_spec, o_spec, lse_spec = attention_specs(rows, block, groups)
+    table = pl.BlockSpec((rows, HEAD), lambda g, i: (0, 0))
+    pairs = groups * 2 * rows * rows // 2
+    return pl.pallas_call(
+        functools.partial(attend_back_kernel, trunk, leaf_begin, block, blocks),
+        grid=(groups, blocks),
+        in_specs=[q_spec, k_spec, v_spec, o_spec, o_spec, lab_spec, row_spec, lse_spec, table, table],
+        out_specs=pl.BlockSpec((rows, 4 * HEAD), lambda g, i: (0, g)),
+        out_shape=jax.ShapeDtypeStruct((rows, groups * 4 * HEAD), jnp.bfloat16),
+        scratch_shapes=[
+            pltpu.VMEM((HEAD, rows), jnp.bfloat16),
+            pltpu.VMEM((rows, HEAD), jnp.float32),
+            pltpu.VMEM((rows, HEAD), jnp.float32),
+        ],
+        compiler_params=pltpu.CompilerParams(vmem_limit_bytes=VMEM_LIMIT),
+        cost_estimate=pl.CostEstimate(
+            flops=10 * 4 * pairs * HEAD, bytes_accessed=40 * rows * HEAD * 2, transcendentals=pairs
+        ),
+        name="attend_back",
+    )(qkv, qkv, qkv, attn, attn_grad, label_col, label_rows, lse, cosine, sine)
+
+
+def halves_out(acc, own_ref, send_ref):
+    half = own_ref.shape[1]
+    own_ref[...] = low(acc[:, :half])
+    send_ref[...] = low(acc[:, half:])
+
+
+def out_kernel(a_ref, w_ref, own_ref, send_ref):
+    halves_out(mxu(a_ref[...], w_ref[...], NN), own_ref, send_ref)
+
+
+def two_out_kernel(a_ref, b_ref, wa_ref, wb_ref, own_ref, send_ref):
+    acc = mxu(a_ref[...], wa_ref[...], NN) + mxu(b_ref[...], wb_ref[...], NN)
+    halves_out(acc, own_ref, send_ref)
+
+
+def project_back_kernel(d_ref, w_ref, own_ref, send_ref):
+    groups = w_ref.shape[0]
+    span = w_ref.shape[2]
+    acc = sum(mxu(d_ref[:, g * span : (g + 1) * span], w_ref[g], NT) for g in range(groups))
+    halves_out(acc, own_ref, send_ref)
+
+
+def attn_grad_kernel(h0, h1, h2, h3, w_ref, out_ref):
+    width = h0.shape[1]
+    acc = sum(
+        mxu(h[...], w_ref[:, i * width : (i + 1) * width], NT)
+        for i, h in enumerate((h0, h1, h2, h3))
+    )
+    out_ref[...] = low(acc)
+
+
+def hidden_kernel(
+    x0, x1, x2, x3, g0, g1, g2, g3, wa_ref, wb_ref, da_ref, db_ref, ha_ref, hb_ref, pa_ref, pb_ref,
+    xs_ref, gs_ref,
+):
+    width = x0.shape[1]
+    for i, (x, g) in enumerate(zip((x0, x1, x2, x3), (g0, g1, g2, g3))):
+        xs_ref[:, i * width : (i + 1) * width] = x[...]
+        gs_ref[:, i * width : (i + 1) * width] = g[...]
+    normed = xs_ref[...]
+    grads = gs_ref[...]
+    for w_ref, d_ref, h_ref, p_ref in ((wa_ref, da_ref, ha_ref, pa_ref), (wb_ref, db_ref, hb_ref, pb_ref)):
+        parts = w_ref.shape[0]
+        unit = w_ref.shape[1] // 2
+        for z in range(parts):
+            pair = mxu(normed, w_ref[z], NT)
+            hidden_grad = mxu(grads, d_ref[z], NT)
+            gate = pair[:, :unit]
+            upper = pair[:, unit:]
+            sigma = jax.nn.sigmoid(gate)
+            silu_value = gate * sigma
+            h_ref[:, z * unit : (z + 1) * unit] = low(silu_value * upper)
+            at = 2 * z * unit
+            p_ref[:, at : at + unit] = low(
+                hidden_grad * upper * sigma * (1.0 + gate * (1.0 - sigma))
+            )
+            p_ref[:, at + unit : at + 2 * unit] = low(hidden_grad * silu_value)
+
+
+def weight_grad_kernel(count, joined, *refs):
+    a_ref = refs[0]
+    b_refs = refs[1 : 1 + count]
+    o_refs = refs[1 + count :]
+    left = a_ref[...].T
+    for i, b in enumerate(b_refs):
+        width = b.shape[1]
+        acc = low(mxu(left, b[...], NN))
+        if joined:
+            o_refs[0][:, i * width : (i + 1) * width] = acc
+        else:
+            o_refs[i][...] = acc
+
+
+def weight_grad(a, bs, joined, block, name):
+    rows, m = a.shape
+    n = sum(b.shape[1] for b in bs)
+    widths = [n] if joined else [b.shape[1] for b in bs]
+    in_specs = [pl.BlockSpec((rows, block), lambda i: (0, i))]
+    for b in bs:
+        in_specs.append(
+            pl.BlockSpec(b.shape, lambda i: (0, 0), pipeline_mode=pl.Buffered(1))
+        )
+    return pl.pallas_call(
+        functools.partial(weight_grad_kernel, len(bs), joined),
+        grid=(m // block,),
+        in_specs=in_specs,
+        out_specs=[pl.BlockSpec((block, w), lambda i: (i, 0)) for w in widths],
+        out_shape=[jax.ShapeDtypeStruct((m, w), jnp.bfloat16) for w in widths],
+        compiler_params=pltpu.CompilerParams(vmem_limit_bytes=VMEM_LIMIT),
+        cost_estimate=pl.CostEstimate(
+            flops=2 * rows * m * n, bytes_accessed=2 * (rows * m + rows * n + m * n), transcendentals=0
+        ),
+        name=name,
+    )(a, *bs)
+
+
+def take(a, index, axis):
+    return lax.dynamic_index_in_dim(a, index, axis, keepdims=False)
+
+
+def in_order(index, mine, other, axis=0):
+    first = jnp.where(index == 0, mine, other)
+    second = jnp.where(index == 0, other, mine)
+    return jnp.stack([first, second], axis=axis)
+
+
+def spread(a):
+    b = swap_col(a)
+    return [a, b, swap_core(a), swap_core(b)]
+
+
+def collect(own, send):
+    quarter = own.shape[1] // 2
+    got = swap_core(send)
+    outgoing = low(wide(own[:, quarter:]) + wide(got[:, quarter:]))
+    back = swap_col(outgoing)
+    return wide(own[:, :quarter]) + wide(got[:, :quarter]) + wide(back)
+
+
+def small_sum(v):
+    v = v + swap_core(v)
+    return v + swap_col(v)
+
+
+def tree_body(
+    tokens,
+    out_grad,
+    path,
+    positions,
+    w_query,
+    w_key,
+    w_value,
+    w_out,
+    w_gate,
+    w_up,
+    w_down,
+    gain_attn,
+    gain_ffn,
+):
+    dp = lax.axis_index("dp")
+    x = dp // 2
+    c = lax.rem(dp, 2)
+    z = lax.axis_index("row")
+    y = lax.axis_index("col")
+    micro, local_rows, half = tokens.shape
+    quarter = half // 2
+    rows = path.shape[1]
+    planes = lax.axis_size("row")
+    features = 2 * half
+    block = 256
+    trunk = TRUNK
+    leaf_begin = LEAF_BEGIN
+
+    def to_tree(a):
+        parts = a.reshape(micro, local_rows, 2, quarter)
+        mine = take(parts, c, 2)
+        other = swap_core(take(parts, 1 - c, 2))
+        trees = in_order(c, mine, other).reshape(planes * local_rows, quarter)
+        return lax.all_to_all(trees, "row", 0, 0, tiled=True)
+
+    def from_tree(a):
+        trees = lax.all_to_all(a, "row", 0, 0, tiled=True)
+        trees = trees.reshape(2, micro, local_rows, quarter)
+        mine = take(trees, c, 0)
+        other = swap_core(take(trees, 1 - c, 0))
+        return in_order(c, mine, other, 2).reshape(micro, local_rows, half)
+
+    def of_tree(a):
+        both = in_order(c, a, swap_core(a))
+        return take(both.reshape((2 * micro,) + a.shape[1:]), z, 0)
+
+    tree_path = of_tree(path)
+    tree_place = of_tree(positions)
+    cosine, sine = rope_tables(tree_place)
+    sign = jnp.where(jnp.arange(HEAD) < HEAD // 2, -1.0, 1.0).astype(jnp.float32)
+    sine = sine * sign[None, :]
+    label_col = tree_path[:, 0:1]
+    label_rows = jnp.pad(tree_path.T, ((0, 5), (0, 0)))
+
+    block_in = to_tree(tokens)
+
+    key_width = w_key.shape[1]
+    groups = key_width // HEAD
+    share = quarter // 2
+    first_row = c * quarter + x * share
+
+    def group_cols(g):
+        return jnp.concatenate(
+            [
+                lax.dynamic_slice_in_dim(w_query, g * 2 * HEAD, 2 * HEAD, 1),
+                lax.dynamic_slice_in_dim(w_key, g * HEAD, HEAD, 1),
+                lax.dynamic_slice_in_dim(w_value, g * HEAD, HEAD, 1),
+            ],
+            axis=1,
+        )
+
+    def own_rows(a):
+        return lax.dynamic_slice_in_dim(a, first_row, share, 0)
+
+    def spread_attn(kept, sent):
+        piece = jnp.stack([kept, swap_col(sent)])
+        mine = lax.all_gather(piece, "row", axis=0)
+        both = in_order(x, mine, swap_x(mine), 2)
+        pairs = both.reshape((2, planes // 2) + both.shape[1:])
+        own = take(pairs, c, 0)
+        other = swap_core(take(pairs, 1 - c, 0))
+        return jnp.stack([own, other], axis=1)
+
+    w_project = spread_attn(own_rows(group_cols(y)), own_rows(group_cols(1 - y)))
+    w_project = w_project.reshape(groups, features, 4 * HEAD)
+
+    def head_rows(g):
+        at = (g * 2 + x) * HEAD
+        return lax.dynamic_slice(w_out, (at, c * quarter), (HEAD, quarter))
+
+    w_mix = spread_attn(head_rows(y), head_rows(1 - y))
+    w_mix = jnp.transpose(w_mix, (0, 3, 4, 1, 2, 5)).reshape(groups * 2 * HEAD, features)
+
+    hidden_width = w_gate.shape[1]
+    unit = hidden_width // 8
+
+    def unit_at(j):
+        return (2 * j + c) * 2 * unit + x * unit
+
+    def by_core(a):
+        parts = a.reshape(unit, 2, quarter)
+        return jnp.where(c == 0, parts, parts[:, ::-1])
+
+    def hidden_pieces(j):
+        at = unit_at(j)
+        gate = lax.dynamic_slice_in_dim(w_gate, at, unit, 1).T
+        upper = lax.dynamic_slice_in_dim(w_up, at, unit, 1).T
+        return jnp.stack([by_core(gate), by_core(upper)]), by_core(
+            lax.dynamic_slice_in_dim(w_down, at, unit, 0)
+        )
+
+    pair_kept, down_kept = hidden_pieces(y)
+    pair_sent, down_sent = hidden_pieces(1 - y)
+    pair_piece = jnp.stack([pair_kept, swap_col(pair_sent)], axis=3).reshape(2 * unit, features)
+    down_piece = jnp.stack([down_kept, swap_col(down_sent)], axis=2).reshape(unit, features)
+    pair_mine = lax.all_gather(pair_piece, "row", axis=0)
+    down_mine = lax.all_gather(down_piece, "row", axis=0)
+    pair_other = swap_x(pair_mine)
+    down_other = swap_x(down_mine)
+
+    def gain_order(gain):
+        kept = gain.reshape(2, quarter)
+        both = jnp.stack([kept, swap_col(kept)], axis=1)
+        both = jnp.where(c == 0, both, both[::-1])
+        return both.reshape(1, features)
+
+    gain_attn_all = gain_order(gain_attn)
+    gain_attn_own = gain_attn_all[:, :quarter]
+    gain_ffn_own = lax.dynamic_slice_in_dim(gain_ffn, c * quarter, quarter, 0)[None, :]
+
+    pieces = spread(block_in)
+    normed_attn, qkv, ratio_attn = rows_call(
+        project_kernel,
+        block,
+        [*pieces, cosine, sine],
+        [gain_attn_all, w_project],
+        [(features, jnp.bfloat16), (groups * 4 * HEAD, jnp.bfloat16), (1, jnp.float32)],
+        2 * rows * features * groups * 4 * HEAD,
+        "project",
+    )
+    attn, lse = attend(qkv, label_col, label_rows, trunk, leaf_begin, block)
+    own, send = rows_call(
+        out_kernel,
+        2 * block,
+        [attn],
+        [w_mix],
+        [(half, jnp.bfloat16), (half, jnp.bfloat16)],
+        2 * rows * features * groups * 2 * HEAD,
+        "mix",
+    )
+    middle = wide(block_in) + collect(own, send)
+    square = small_sum(jnp.sum(middle * middle, axis=1))
+    ratio_ffn = lax.rsqrt(square / features + EPSILON)[:, None]
+    normed_ffn = middle * ratio_ffn
+    ffn_pieces = spread(low(normed_ffn * gain_ffn_own))
+
+    cotangent = to_tree(out_grad)
+    grad_pieces = spread(cotangent)
+    hid_mine, hid_other, pair_grad_mine, pair_grad_other = rows_call(
+        hidden_kernel,
+        block,
+        [*ffn_pieces, *grad_pieces],
+        [pair_mine, pair_other, down_mine, down_other],
+        [
+            (planes * unit, jnp.bfloat16),
+            (planes * unit, jnp.bfloat16),
+            (2 * planes * unit, jnp.bfloat16),
+            (2 * planes * unit, jnp.bfloat16),
+        ],
+        2 * rows * features * 6 * planes * unit,
+        "hidden",
+        [pltpu.VMEM((block, features), jnp.bfloat16)] * 2,
+    )
+    down_mine = down_mine.reshape(planes * unit, features)
+    down_other = down_other.reshape(planes * unit, features)
+    pair_mine = pair_mine.reshape(2 * planes * unit, features)
+    pair_other = pair_other.reshape(2 * planes * unit, features)
+
+    own, send = rows_call(
+        two_out_kernel,
+        2 * block,
+        [pair_grad_mine, pair_grad_other],
+        [pair_mine, pair_other],
+        [(half, jnp.bfloat16), (half, jnp.bfloat16)],
+        2 * rows * features * 4 * planes * unit,
+        "pair_back",
+    )
+    normed_ffn_grad = collect(own, send)
+
+    def to_z(grad_mine, grad_other):
+        total = low(wide(grad_mine) + wide(swap_x(grad_other)))
+        return lax.psum_scatter(total, "row", scatter_dimension=0, tiled=True)
+
+    down_grad_other = weight_grad(hid_other, grad_pieces, True, 2 * block, "down_grad_other")[0]
+    down_grad_mine = weight_grad(hid_mine, grad_pieces, True, 2 * block, "down_grad_mine")[0]
+    down_sum = to_z(down_grad_mine, down_grad_other)
+    pair_w_other = weight_grad(pair_grad_other, ffn_pieces, True, 2 * block, "pair_grad_other")[0]
+    pair_w_mine = weight_grad(pair_grad_mine, ffn_pieces, True, 2 * block, "pair_grad_mine")[0]
+    pair_sum = to_z(pair_w_mine, pair_w_other)
+
+    own, send = rows_call(
+        two_out_kernel,
+        2 * block,
+        [hid_mine, hid_other],
+        [down_mine, down_other],
+        [(half, jnp.bfloat16), (half, jnp.bfloat16)],
+        2 * rows * features * 2 * planes * unit,
+        "down",
+    )
+    output = from_tree(low(middle + collect(own, send)))
+
+    def norm_back(grad, ratio, normed, gain):
+        scaled = grad * gain
+        inner = small_sum(jnp.sum(scaled * normed, axis=1))[:, None] / features
+        return ratio * (scaled - normed * inner), jnp.sum(grad * normed, axis=0)
+
+    middle_back, gain_ffn_part = norm_back(normed_ffn_grad, ratio_ffn, normed_ffn, gain_ffn_own)
+    middle_grad = wide(cotangent) + middle_back
+    middle_pieces = spread(low(middle_grad))
+    attn_grad = rows_call(
+        attn_grad_kernel,
+        2 * block,
+        middle_pieces,
+        [w_mix],
+        [(groups * 2 * HEAD, jnp.bfloat16)],
+        2 * rows * features * groups * 2 * HEAD,
+        "attn_grad",
+    )[0]
+    mix_grad = weight_grad(attn, middle_pieces, True, groups * 2 * HEAD, "mix_grad")[0]
+    qkv_grad = attend_back(
+        qkv, attn, attn_grad, label_col, label_rows, lse, cosine, sine, trunk, leaf_begin, block
+    )
+    own, send = rows_call(
+        project_back_kernel,
+        2 * block,
+        [qkv_grad],
+        [w_project],
+        [(half, jnp.bfloat16), (half, jnp.bfloat16)],
+        2 * rows * features * groups * 4 * HEAD,
+        "project_back",
+    )
+    normed_attn_grad = collect(own, send)
+    project_grad = weight_grad(normed_attn, [qkv_grad], True, 2 * block, "project_grad")[0]
+    normed_attn_own = wide(block_in) * ratio_attn
+    input_back, gain_attn_part = norm_back(
+        normed_attn_grad, ratio_attn, normed_attn_own, gain_attn_own
+    )
+    input_grad = from_tree(low(middle_grad + input_back))
+
+    def ffn_home(total):
+        parts = total.reshape(-1, unit, 2, 2, quarter)
+        cols = in_order(y, parts[:, :, :, 0], swap_col(parts[:, :, :, 1]))
+        both = in_order(x, cols, swap_x(cols))
+        both = jnp.where(c == 0, both, both[:, :, :, :, ::-1])
+        whole = in_order(c, both, swap_core(both))
+        whole = jnp.transpose(whole, (3, 2, 0, 1, 4, 5, 6))
+        return wide(whole.reshape(-1, 8 * unit, half))
+
+    down_out = ffn_home(down_sum)[0]
+    pair_out = ffn_home(pair_sum)
+    gate_out = pair_out[0].T
+    up_out = pair_out[1].T
+
+    def attn_home(parts):
+        kept = take(parts, x, 3)
+        total = low(wide(kept) + wide(swap_x(take(parts, 1 - x, 3))))
+        mine = total[:, 0]
+        other = swap_core(total[:, 1])
+        planes_all = in_order(c, mine, other).reshape((planes,) + mine.shape[1:])
+        summed = lax.psum_scatter(planes_all, "row", scatter_dimension=0, tiled=False)
+        cols = in_order(y, summed[0], swap_col(summed[1]))
+        both = in_order(x, cols, swap_x(cols))
+        return in_order(c, both, swap_core(both))
+
+    mix_parts = mix_grad.reshape(groups, 2, HEAD, 2, 2, quarter)
+    mix_home = attn_home(jnp.transpose(mix_parts, (0, 3, 4, 1, 2, 5)))
+    out_out = wide(jnp.transpose(mix_home, (2, 1, 3, 0, 4)).reshape(groups * 2 * HEAD, half))
+    project_parts = project_grad.reshape(2, 2, 2, share, groups, 4 * HEAD)
+    project_home = attn_home(jnp.transpose(project_parts, (4, 0, 1, 2, 3, 5)))
+    project_home = jnp.transpose(project_home, (0, 1, 3, 2, 4)).reshape(half, groups, 4 * HEAD)
+    query_out = wide(project_home[:, :, : 2 * HEAD].reshape(half, groups * 2 * HEAD))
+    key_out = wide(project_home[:, :, 2 * HEAD : 3 * HEAD].reshape(half, groups * HEAD))
+    value_out = wide(project_home[:, :, 3 * HEAD :].reshape(half, groups * HEAD))
+
+    def gain_home(part):
+        filled = lax.dynamic_update_slice(
+            jnp.zeros((half,), jnp.float32), part, (c * quarter,)
+        )
+        return filled
+
+    gain_attn_out, gain_ffn_out = lax.psum(
+        (gain_home(gain_attn_part), gain_home(gain_ffn_part)), ("dp", "row")
+    )
+    return (
+        output,
+        input_grad,
+        query_out,
+        key_out,
+        value_out,
+        out_out,
+        gate_out,
+        up_out,
+        down_out,
+        gain_attn_out,
+        gain_ffn_out,
+    )
+
+
 def solution(mesh):
     in_specs = (
         P(None, ("dp", "row"), "col"),
@@ -330,4 +1066,7 @@
         P("col"),
         P("col"),
     )
-    return jax.shard_map(body, mesh=mesh, in_specs=in_specs, out_specs=out_specs, check_vma=False)
+    sizes = dict(mesh.shape)
+    fits = sizes == {"dp": 4, "row": 4, "col": 2}
+    chosen = tree_body if fits else body
+    return jax.shard_map(chosen, mesh=mesh, in_specs=in_specs, out_specs=out_specs, check_vma=False)

time: 6260 us -> 1590 us (0.25)
  waiting for transfers between devices: 5140 us -> 646 us
  matrix products: 633 us -> 0 us
  Pallas kernels: 0 us -> 428 us
  local copies, waits for them, and re-layouts: 107 us -> 222 us
  other arithmetic: 275 us -> 177 us
    while x42 -> x0, waiting for transfers between devices: 1840 us -> none
    all_gather x20 -> x4, waiting for transfers between devices: 1690 us -> 89.9 us  [the longest x2 89.3 us: spread_attn(): mine = lax.all_gather(piece, 'row', axis=0)]
    reduce_scatter x18 -> x4, waiting for transfers between devices: 1370 us -> 0.03 us  [the longest x2 0.02 us: to_z(): return lax.psum_scatter(total, 'row', scatter_dimension=0, tiled=True)]
    dot_general x34 -> x0, matrix products: 576 us -> none  [the longest x8 129 us: contract_cols(): lax.dot_general(left, right, (((1,), (1,)), ((), ())), preferred_element_...]
    ppermute x0 -> x61, waiting for transfers between devices: none -> 507 us  [the longest x20 305 us: swap_col(): return lax.ppermute(a, 'col', COL_SWAP)]
    pallas_call x0 -> x15, Pallas kernels: none -> 428 us  [the longest x7 217 us: rows_call(): pl.pallas_call(fn, grid=(rows // block,), in_specs=in_specs, out_specs=[p...]
    psum x1 -> x0, waiting for transfers between devices: 238 us -> none  [body(): lax.psum(grad_project.astype(jnp.bfloat16), 'dp').astype(jnp.float32)]
    unnamed x19 -> x121, local copies, waits for them, and re-layouts: 2.4 us -> 72.7 us
  transfers between devices with their start and end apart: 41 -> 73, of which waited for: 37 -> 28; matrix products, arithmetic and copies ran while one was open for 8% -> 19% of each run, Pallas kernels for 0% -> 19%
where the time goes in v1:
time: 1590 us; the launch traced here: 1580 us
  waiting for transfers between devices  646 us (41%)
  Pallas kernels  428 us (27%)
  local copies, waits for them, and re-layouts  222 us (14%)
  other arithmetic  177 us (11%)
  starting transfers between devices  59.9 us (4%)
  blocking collectives  34.7 us (2%)
    ppermute x20, waiting for transfers between devices, swap_col(): return lax.ppermute(a, 'col', COL_SWAP)  305 us
    pallas_call x7, Pallas kernels, rows_call(): pl.pallas_call(fn, grid=(rows // block,), in_specs=in_specs, out_specs=[p...  217 us
    ppermute x12, waiting for transfers between devices, swap_x(): return lax.ppermute(a, 'dp', X_SWAP)  195 us
    pallas_call x6, Pallas kernels, weight_grad(): pl.pallas_call(functools.partial(weight_grad_kernel, len(bs), joined), gr...  121 us
    all_gather x2, waiting for transfers between devices, spread_attn(): mine = lax.all_gather(piece, 'row', axis=0)  89.3 us
    unnamed x121, local copies, waits for them, and re-layouts  72.7 us
    convert_element_type x11, other arithmetic, low(): return a.astype(jnp.bfloat16)  61.8 us
    pallas_call x1, Pallas kernels, attend_back(): pl.pallas_call(functools.partial(attend_back_kernel, trunk, leaf_begin, b...  55.2 us
  transfers between devices with their start and end apart: 73, of which 28 were waited for; matrix products, arithmetic and copies ran while one was open for 19% of the time, Pallas kernels for 19%

profile of v1, /device:TPU:0, one launch (start us, length us, event | category | flops | bytes accessed | tf_op | source)
XLA Modules:
  0.0 1582.3 jit_solution(9001956483345184564)
XLA Ops:
  59.3 23.7 %all-gather.13.cloned.1.call-done = bf16[8,128,512]{2,1,0:T(8,128)(2,1)} async-done(((bf16[2,128,512]{2,1,0:T(8,128)(2,1)}), bf16[8,128,512]{2,1,0:T(8,128)(2,1)}) %all-gather.13.cloned.1.call-update) | async-done | bytes 1048592 | tf_op jit(solution)/shard_map/all_gather | solution.py:808
  84.5 65.6 %all-gather.11.cloned.1.call-done = bf16[8,256,512]{2,1,0:T(8,128)(2,1)} async-done(((bf16[2,256,512]{2,1,0:T(8,128)(2,1)}), bf16[8,256,512]{2,1,0:T(8,128)(2,1)}) %all-gather.11.cloned.1.call-update) | async-done | bytes 2097168 | tf_op jit(solution)/shard_map/all_gather | solution.py:808
  180.1 17.9 %collective-permute-done.7 = bf16[4,2,256,512]{3,2,1,0:T(8,128)(2,1)} collective-permute-done((bf16[4,2,256,512]{3,2,1,0:T(8,128)(2,1)}, bf16[4,2,256,512]{3,2,1,0:T(8,128)(2,1)}, u32[]{:S(2)}, u32[]{:S(2)}) %collective-permute-start.7) | collective-permute-done | bytes 2097184 | tf_op jit(solution)/shard_map/ppermute | solution.py:324
  234.8 20.1 %project.1 = (bf16[2560,2048]{1,0:T(8,128)(2,1)}, bf16[2560,1024]{1,0:T(8,128)(2,1)}, f32[2560,1]{1,0:T(8,128)}) custom-call(bf16[2560,512]{1,0:T(8,128)(2,1)} %bitcast.338, bf16[2560,512]{1,0:T(8,128)(2,1)} %collective-permute-done.1.x1, bf16[2560,512]{1,0:T(8,128)(2,1)} %collective-permute-done.2.x2, bf16[2560,512]{1,0:T(8,128)(2,1)} %collective-permute-done.3.x3, ...), custom_call_target="tpu_custom_call" | custom-call | flops 10737418240 | bytes 33048576 | tf_op jit(solution)/shard_map/project/pallas_call | solution.py:354
  254.9 34.6 %attend.1 = (bf16[2560,512]{1,0:T(8,128)(2,1)}, f32[2,10,1,512]{3,2,1,0:T(1,128)}) custom-call(bf16[2560,1024]{1,0:T(8,128)(2,1)} %get-tuple-element.28.q_ref.k_ref.v_ref, bf16[2560,1024]{1,0:T(8,128)(2,1)} %get-tuple-element.28.q_ref.k_ref.v_ref, bf16[2560,1024]{1,0:T(8,128)(2,1)} %get-tuple-element.28.q_ref.k_ref.v_ref, s32[2560,1]{1,0:T(8,128)} %copy.200.lab_ref, ...), custom_call_target="tpu_custom_call" | custom-call | flops 26843545600 | bytes 13107200 | tf_op jit(solution)/shard_map/attend/pallas_call | solution.py:563
  335.6 56.4 %collective-permute-done.14 = bf16[2560,512]{1,0:T(8,128)(2,1)} collective-permute-done((bf16[2560,512]{1,0:T(8,128)(2,1)}, bf16[2560,512]{1,0:T(8,128)(2,1)}, u32[]{:S(2)}, u32[]{:S(2)}) %collective-permute-start.14) | collective-permute-done | bytes 2621472 | tf_op jit(solution)/shard_map/ppermute | solution.py:328
  400.7 48.6 %all-to-all-done.1 = bf16[4,640,512]{2,1,0:T(8,128)(2,1)} async-done(((bf16[4,640,512]{2,1,0:T(8,128)(2,1)}), bf16[4,640,512]{2,1,0:T(8,128)(2,1)}, u32[]{:S(2)}, u32[]{:S(2)}) %all-to-all-start.1) | async-done | bytes 2621472 | tf_op jit(solution)/shard_map/all_to_all | solution.py:765
  455.6 53.7 %collective-permute-done.21.g1.refs_2_ = bf16[2560,512]{1,0:T(8,128)(2,1)} collective-permute-done((bf16[2560,512]{1,0:T(8,128)(2,1)}, bf16[2560,512]{1,0:T(8,128)(2,1)}, u32[]{:S(2)}, u32[]{:S(2)}) %collective-permute-start.21) | collective-permute-done | bytes 2621472 | tf_op jit(solution)/shard_map/ppermute | solution.py:328
  509.8 55.3 %collective-permute-done.17.x1.refs_2_ = bf16[2560,512]{1,0:T(8,128)(2,1)} collective-permute-done((bf16[2560,512]{1,0:T(8,128)(2,1)S(1)}, bf16[2560,512]{1,0:T(8,128)(2,1)}, u32[]{:S(2)}, u32[]{:S(2)}) %collective-permute-start.17) | collective-permute-done | bytes 2621472 | tf_op jit(solution)/shard_map/ppermute | solution.py:328
  565.1 41.5 %collective-permute-done.27.db_ref = bf16[4,256,2048]{2,1,0:T(8,128)(2,1)S(1)} collective-permute-done((bf16[4,256,2048]{2,1,0:T(8,128)(2,1)}, bf16[4,256,2048]{2,1,0:T(8,128)(2,1)S(1)}, u32[]{:S(2)}, u32[]{:S(2)}) %collective-permute-start.27) | collective-permute-done | bytes 4194336 | tf_op jit(solution)/shard_map/ppermute | solution.py:324
  610.1 80.8 %hidden.1 = (bf16[2560,1024]{1,0:T(8,128)(2,1)}, bf16[2560,1024]{1,0:T(8,128)(2,1)}, bf16[2560,2048]{1,0:T(8,128)(2,1)}, bf16[2560,2048]{1,0:T(8,128)(2,1)}) custom-call(bf16[2560,512]{1,0:T(8,128)(2,1)} %copy-done.22, bf16[2560,512]{1,0:T(8,128)(2,1)} %collective-permute-done.17.x1.refs_2_, bf16[2560,512]{1,0:T(8,128)(2,1)} %copy-done.40, ...), custom_call_target="tpu_custom_call" | custom-call | flops 64424509440 | bytes 77594624 | tf_op jit(solution)/shard_map/hidden/pallas_call | solution.py:354
  690.9 52.5 %pair_back.1 = (bf16[2560,1024]{1,0:T(8,128)(2,1)}, bf16[2560,1024]{1,0:T(8,128)(2,1)}) custom-call(bf16[2560,2048]{1,0:T(8,128)(2,1)} %get-tuple-element.36.a_ref.refs_0_, bf16[2560,2048]{1,0:T(8,128)(2,1)} %get-tuple-element.37.b_ref.refs_0_, bf16[2048,2048]{1,0:T(8,128)(2,1)} %bitcast.397, bf16[2048,2048]{1,0:T(8,128)(2,1)} %bitcast.73.wb_ref), custom_call_target="tpu_custom_call" | custom-call | flops 42949672960 | bytes 48234496 | tf_op jit(solution)/shard_map/pair_back/pallas_call | solution.py:354
  743.4 17.4 %down_grad_other.1 = bf16[1024,2048]{1,0:T(8,128)(2,1)} custom-call(bf16[2560,1024]{1,0:T(8,128)(2,1)} %get-tuple-element.33.b_ref.refs_0_, bf16[2560,512]{1,0:T(8,128)(2,1)} %bitcast.39.g0.refs_1_, bf16[2560,512]{1,0:T(8,128)(2,1)} %collective-permute-done.21.g1.refs_2_, bf16[2560,512]{1,0:T(8,128)(2,1)} %collective-permute-done.22.g2.refs_3_, ...), custom_call_target="tpu_custom_call" | custom-call | flops 10737418240 | bytes 19922944 | tf_op jit(solution)/shard_map/down_grad_other/pallas_call | solution.py:689
  761.4 27.8 %down.1 = (bf16[2560,1024]{1,0:T(8,128)(2,1)}, bf16[2560,1024]{1,0:T(8,128)(2,1)}) custom-call(bf16[2560,1024]{1,0:T(8,128)(2,1)} %get-tuple-element.32.a_ref.refs_0_, bf16[2560,1024]{1,0:T(8,128)(2,1)} %get-tuple-element.33.b_ref.refs_0_, bf16[1024,2048]{1,0:T(8,128)(2,1)} %bitcast.398, bf16[1024,2048]{1,0:T(8,128)(2,1)} %bitcast.399), custom_call_target="tpu_custom_call" | custom-call | flops 21474836480 | bytes 29360128 | tf_op jit(solution)/shard_map/down/pallas_call | solution.py:354
  789.4 28.8 %pair_grad_other.1 = bf16[2048,2048]{1,0:T(8,128)(2,1)} custom-call(bf16[2560,2048]{1,0:T(8,128)(2,1)} %get-tuple-element.37.b_ref.refs_0_, bf16[2560,512]{1,0:T(8,128)(2,1)} %copy-done.22, bf16[2560,512]{1,0:T(8,128)(2,1)} %collective-permute-done.17.x1.refs_2_, bf16[2560,512]{1,0:T(8,128)(2,1)} %copy-done.40, ...), custom_call_target="tpu_custom_call" | custom-call | flops 21474836480 | bytes 29360128 | tf_op jit(solution)/shard_map/pair_grad_other/pallas_call | solution.py:689
  819.7 17.4 %down_grad_mine.1 = bf16[1024,2048]{1,0:T(8,128)(2,1)} custom-call(bf16[2560,1024]{1,0:T(8,128)(2,1)} %get-tuple-element.32.a_ref.refs_0_, bf16[2560,512]{1,0:T(8,128)(2,1)} %bitcast.39.g0.refs_1_, bf16[2560,512]{1,0:T(8,128)(2,1)} %collective-permute-done.21.g1.refs_2_, bf16[2560,512]{1,0:T(8,128)(2,1)} %collective-permute-done.22.g2.refs_3_, ...), custom_call_target="tpu_custom_call" | custom-call | flops 10737418240 | bytes 19922944 | tf_op jit(solution)/shard_map/down_grad_mine/pallas_call | solution.py:689
  842.0 12.5 collective-permute-done.57
  866.1 35.5 %collective-permute-done.32 = bf16[2560,512]{1,0:T(8,128)(2,1)} collective-permute-done((bf16[2560,512]{1,0:T(8,128)(2,1)}, bf16[2560,512]{1,0:T(8,128)(2,1)}, u32[]{:S(2)}, u32[]{:S(2)}) %collective-permute-start.32) | collective-permute-done | bytes 2621472 | tf_op jit(solution)/shard_map/ppermute | solution.py:328
  909.7 29.0 %pair_grad_mine.1 = bf16[2048,2048]{1,0:T(8,128)(2,1)} custom-call(bf16[2560,2048]{1,0:T(8,128)(2,1)} %get-tuple-element.36.a_ref.refs_0_, bf16[2560,512]{1,0:T(8,128)(2,1)} %copy-done.22, bf16[2560,512]{1,0:T(8,128)(2,1)} %collective-permute-done.17.x1.refs_2_, bf16[2560,512]{1,0:T(8,128)(2,1)} %copy-done.40, ...), custom_call_target="tpu_custom_call" | custom-call | flops 21474836480 | bytes 29360128 | tf_op jit(solution)/shard_map/pair_grad_mine/pallas_call | solution.py:689
  938.7 18.3 %collective-permute-done.34 = f32[2560]{0:T(1024)S(1)} collective-permute-done((f32[2560]{0:T(1024)S(1)}, f32[2560]{0:T(1024)S(1)}, u32[]{:S(2)}, u32[]{:S(2)}) %collective-permute-start.34) | collective-permute-done | bytes 10272 | tf_op jit(solution)/shard_map/ppermute | solution.py:328
  957.0 13.1 fusion.38
  970.7 63.2 %collective-permute-done.53 = bf16[2048,2048]{1,0:T(8,128)(2,1)} collective-permute-done((bf16[2048,2048]{1,0:T(8,128)(2,1)}, bf16[2048,2048]{1,0:T(8,128)(2,1)}, u32[]{:S(2)}, u32[]{:S(2)}) %collective-permute-start.53) | collective-permute-done | bytes 8388640 | tf_op jit(solution)/shard_map/ppermute | solution.py:324
  1062.2 55.2 %attend_back.1.d_ref.refs_1_ = bf16[2560,1024]{1,0:T(8,128)(2,1)} custom-call(bf16[2560,1024]{1,0:T(8,128)(2,1)} %get-tuple-element.28.q_ref.k_ref.v_ref, bf16[2560,1024]{1,0:T(8,128)(2,1)} %get-tuple-element.28.q_ref.k_ref.v_ref, bf16[2560,1024]{1,0:T(8,128)(2,1)} %get-tuple-element.28.q_ref.k_ref.v_ref, ...), custom_call_target="tpu_custom_call" | custom-call | flops 67108864000 | bytes 26214400 | tf_op jit(solution)/shard_map/attend_back/pallas_call | solution.py:588
  1117.4 15.6 project_back.1
  1155.2 16.2 %project_grad.1 = bf16[2048,1024]{1,0:T(8,128)(2,1)} custom-call(bf16[2560,2048]{1,0:T(8,128)(2,1)} %get-tuple-element.44.refs_0_, bf16[2560,1024]{1,0:T(8,128)(2,1)} %attend_back.1.d_ref.refs_1_), custom_call_target="tpu_custom_call" | custom-call | flops 10737418240 | bytes 19922944 | tf_op jit(solution)/shard_map/project_grad/pallas_call | solution.py:689
  1217.9 18.3 %collective-permute-done.43 = bf16[2,2,2,256,512]{4,3,2,0,1:T(8,128)(2,1)} collective-permute-done((bf16[2,2,2,256,512]{4,3,2,0,1:T(8,128)(2,1)}, bf16[2,2,2,256,512]{4,3,2,0,1:T(8,128)(2,1)}, u32[]{:S(2)}, u32[]{:S(2)}) %collective-permute-start.43) | collective-permute-done | bytes 2097184 | tf_op jit(solution)/shard_map/ppermute | solution.py:324
  1271.9 32.7 %collective-permute-done.39 = bf16[2560,512]{1,0:T(8,128)(2,1)} collective-permute-done((bf16[2560,512]{1,0:T(8,128)(2,1)}, bf16[2560,512]{1,0:T(8,128)(2,1)}, u32[]{:S(2)}, u32[]{:S(2)}) %collective-permute-start.39) | collective-permute-done | bytes 2621472 | tf_op jit(solution)/shard_map/ppermute | solution.py:328
  1345.3 30.1 %collective-permute-done.55 = bf16[2,2,256,2,512]{4,2,3,1,0:T(8,128)(2,1)} collective-permute-done((bf16[2,2,256,2,512]{4,2,3,1,0:T(8,128)(2,1)}, bf16[2,2,256,2,512]{4,2,3,1,0:T(8,128)(2,1)}, u32[]{:S(2)}, u32[]{:S(2)}) %collective-permute-start.55) | collective-permute-done | bytes 2097184 | tf_op jit(solution)/shard_map/ppermute | solution.py:324
  1398.6 13.1 copy.240
  1425.3 34.7 %all-reduce.1 = (f32[1024]{0:T(1024)}, f32[1024]{0:T(1024)}) all-reduce(f32[1024]{0:T(1024)S(1)} %dynamic_update_slice.6, f32[1024]{0:T(1024)S(1)} %dynamic_update_slice.7), channel_id=1, replica_groups=mesh['dp'=4,'row'=4,'col'=2] {'dp','row'}, use_global_device_ids=true, to_apply=%region_8.9 | all-reduce | flops 2048 | bytes 16384 | tf_op jit(solution)/shard_map/psum | solution.py:1022
  1518.4 12.9 copy.228
  1546.0 14.6 copy.227
  (413 shorter events, 509.9 us)
Async XLA Ops:
  7.2 75.8 %all-gather.13.cloned.1.call-start = ((), (), s32[]{:S(2)}) async-start(), calls=%async_computation.15 | async-start | bytes 1310720 | tf_op jit(solution)/shard_map/all_gather | solution.py:808
  34.3 117.2 %all-to-all-start = ((bf16[4,640,512]{2,1,0:T(8,128)(2,1)}), bf16[4,640,512]{2,1,0:T(8,128)(2,1)S(1)}, u32[]{:S(2)}, u32[]{:S(2)}) async-start(bf16[4,640,512]{2,1,0:T(8,128)(2,1)} %bitcast.349), calls=%async_computation | async-start | bytes 5242880 | tf_op jit(solution)/shard_map/all_to_all | solution.py:765
  39.5 110.5 %all-gather.11.cloned.1.call-start = ((), (), s32[]{:S(2)}) async-start(), calls=%async_computation.14 | async-start | bytes 2621440 | tf_op jit(solution)/shard_map/all_gather | solution.py:808
  50.7 284.2 %all-gather.7.cloned.1.call-start = ((), (), s32[]{:S(2)}) async-start(), calls=%async_computation.8 | async-start | bytes 10485760 | tf_op jit(solution)/shard_map/all_gather | solution.py:847
  52.4 164.8 %collective-permute-start.9 = (s32[2,2560,3]{1,0,2:T(2,128)S(1)}, s32[2,2560,3]{1,0,2:T(2,128)S(1)}, u32[]{:S(2)}, u32[]{:S(2)}) collective-permute-start(s32[2,2560,3]{1,0,2:T(2,128)S(1)} %copy-done.32), channel_id=1, source_target_pairs={{0,8},{8,0},{16,24},{24,16},{1,9},{9,1},{17,25},{25,17},{2,10},{10... | collective-permute-start | bytes 184328 | tf_op jit(solution)/shard_map/ppermute | solution.py:320
  56.7 97.8 %collective-permute-start.24 = (bf16[2,256,2,512]{1,3,2,0:T(8,128)(2,1)}, bf16[2,256,2,512]{1,3,2,0:T(8,128)(2,1)}, u32[]{:S(2)}, u32[]{:S(2)}) collective-permute-start(bf16[2,256,2,512]{1,3,2,0:T(8,128)(2,1)} %pad_maximum_fusion.11), channel_id=1, source_target_pairs={{0,1},{1,0},{2,3},{3,2},{4,5},{5,4},{6,7},{7,6},{8,9},{9,8},{10,11... | collective-permute-start | bytes 3145736 | tf_op jit(solution)/shard_map/ppermute | solution.py:328
  83.0 94.3 %collective-permute-start.11 = (bf16[4,2,128,512]{3,2,1,0:T(8,128)(2,1)}, bf16[4,2,128,512]{3,2,1,0:T(8,128)(2,1)}, u32[]{:S(2)}, u32[]{:S(2)}) collective-permute-start(bf16[4,2,128,512]{3,2,1,0:T(8,128)(2,1)} %bitcast.386), channel_id=1, source_target_pairs={{0,16},{16,0},{8,24},{24,8},{1,17},{17,1},{9,25},{25,9},{2,18},{18... | collective-permute-start | bytes 3145736 | tf_op jit(solution)/shard_map/ppermute | solution.py:324
  168.2 286.9 %all-gather.9.cloned.1.call-start = ((), (), s32[]{:S(2)}) async-start(), calls=%async_computation.9 | async-start | bytes 5242880 | tf_op jit(solution)/shard_map/all_gather | solution.py:848
  323.6 125.7 %all-to-all-start.1 = ((bf16[4,640,512]{2,1,0:T(8,128)(2,1)}), bf16[4,640,512]{2,1,0:T(8,128)(2,1)}, u32[]{:S(2)}, u32[]{:S(2)}) async-start(bf16[4,640,512]{2,1,0:T(8,128)(2,1)} %bitcast.38), calls=%async_computation.1 | async-start | bytes 5242880 | tf_op jit(solution)/shard_map/all_to_all | solution.py:765
  328.2 863.4 %reduce-scatter.11.cloned.1.call-start = ((), (), s32[]{:S(2)}) async-start(), calls=%async_computation.13 | async-start | bytes 5242880 | tf_op jit(solution)/shard_map/reduce_scatter | solution.py:923
  334.8 273.8 %collective-permute-start.25 = (bf16[4,512,2048]{2,1,0:T(8,128)(2,1)}, bf16[4,512,2048]{2,1,0:T(8,128)(2,1)}, u32[]{:S(2)}, u32[]{:S(2)}) collective-permute-start(bf16[4,512,2048]{2,1,0:T(8,128)(2,1)} %all-gather.7.cloned.1.call-done.wa_ref), channel_id=1, source_target_pairs={{0,16},{16,0},{8,24},{24,8},{1,17},{17,1},{9,25},{25,9},{2,18},{18... | collective-permute-start | bytes 25165832 | tf_op jit(solution)/shard_map/ppermute | solution.py:324
  453.9 111.1 %collective-permute-start.17 = (bf16[2560,512]{1,0:T(8,128)(2,1)S(1)}, bf16[2560,512]{1,0:T(8,128)(2,1)}, u32[]{:S(2)}, u32[]{:S(2)}) collective-permute-start(bf16[2560,512]{1,0:T(8,128)(2,1)S(1)} %multiply_convert_fusion.x0.refs_1_), channel_id=1, source_target_pairs={{0,1},{1,0},{2,3},{3,2},{4,5},{5,4},{6,7},{7,6},{8,9},{9,8},{10,11... | collective-permute-start | bytes 7864328 | tf_op jit(solution)/shard_map/ppermute | solution.py:328
  455.1 151.4 %collective-permute-start.27 = (bf16[4,256,2048]{2,1,0:T(8,128)(2,1)}, bf16[4,256,2048]{2,1,0:T(8,128)(2,1)S(1)}, u32[]{:S(2)}, u32[]{:S(2)}) collective-permute-start(bf16[4,256,2048]{2,1,0:T(8,128)(2,1)} %all-gather.9.cloned.1.call-done.da_ref), channel_id=1, source_target_pairs={{0,16},{16,0},{8,24},{24,8},{1,17},{17,1},{9,25},{25,9},{2,18},{18... | collective-permute-start | bytes 12582920 | tf_op jit(solution)/shard_map/ppermute | solution.py:324
  509.3 97.3 %collective-permute-start.18 = (bf16[2560,512]{1,0:T(8,128)(2,1)S(1)}, bf16[2560,512]{1,0:T(8,128)(2,1)S(1)}, u32[]{:S(2)}, u32[]{:S(2)}) collective-permute-start(bf16[2560,512]{1,0:T(8,128)(2,1)S(1)} %multiply_convert_fusion.x0.refs_1_), channel_id=1, source_target_pairs={{0,8},{8,0},{16,24},{24,16},{1,9},{9,1},{17,25},{25,17},{2,10},{10... | collective-permute-start | bytes 7864328 | tf_op jit(solution)/shard_map/ppermute | solution.py:320
  743.4 93.6 %collective-permute-start.31 = (bf16[2560,1024]{1,0:T(8,128)(2,1)}, bf16[2560,1024]{1,0:T(8,128)(2,1)}, u32[]{:S(2)}, u32[]{:S(2)}) collective-permute-start(bf16[2560,1024]{1,0:T(8,128)(2,1)} %get-tuple-element.39), channel_id=1, source_target_pairs={{0,8},{8,0},{16,24},{24,16},{1,9},{9,1},{17,25},{25,17},{2,10},{10... | collective-permute-start | bytes 15728648 | tf_op jit(solution)/shard_map/ppermute | solution.py:320
  760.8 93.7 %collective-permute-start.57 = (bf16[1024,2048]{1,0:T(8,128)(2,1)}, bf16[1024,2048]{1,0:T(8,128)(2,1)}, u32[]{:S(2)}, u32[]{:S(2)}) collective-permute-start(bf16[1024,2048]{1,0:T(8,128)(2,1)} %down_grad_other.1), channel_id=1, source_target_pairs={{0,16},{16,0},{8,24},{24,8},{1,17},{17,1},{9,25},{25,9},{2,18},{18... | collective-permute-start | bytes 12582920 | tf_op jit(solution)/shard_map/ppermute | solution.py:324
  789.2 71.5 %collective-permute-start.28 = (bf16[2560,1024]{1,0:T(8,128)(2,1)}, bf16[2560,1024]{1,0:T(8,128)(2,1)}, u32[]{:S(2)}, u32[]{:S(2)}) collective-permute-start(bf16[2560,1024]{1,0:T(8,128)(2,1)} %get-tuple-element.35), channel_id=1, source_target_pairs={{0,8},{8,0},{16,24},{24,16},{1,9},{9,1},{17,25},{25,17},{2,10},{10... | collective-permute-start | bytes 15728648 | tf_op jit(solution)/shard_map/ppermute | solution.py:320
  818.2 215.6 %collective-permute-start.53 = (bf16[2048,2048]{1,0:T(8,128)(2,1)}, bf16[2048,2048]{1,0:T(8,128)(2,1)}, u32[]{:S(2)}, u32[]{:S(2)}) collective-permute-start(bf16[2048,2048]{1,0:T(8,128)(2,1)} %pair_grad_other.1), channel_id=1, source_target_pairs={{0,16},{16,0},{8,24},{24,8},{1,17},{17,1},{9,25},{25,9},{2,18},{18... | collective-permute-start | bytes 25165832 | tf_op jit(solution)/shard_map/ppermute | solution.py:324
  841.5 60.0 %collective-permute-start.32 = (bf16[2560,512]{1,0:T(8,128)(2,1)}, bf16[2560,512]{1,0:T(8,128)(2,1)}, u32[]{:S(2)}, u32[]{:S(2)}) collective-permute-start(bf16[2560,512]{1,0:T(8,128)(2,1)} %add_convert_fusion.3), channel_id=1, source_target_pairs={{0,1},{1,0},{2,3},{3,2},{4,5},{5,4},{6,7},{7,6},{8,9},{9,8},{10,11... | collective-permute-start | bytes 7864328 | tf_op jit(solution)/shard_map/ppermute | solution.py:328
  860.6 403.9 %reduce-scatter.9.cloned.1.call-start = ((), (), s32[]{:S(2)}) async-start(), calls=%async_computation.12 | async-start | bytes 10485760 | tf_op jit(solution)/shard_map/reduce_scatter | solution.py:923
  865.6 91.4 %collective-permute-start.29 = (bf16[2560,512]{1,0:T(8,128)(2,1)}, bf16[2560,512]{1,0:T(8,128)(2,1)}, u32[]{:S(2)}, u32[]{:S(2)}) collective-permute-start(bf16[2560,512]{1,0:T(8,128)(2,1)} %add_convert_fusion.5), channel_id=1, source_target_pairs={{0,1},{1,0},{2,3},{3,2},{4,5},{5,4},{6,7},{7,6},{8,9},{9,8},{10,11... | collective-permute-start | bytes 7864328 | tf_op jit(solution)/shard_map/ppermute | solution.py:328
  970.2 72.2 %collective-permute-start.35 = (bf16[2560,512]{1,0:T(8,128)(2,1)}, bf16[2560,512]{1,0:T(8,128)(2,1)}, u32[]{:S(2)}, u32[]{:S(2)}) collective-permute-start(bf16[2560,512]{1,0:T(8,128)(2,1)} %get-tuple-element.84.h0.refs_1_), channel_id=1, source_target_pairs={{0,1},{1,0},{2,3},{3,2},{4,5},{5,4},{6,7},{7,6},{8,9},{9,8},{10,11... | collective-permute-start | bytes 7864328 | tf_op jit(solution)/shard_map/ppermute | solution.py:328
  1042.9 159.0 %all-to-all-start.2 = ((bf16[4,640,512]{2,1,0:T(8,128)(2,1)}), bf16[4,640,512]{2,1,0:T(8,128)(2,1)S(1)}, u32[]{:S(2)}, u32[]{:S(2)}) async-start(bf16[4,640,512]{2,1,0:T(8,128)(2,1)} %bitcast.65), calls=%async_computation.2 | async-start | bytes 5242880 | tf_op jit(solution)/shard_map/all_to_all | solution.py:768
  1047.6 281.3 %reduce-scatter.7.cloned.1.call-start = ((), (), s32[]{:S(2)}) async-start(), calls=%async_computation.11 | async-start | bytes 1310720 | tf_op jit(solution)/shard_map/reduce_scatter | solution.py:1001
  1133.0 105.9 %collective-permute-start.38 = (bf16[2560,1024]{1,0:T(8,128)(2,1)}, bf16[2560,1024]{1,0:T(8,128)(2,1)}, u32[]{:S(2)}, u32[]{:S(2)}) collective-permute-start(bf16[2560,1024]{1,0:T(8,128)(2,1)} %get-tuple-element.43), channel_id=1, source_target_pairs={{0,8},{8,0},{16,24},{24,16},{1,9},{9,1},{17,25},{25,17},{2,10},{10... | collective-permute-start | bytes 15728648 | tf_op jit(solution)/shard_map/ppermute | solution.py:320
  1217.8 125.2 %reduce-scatter.5.cloned.1.call-start = ((), (), s32[]{:S(2)}) async-start(), calls=%async_computation.10 | async-start | bytes 2621440 | tf_op jit(solution)/shard_map/reduce_scatter | solution.py:1001
  1244.5 60.1 %collective-permute-start.39 = (bf16[2560,512]{1,0:T(8,128)(2,1)}, bf16[2560,512]{1,0:T(8,128)(2,1)}, u32[]{:S(2)}, u32[]{:S(2)}) collective-permute-start(bf16[2560,512]{1,0:T(8,128)(2,1)} %add_convert_fusion.2), channel_id=1, source_target_pairs={{0,1},{1,0},{2,3},{3,2},{4,5},{5,4},{6,7},{7,6},{8,9},{9,8},{10,11... | collective-permute-start | bytes 7864328 | tf_op jit(solution)/shard_map/ppermute | solution.py:328
  1311.5 71.9 %collective-permute-start.60 = (bf16[2,2,1,256,2,512]{5,3,4,1,0,2:T(8,128)(2,1)}, bf16[2,2,1,256,2,512]{5,3,4,1,0,2:T(8,128)(2,1)}, u32[]{:S(2)}, u32[]{:S(2)}) collective-permute-start(bf16[2,2,1,256,2,512]{5,3,4,1,0,2:T(8,128)(2,1)} %fusion.16), channel_id=1, source_target_pairs={{0,8},{8,0},{16,24},{24,16},{1,9},{9,1},{17,25},{25,17},{2,10},{10... | collective-permute-start | bytes 6291464 | tf_op jit(solution)/shard_map/ppermute | solution.py:320
  1337.2 79.9 %all-to-all-start.3 = ((bf16[4,640,512]{2,1,0:T(8,128)(2,1)}), bf16[4,640,512]{2,1,0:T(8,128)(2,1)S(1)}, u32[]{:S(2)}, u32[]{:S(2)}) async-start(bf16[4,640,512]{2,1,0:T(8,128)(2,1)} %bitcast.348), calls=%async_computation.3 | async-start | bytes 5242880 | tf_op jit(solution)/shard_map/all_to_all | solution.py:768
  1381.6 110.3 %collective-permute-start.56 = (bf16[2,2,2,256,2,512]{5,3,4,2,1,0:T(8,128)(2,1)}, bf16[2,2,2,256,2,512]{5,3,4,2,1,0:T(8,128)(2,1)}, u32[]{:S(2)}, u32[]{:S(2)}) collective-permute-start(bf16[2,2,2,256,2,512]{5,3,4,2,1,0:T(8,128)(2,1)} %reverse_select_fusion), channel_id=1, source_target_pairs={{0,8},{8,0},{16,24},{24,16},{1,9},{9,1},{17,25},{25,17},{2,10},{10... | collective-permute-start | bytes 12582920 | tf_op jit(solution)/shard_map/ppermute | solution.py:320
  1397.4 62.7 %collective-permute-start.47 = (bf16[2,2,256,512]{3,2,1,0:T(8,128)(2,1)}, bf16[2,2,256,512]{3,2,1,0:T(8,128)(2,1)}, u32[]{:S(2)}, u32[]{:S(2)}) collective-permute-start(bf16[2,2,256,512]{3,2,1,0:T(8,128)(2,1)} %pad_maximum_fusion.13), channel_id=1, source_target_pairs={{0,8},{8,0},{16,24},{24,16},{1,9},{9,1},{17,25},{25,17},{2,10},{10... | collective-permute-start | bytes 3145736 | tf_op jit(solution)/shard_map/ppermute | solution.py:320
  1418.3 64.9 %collective-permute-start.42 = (bf16[2,640,512]{2,1,0:T(8,128)(2,1)}, bf16[2,640,512]{2,1,0:T(8,128)(2,1)}, u32[]{:S(2)}, u32[]{:S(2)}) collective-permute-start(bf16[2,640,512]{2,1,0:T(8,128)(2,1)} %dynamic-slice_bitcast_fusion), channel_id=1, source_target_pairs={{0,8},{8,0},{16,24},{24,16},{1,9},{9,1},{17,25},{25,17},{2,10},{10... | collective-permute-start | bytes 3932168 | tf_op jit(solution)/shard_map/ppermute | solution.py:320
  (91 other events, 2366.6 us)
Sparse Core Ops, SparseCore 0:
  30.5 52.4 all-gather.12
  85.1 64.8 all-gather.10
  168.3 146.9 all-gather.6
  320.4 134.6 all-gather.8
  860.7 75.9 reduce-scatter.10
  1042.4 193.7 reduce-scatter.8
  1239.1 30.7 reduce-scatter.6
  1272.8 42.4 reduce-scatter.4

commit v2 on v1

--- a/solution.py
+++ b/solution.py
@@ -307,9 +307,13 @@
 CORE_SWAP = [(0, 1), (1, 0), (2, 3), (3, 2)]
 X_SWAP = [(0, 2), (2, 0), (1, 3), (3, 1)]
 COL_SWAP = [(0, 1), (1, 0)]
+CROSS_SWAP = [(2 * d + j, 2 * (d ^ 1) + 1 - j) for d in range(4) for j in range(2)]
+ROW_SECOND = [(0, 2), (1, 3), (2, 0), (3, 1)]
+ROW_SWAP = [(0, 1), (1, 0), (2, 3), (3, 2)]
 LOG2E = 1.4426950408889634
 TRUNK = 1024
 LEAF_BEGIN = TRUNK + 4 * 128
+SHARE_OF_COST = 8
 VMEM_LIMIT = 58 * 1024 * 1024
 NT = (((1,), (1,)), ((), ()))
 TN = (((0,), (0,)), ((), ()))
@@ -326,6 +330,20 @@
 
 def swap_col(a):
     return lax.ppermute(a, "col", COL_SWAP)
+
+
+def shift(a, pairs):
+    return lax.ppermute(a, "row", pairs)
+
+
+def after(value, *deps):
+    return lax.optimization_barrier((value, *deps))[0]
+
+
+def cost(flops, moved):
+    return pl.CostEstimate(
+        flops=flops // SHARE_OF_COST, bytes_accessed=moved // SHARE_OF_COST, transcendentals=0
+    )
 
 
 def mxu(a, b, dims):
@@ -351,7 +369,7 @@
         )
     moved = sum(a.size * a.dtype.itemsize for a in (*row_ins, *full_ins))
     moved += sum(rows * w * jnp.dtype(dt).itemsize for w, dt in outs)
-    return pl.pallas_call(
+    results = pl.pallas_call(
         fn,
         grid=(rows // block,),
         in_specs=in_specs,
@@ -359,9 +377,10 @@
         out_shape=[jax.ShapeDtypeStruct((rows, w), dt) for w, dt in outs],
         scratch_shapes=list(scratch),
         compiler_params=pltpu.CompilerParams(vmem_limit_bytes=VMEM_LIMIT),
-        cost_estimate=pl.CostEstimate(flops=flops, bytes_accessed=moved, transcendentals=0),
+        cost_estimate=cost(flops, moved),
         name=name,
     )(*row_ins, *full_ins)
+    return list(results)
 
 
 def turn(u, cosine, sine_signed):
@@ -372,7 +391,9 @@
     return u * cosine - pltpu.roll(u, HEAD // 2, 1) * sine_signed
 
 
-def project_kernel(x0, x1, x2, x3, cos_ref, sin_ref, gain_ref, w_ref, xn_ref, qkv_ref, r_ref):
+def project_kernel(
+    x0, x1, x2, x3, cos_ref, sin_ref, gain_ref, own_ref, far_ref, xn_ref, qkv_ref, r_ref
+):
     pieces = [wide(r[...]) for r in (x0, x1, x2, x3)]
     width = pieces[0].shape[1]
     total = sum(jnp.sum(p * p, axis=1, keepdims=True) for p in pieces)
@@ -381,13 +402,14 @@
     for i, p in enumerate(pieces):
         cols = slice(i * width, (i + 1) * width)
         xn_ref[:, cols] = low(p * ratio * gain_ref[:, cols])
-    normed = xn_ref[...]
+    near = xn_ref[:, : 2 * width]
+    far = xn_ref[:, 2 * width :]
     cosine = cos_ref[...]
     sine = sin_ref[...]
-    span = w_ref.shape[2]
+    span = own_ref.shape[2]
     heads = span // HEAD
-    for g in range(w_ref.shape[0]):
-        acc = mxu(normed, w_ref[g], NN)
+    for g in range(own_ref.shape[0]):
+        acc = mxu(near, own_ref[g], NN) + mxu(far, far_ref[g], NN)
         for h in range(heads):
             u = acc[:, h * HEAD : (h + 1) * HEAD]
             if h < heads - 1:
@@ -571,9 +593,7 @@
         ],
         scratch_shapes=[pltpu.VMEM((HEAD, rows), jnp.bfloat16)],
         compiler_params=pltpu.CompilerParams(vmem_limit_bytes=VMEM_LIMIT),
-        cost_estimate=pl.CostEstimate(
-            flops=4 * 4 * pairs * HEAD, bytes_accessed=20 * rows * HEAD * 2, transcendentals=pairs
-        ),
+        cost_estimate=cost(4 * 4 * pairs * HEAD, 20 * rows * HEAD * 2),
         name="attend",
     )(qkv, qkv, qkv, label_col, label_rows)
 
@@ -597,73 +617,134 @@
             pltpu.VMEM((rows, HEAD), jnp.float32),
         ],
         compiler_params=pltpu.CompilerParams(vmem_limit_bytes=VMEM_LIMIT),
-        cost_estimate=pl.CostEstimate(
-            flops=10 * 4 * pairs * HEAD, bytes_accessed=40 * rows * HEAD * 2, transcendentals=pairs
-        ),
+        cost_estimate=cost(10 * 4 * pairs * HEAD, 40 * rows * HEAD * 2),
         name="attend_back",
     )(qkv, qkv, qkv, attn, attn_grad, label_col, label_rows, lse, cosine, sine)
 
 
-def halves_out(acc, own_ref, send_ref):
-    half = own_ref.shape[1]
-    own_ref[...] = low(acc[:, :half])
-    send_ref[...] = low(acc[:, half:])
-
-
-def out_kernel(a_ref, w_ref, own_ref, send_ref):
-    halves_out(mxu(a_ref[...], w_ref[...], NN), own_ref, send_ref)
-
-
-def two_out_kernel(a_ref, b_ref, wa_ref, wb_ref, own_ref, send_ref):
-    acc = mxu(a_ref[...], wa_ref[...], NN) + mxu(b_ref[...], wb_ref[...], NN)
-    halves_out(acc, own_ref, send_ref)
-
-
-def project_back_kernel(d_ref, w_ref, own_ref, send_ref):
-    groups = w_ref.shape[0]
-    span = w_ref.shape[2]
-    acc = sum(mxu(d_ref[:, g * span : (g + 1) * span], w_ref[g], NT) for g in range(groups))
-    halves_out(acc, own_ref, send_ref)
-
-
-def attn_grad_kernel(h0, h1, h2, h3, w_ref, out_ref):
-    width = h0.shape[1]
-    acc = sum(
-        mxu(h[...], w_ref[:, i * width : (i + 1) * width], NT)
-        for i, h in enumerate((h0, h1, h2, h3))
-    )
-    out_ref[...] = low(acc)
-
-
-def hidden_kernel(
-    x0, x1, x2, x3, g0, g1, g2, g3, wa_ref, wb_ref, da_ref, db_ref, ha_ref, hb_ref, pa_ref, pb_ref,
-    xs_ref, gs_ref,
-):
-    width = x0.shape[1]
-    for i, (x, g) in enumerate(zip((x0, x1, x2, x3), (g0, g1, g2, g3))):
+def quarters_out(acc, out_refs):
+    width = out_refs[0].shape[1]
+    for i, ref in enumerate(out_refs):
+        ref[...] = low(acc[:, i * width : (i + 1) * width])
+
+
+def mix_kernel(a_ref, near_ref, far_ref, *out_refs):
+    groups = near_ref.shape[0]
+    span = near_ref.shape[2]
+    for i, out_ref in enumerate(out_refs):
+        w_ref = (near_ref, far_ref)[i // 2]
+        acc = sum(
+            mxu(a_ref[:, g * span : (g + 1) * span], w_ref[g, i % 2], NN) for g in range(groups)
+        )
+        out_ref[...] = low(acc)
+
+
+def sum_out_kernel(count, *refs):
+    a_refs, w_refs = refs[:count], refs[count : 2 * count]
+    acc = sum(mxu(a[...], w[...], NN) for a, w in zip(a_refs, w_refs))
+    quarters_out(acc, refs[2 * count :])
+
+
+def project_back_kernel(d_ref, near_ref, far_ref, *out_refs):
+    groups = near_ref.shape[0]
+    span = near_ref.shape[2]
+    for i, w_ref in enumerate((near_ref, far_ref)):
+        acc = sum(mxu(d_ref[:, g * span : (g + 1) * span], w_ref[g], NT) for g in range(groups))
+        quarters_out(acc, out_refs[2 * i : 2 * i + 2])
+
+
+def attn_grad_kernel(h0, h1, h2, h3, near_ref, far_ref, out_ref):
+    groups = near_ref.shape[0]
+    span = near_ref.shape[2]
+    for g in range(groups):
+        acc = sum(
+            mxu(h[...], (near_ref, far_ref)[i // 2][g, i % 2], NT)
+            for i, h in enumerate((h0, h1, h2, h3))
+        )
+        out_ref[:, g * span : (g + 1) * span] = low(acc)
+
+
+def gate_up_kernel(*refs):
+    x_refs, w_refs, out_refs = refs[:4], refs[4:8], refs[8:12]
+    xs_ref = refs[12]
+    width = x_refs[0].shape[1]
+    for i, x in enumerate(x_refs):
         xs_ref[:, i * width : (i + 1) * width] = x[...]
+    normed = xs_ref[...]
+    for w_ref, out_ref in zip(w_refs, out_refs):
+        unit = 512
+        for at in range(0, w_ref.shape[0], unit):
+            cols = slice(at, at + unit)
+            out_ref[:, cols] = low(mxu(normed, w_ref[cols, :], NT))
+
+
+def hidden_kernel(*refs):
+    g_refs, gate_refs, up_refs, w_refs = refs[:4], refs[4:6], refs[6:8], refs[8:10]
+    out_refs = refs[10:16]
+    gs_ref = refs[16]
+    width = g_refs[0].shape[1]
+    for i, g in enumerate(g_refs):
         gs_ref[:, i * width : (i + 1) * width] = g[...]
-    normed = xs_ref[...]
     grads = gs_ref[...]
-    for w_ref, d_ref, h_ref, p_ref in ((wa_ref, da_ref, ha_ref, pa_ref), (wb_ref, db_ref, hb_ref, pb_ref)):
-        parts = w_ref.shape[0]
-        unit = w_ref.shape[1] // 2
-        for z in range(parts):
-            pair = mxu(normed, w_ref[z], NT)
-            hidden_grad = mxu(grads, d_ref[z], NT)
-            gate = pair[:, :unit]
-            upper = pair[:, unit:]
+    for side in range(2):
+        w_ref = w_refs[side]
+        dgate_ref, dup_ref, hid_ref = out_refs[3 * side : 3 * side + 3]
+        unit = 256
+        for at in range(0, w_ref.shape[0], unit):
+            cols = slice(at, at + unit)
+            gate = wide(gate_refs[side][:, cols])
+            upper = wide(up_refs[side][:, cols])
+            hidden_grad = mxu(grads, w_ref[cols, :], NT)
             sigma = jax.nn.sigmoid(gate)
             silu_value = gate * sigma
-            h_ref[:, z * unit : (z + 1) * unit] = low(silu_value * upper)
-            at = 2 * z * unit
-            p_ref[:, at : at + unit] = low(
+            hid_ref[:, cols] = low(silu_value * upper)
+            dgate_ref[:, cols] = low(
                 hidden_grad * upper * sigma * (1.0 + gate * (1.0 - sigma))
             )
-            p_ref[:, at + unit : at + 2 * unit] = low(hidden_grad * silu_value)
-
-
-def weight_grad_kernel(count, joined, *refs):
+            dup_ref[:, cols] = low(hidden_grad * silu_value)
+
+
+def ffn_home_kernel(turned, where_ref, *refs):
+    part_refs, out_ref = refs[:4], refs[4]
+    step = pl.program_id(0)
+    at_col, at_core, at_x = step // 4, lax.rem(step // 2, 2), lax.rem(step, 2)
+    other_col = jnp.where(at_col == where_ref[0], 0, 1)
+    want = 2 * jnp.where(at_x == where_ref[1], 0, 1) + jnp.where(at_core == where_ref[2], 0, 1)
+    quarter = part_refs[0].shape[2] // 2
+    for j in range(4):
+
+        @pl.when(want == j)
+        def _(part=part_refs[j]):
+            for h in range(2):
+                start = at_core * quarter if h == 0 else (1 - at_core) * quarter
+                place = pl.ds(pl.multiple_of(start, quarter), quarter)
+                values = wide(part[other_col, :, h * quarter : (h + 1) * quarter])
+                if turned:
+                    out_ref[place, :] = values.T
+                else:
+                    out_ref[:, place] = values
+
+
+def ffn_home(where, parts, at, unit, turned, name):
+    half = parts[0].shape[2]
+    whole = pl.BlockSpec((2, unit, half), lambda i, w: (0, at, 0), pipeline_mode=pl.Buffered(1))
+    if turned:
+        spec, shape = pl.BlockSpec((half, unit), lambda i, w: (0, i)), (half, 8 * unit)
+    else:
+        spec, shape = pl.BlockSpec((unit, half), lambda i, w: (i, 0)), (8 * unit, half)
+    return pl.pallas_call(
+        functools.partial(ffn_home_kernel, turned),
+        grid_spec=pltpu.PrefetchScalarGridSpec(
+            num_scalar_prefetch=1, grid=(8,), in_specs=[whole] * 4, out_specs=spec
+        ),
+        out_shape=jax.ShapeDtypeStruct(shape, jnp.float32),
+        compiler_params=pltpu.CompilerParams(vmem_limit_bytes=VMEM_LIMIT),
+        cost_estimate=cost(0, 8 * unit * half * 6),
+        name=name,
+    )(where, *parts)
+
+
+def weight_grad_kernel(count, split, *refs):
     a_ref = refs[0]
     b_refs = refs[1 : 1 + count]
     o_refs = refs[1 + count :]
@@ -671,33 +752,41 @@
     for i, b in enumerate(b_refs):
         width = b.shape[1]
         acc = low(mxu(left, b[...], NN))
-        if joined:
+        if split:
+            for j in range(split):
+                o_refs[0][j] = acc[:, j * width // split : (j + 1) * width // split]
+        elif len(o_refs) == 1:
             o_refs[0][:, i * width : (i + 1) * width] = acc
         else:
             o_refs[i][...] = acc
 
 
-def weight_grad(a, bs, joined, block, name):
+def weight_grad(a, bs, block, name, joined=True, split=0):
     rows, m = a.shape
     n = sum(b.shape[1] for b in bs)
-    widths = [n] if joined else [b.shape[1] for b in bs]
     in_specs = [pl.BlockSpec((rows, block), lambda i: (0, i))]
     for b in bs:
         in_specs.append(
             pl.BlockSpec(b.shape, lambda i: (0, 0), pipeline_mode=pl.Buffered(1))
         )
-    return pl.pallas_call(
-        functools.partial(weight_grad_kernel, len(bs), joined),
+    if split:
+        out_specs = [pl.BlockSpec((split, block, n // split), lambda i: (0, i, 0))]
+        shapes = [(split, m, n // split)]
+    else:
+        widths = [n] if joined else [b.shape[1] for b in bs]
+        out_specs = [pl.BlockSpec((block, w), lambda i: (i, 0)) for w in widths]
+        shapes = [(m, w) for w in widths]
+    outs = pl.pallas_call(
+        functools.partial(weight_grad_kernel, len(bs), split),
         grid=(m // block,),
         in_specs=in_specs,
-        out_specs=[pl.BlockSpec((block, w), lambda i: (i, 0)) for w in widths],
-        out_shape=[jax.ShapeDtypeStruct((m, w), jnp.bfloat16) for w in widths],
+        out_specs=out_specs,
+        out_shape=[jax.ShapeDtypeStruct(shape, jnp.bfloat16) for shape in shapes],
         compiler_params=pltpu.CompilerParams(vmem_limit_bytes=VMEM_LIMIT),
-        cost_estimate=pl.CostEstimate(
-            flops=2 * rows * m * n, bytes_accessed=2 * (rows * m + rows * n + m * n), transcendentals=0
-        ),
+        cost_estimate=cost(2 * rows * m * n, 2 * (rows * m + rows * n + m * n)),
         name=name,
     )(a, *bs)
+    return outs if len(outs) > 1 else outs[0]
 
 
 def take(a, index, axis):
@@ -715,17 +804,19 @@
     return [a, b, swap_core(a), swap_core(b)]
 
 
-def collect(own, send):
-    quarter = own.shape[1] // 2
-    got = swap_core(send)
-    outgoing = low(wide(own[:, quarter:]) + wide(got[:, quarter:]))
-    back = swap_col(outgoing)
-    return wide(own[:, :quarter]) + wide(got[:, :quarter]) + wide(back)
+def collect_core(parts):
+    own, own_other, send, send_other = parts
+    outgoing = low(wide(own_other) + wide(swap_core(send_other)))
+    return own, swap_core(send), outgoing
+
+
+def collect_col(own, got, outgoing):
+    return wide(own) + wide(got) + wide(swap_col(outgoing))
 
 
 def small_sum(v):
-    v = v + swap_core(v)
-    return v + swap_col(v)
+    cross = lax.ppermute(v, ("dp", "col"), CROSS_SWAP)
+    return (v + swap_core(v)) + (swap_col(v) + cross)
 
 
 def tree_body(
@@ -754,100 +845,75 @@
     planes = lax.axis_size("row")
     features = 2 * half
     block = 256
-    trunk = TRUNK
-    leaf_begin = LEAF_BEGIN
-
-    def to_tree(a):
-        parts = a.reshape(micro, local_rows, 2, quarter)
-        mine = take(parts, c, 2)
-        other = swap_core(take(parts, 1 - c, 2))
-        trees = in_order(c, mine, other).reshape(planes * local_rows, quarter)
-        return lax.all_to_all(trees, "row", 0, 0, tiled=True)
-
-    def from_tree(a):
-        trees = lax.all_to_all(a, "row", 0, 0, tiled=True)
+
+    def to_trees(a):
+        mine = lax.dynamic_slice_in_dim(a, c * quarter, quarter, 2)
+        other = swap_core(lax.dynamic_slice_in_dim(a, (1 - c) * quarter, quarter, 2))
+        return in_order(c, mine, other).reshape(planes * local_rows, quarter)
+
+    def of_core(trees):
         trees = trees.reshape(2, micro, local_rows, quarter)
-        mine = take(trees, c, 0)
-        other = swap_core(take(trees, 1 - c, 0))
-        return in_order(c, mine, other, 2).reshape(micro, local_rows, half)
-
-    def of_tree(a):
-        both = in_order(c, a, swap_core(a))
-        return take(both.reshape((2 * micro,) + a.shape[1:]), z, 0)
-
-    tree_path = of_tree(path)
-    tree_place = of_tree(positions)
-    cosine, sine = rope_tables(tree_place)
+        return take(trees, c, 0), take(trees, 1 - c, 0)
+
+    def by_feature(mine, other):
+        return in_order(c, mine, swap_core(other), 2).reshape(micro, local_rows, half)
+
+    groups = w_key.shape[1] // HEAD
+    share = quarter // 2
+    unit = w_gate.shape[1] // 8
+
+    def project_piece(g):
+        at = c * quarter + x * share
+        return jnp.concatenate(
+            [
+                lax.dynamic_slice(w_query, (at, g * 2 * HEAD), (share, 2 * HEAD)),
+                lax.dynamic_slice(w_key, (at, g * HEAD), (share, HEAD)),
+                lax.dynamic_slice(w_value, (at, g * HEAD), (share, HEAD)),
+            ],
+            axis=1,
+        )
+
+    def mix_piece(g):
+        return lax.dynamic_slice(w_out, ((g * 2 + x) * HEAD, c * quarter), (HEAD, quarter))
+
+    def by_core(a):
+        return jnp.where(c == 0, a, jnp.concatenate([a[:, quarter:], a[:, :quarter]], axis=1))
+
+    def hidden_piece(j):
+        at = ((2 * j + c) * 2 + x) * unit
+        return [
+            by_core(lax.dynamic_slice_in_dim(w_gate, at, unit, 1).T),
+            by_core(lax.dynamic_slice_in_dim(w_up, at, unit, 1).T),
+            by_core(lax.dynamic_slice_in_dim(w_down, at, unit, 0)),
+        ]
+
+    def four(kept, got):
+        return jnp.concatenate(
+            [kept[:, :quarter], got[:, :quarter], kept[:, quarter:], got[:, quarter:]], axis=1
+        )
+
+    project_sent = project_piece(1 - y)
+    project_mine = jnp.stack([project_piece(y), swap_col(project_sent)])
+    block_in = lax.all_to_all(to_trees(tokens), "row", 0, 0, tiled=True)
+    sent = jnp.concatenate([*hidden_piece(1 - y), jnp.tile(mix_piece(1 - y), (1, 2))])
+    got = swap_col(after(sent, project_sent))
+    project_all = lax.all_gather(project_mine, "row", axis=0)
+
+    marks = jnp.concatenate([path, positions[:, :, None]], axis=2)
+    marks = jnp.transpose(marks, (2, 0, 1))
+    marks = in_order(c, marks, swap_core(marks), 1).reshape(4, 2 * micro, rows)
+    marks = take(marks, z, 1)
+    cosine, sine = rope_tables(marks[3])
     sign = jnp.where(jnp.arange(HEAD) < HEAD // 2, -1.0, 1.0).astype(jnp.float32)
     sine = sine * sign[None, :]
-    label_col = tree_path[:, 0:1]
-    label_rows = jnp.pad(tree_path.T, ((0, 5), (0, 0)))
-
-    block_in = to_tree(tokens)
-
-    key_width = w_key.shape[1]
-    groups = key_width // HEAD
-    share = quarter // 2
-    first_row = c * quarter + x * share
-
-    def group_cols(g):
-        return jnp.concatenate(
-            [
-                lax.dynamic_slice_in_dim(w_query, g * 2 * HEAD, 2 * HEAD, 1),
-                lax.dynamic_slice_in_dim(w_key, g * HEAD, HEAD, 1),
-                lax.dynamic_slice_in_dim(w_value, g * HEAD, HEAD, 1),
-            ],
-            axis=1,
-        )
-
-    def own_rows(a):
-        return lax.dynamic_slice_in_dim(a, first_row, share, 0)
-
-    def spread_attn(kept, sent):
-        piece = jnp.stack([kept, swap_col(sent)])
-        mine = lax.all_gather(piece, "row", axis=0)
-        both = in_order(x, mine, swap_x(mine), 2)
-        pairs = both.reshape((2, planes // 2) + both.shape[1:])
-        own = take(pairs, c, 0)
-        other = swap_core(take(pairs, 1 - c, 0))
-        return jnp.stack([own, other], axis=1)
-
-    w_project = spread_attn(own_rows(group_cols(y)), own_rows(group_cols(1 - y)))
-    w_project = w_project.reshape(groups, features, 4 * HEAD)
-
-    def head_rows(g):
-        at = (g * 2 + x) * HEAD
-        return lax.dynamic_slice(w_out, (at, c * quarter), (HEAD, quarter))
-
-    w_mix = spread_attn(head_rows(y), head_rows(1 - y))
-    w_mix = jnp.transpose(w_mix, (0, 3, 4, 1, 2, 5)).reshape(groups * 2 * HEAD, features)
-
-    hidden_width = w_gate.shape[1]
-    unit = hidden_width // 8
-
-    def unit_at(j):
-        return (2 * j + c) * 2 * unit + x * unit
-
-    def by_core(a):
-        parts = a.reshape(unit, 2, quarter)
-        return jnp.where(c == 0, parts, parts[:, ::-1])
-
-    def hidden_pieces(j):
-        at = unit_at(j)
-        gate = lax.dynamic_slice_in_dim(w_gate, at, unit, 1).T
-        upper = lax.dynamic_slice_in_dim(w_up, at, unit, 1).T
-        return jnp.stack([by_core(gate), by_core(upper)]), by_core(
-            lax.dynamic_slice_in_dim(w_down, at, unit, 0)
-        )
-
-    pair_kept, down_kept = hidden_pieces(y)
-    pair_sent, down_sent = hidden_pieces(1 - y)
-    pair_piece = jnp.stack([pair_kept, swap_col(pair_sent)], axis=3).reshape(2 * unit, features)
-    down_piece = jnp.stack([down_kept, swap_col(down_sent)], axis=2).reshape(unit, features)
-    pair_mine = lax.all_gather(pair_piece, "row", axis=0)
-    down_mine = lax.all_gather(down_piece, "row", axis=0)
-    pair_other = swap_x(pair_mine)
-    down_other = swap_x(down_mine)
+    label_col = marks[0][:, None]
+    label_rows = jnp.pad(marks, ((0, 4), (0, 0)))
+
+    hidden_kept = hidden_piece(y)
+    hidden_mine = [
+        four(kept, got[i * unit : (i + 1) * unit]) for i, kept in enumerate(hidden_kept)
+    ]
+    mix_mine = jnp.stack([mix_piece(y), got[3 * unit :, :quarter]])
 
     def gain_order(gain):
         kept = gain.reshape(2, quarter)
@@ -859,86 +925,115 @@
     gain_attn_own = gain_attn_all[:, :quarter]
     gain_ffn_own = lax.dynamic_slice_in_dim(gain_ffn, c * quarter, quarter, 0)[None, :]
 
+    (
+        project_all, block_in, mix_mine, gate_piece, up_piece, down_piece,
+        cosine, sine, label_col, label_rows, gain_attn_all,
+    ) = lax.optimization_barrier(
+        (
+            project_all, block_in, mix_mine, *hidden_mine,
+            cosine, sine, label_col, label_rows, gain_attn_all,
+        )
+    )
+
     pieces = spread(block_in)
+    mix_all = lax.all_gather(mix_mine, "row", axis=0)
+    gate_mine = lax.all_gather(gate_piece, "row", axis=0, tiled=True)
+    up_mine = lax.all_gather(after(up_piece, mix_all), "row", axis=0, tiled=True)
+    down_mine = lax.all_gather(after(down_piece, gate_mine), "row", axis=0, tiled=True)
+    gate_far, up_far, down_far = (swap_x(u) for u in (gate_mine, up_mine, down_mine))
+
+    def of_core_pairs(mine, other):
+        both = in_order(x, mine, other, 2)
+        pairs = both.reshape((2, planes // 2) + both.shape[1:])
+        return take(pairs, c, 0), swap_core(take(pairs, 1 - c, 0))
+
+    near, far = of_core_pairs(project_all, swap_x(project_all))
+    w_near = near.reshape(groups, half, 4 * HEAD)
+    w_far = far.reshape(groups, half, 4 * HEAD)
+
     normed_attn, qkv, ratio_attn = rows_call(
         project_kernel,
         block,
         [*pieces, cosine, sine],
-        [gain_attn_all, w_project],
+        [gain_attn_all, w_near, w_far],
         [(features, jnp.bfloat16), (groups * 4 * HEAD, jnp.bfloat16), (1, jnp.float32)],
         2 * rows * features * groups * 4 * HEAD,
         "project",
     )
-    attn, lse = attend(qkv, label_col, label_rows, trunk, leaf_begin, block)
-    own, send = rows_call(
-        out_kernel,
+    near, far = of_core_pairs(mix_all, after(swap_x(mix_all), qkv))
+    attn, lse = attend(after(qkv, near), label_col, label_rows, TRUNK, LEAF_BEGIN, block)
+    mix_shape = (groups, 2, 2 * HEAD, quarter)
+    m_near, m_far = near.reshape(mix_shape), after(far, attn).reshape(mix_shape)
+    parts = rows_call(
+        mix_kernel,
         2 * block,
         [attn],
-        [w_mix],
-        [(half, jnp.bfloat16), (half, jnp.bfloat16)],
+        [m_near, m_far],
+        [(quarter, jnp.bfloat16)] * 4,
         2 * rows * features * groups * 2 * HEAD,
         "mix",
     )
-    middle = wide(block_in) + collect(own, send)
+    cotangent = lax.all_to_all(to_trees(out_grad), "row", 0, 0, tiled=True)
+    parts[1] = after(parts[1], cotangent)
+    own, got, outgoing = collect_core(parts)
+    middle = wide(block_in) + collect_col(own, got, outgoing)
     square = small_sum(jnp.sum(middle * middle, axis=1))
     ratio_ffn = lax.rsqrt(square / features + EPSILON)[:, None]
     normed_ffn = middle * ratio_ffn
-    ffn_pieces = spread(low(normed_ffn * gain_ffn_own))
-
-    cotangent = to_tree(out_grad)
-    grad_pieces = spread(cotangent)
-    hid_mine, hid_other, pair_grad_mine, pair_grad_other = rows_call(
+    ffn_pieces = spread(after(low(normed_ffn * gain_ffn_own), up_mine, gate_far))
+    grad_near, grad_across = cotangent, swap_col(after(cotangent, ffn_pieces[1]))
+    gate_m, up_m, gate_o, up_o = rows_call(
+        gate_up_kernel,
+        block,
+        ffn_pieces,
+        [gate_mine, up_mine, gate_far, up_far],
+        [(planes * unit, jnp.bfloat16)] * 4,
+        2 * rows * features * 4 * planes * unit,
+        "gate_up",
+        [pltpu.VMEM((block, features), jnp.bfloat16)],
+    )
+    grad_pieces = [
+        grad_near,
+        grad_across,
+        swap_core(after(grad_near, ffn_pieces[3])),
+        swap_core(after(grad_across, gate_m)),
+    ]
+    dgate_m, dup_m, hid_m, dgate_o, dup_o, hid_o = rows_call(
         hidden_kernel,
         block,
-        [*ffn_pieces, *grad_pieces],
-        [pair_mine, pair_other, down_mine, down_other],
-        [
-            (planes * unit, jnp.bfloat16),
-            (planes * unit, jnp.bfloat16),
-            (2 * planes * unit, jnp.bfloat16),
-            (2 * planes * unit, jnp.bfloat16),
-        ],
-        2 * rows * features * 6 * planes * unit,
+        [*grad_pieces, gate_m, gate_o, up_m, up_o],
+        [down_mine, down_far],
+        [(planes * unit, jnp.bfloat16)] * 6,
+        2 * rows * features * 2 * planes * unit,
         "hidden",
-        [pltpu.VMEM((block, features), jnp.bfloat16)] * 2,
-    )
-    down_mine = down_mine.reshape(planes * unit, features)
-    down_other = down_other.reshape(planes * unit, features)
-    pair_mine = pair_mine.reshape(2 * planes * unit, features)
-    pair_other = pair_other.reshape(2 * planes * unit, features)
-
-    own, send = rows_call(
-        two_out_kernel,
+        [pltpu.VMEM((block, features), jnp.bfloat16)],
+    )
+
+    def unit_grad(a, pieces_of, name, before):
+        return weight_grad(after(a, before), pieces_of, 2 * block, name)
+
+    def to_row(total):
+        return lax.psum_scatter(total, "row", scatter_dimension=0, tiled=True)
+
+    down_other = weight_grad(hid_o, grad_pieces, 2 * block, "down_grad_other")
+    parts = rows_call(
+        functools.partial(sum_out_kernel, 4),
         2 * block,
-        [pair_grad_mine, pair_grad_other],
-        [pair_mine, pair_other],
-        [(half, jnp.bfloat16), (half, jnp.bfloat16)],
+        [after(dgate_m, down_other), dup_m, dgate_o, dup_o],
+        [gate_mine, up_mine, gate_far, up_far],
+        [(quarter, jnp.bfloat16)] * 4,
         2 * rows * features * 4 * planes * unit,
         "pair_back",
     )
-    normed_ffn_grad = collect(own, send)
-
-    def to_z(grad_mine, grad_other):
-        total = low(wide(grad_mine) + wide(swap_x(grad_other)))
-        return lax.psum_scatter(total, "row", scatter_dimension=0, tiled=True)
-
-    down_grad_other = weight_grad(hid_other, grad_pieces, True, 2 * block, "down_grad_other")[0]
-    down_grad_mine = weight_grad(hid_mine, grad_pieces, True, 2 * block, "down_grad_mine")[0]
-    down_sum = to_z(down_grad_mine, down_grad_other)
-    pair_w_other = weight_grad(pair_grad_other, ffn_pieces, True, 2 * block, "pair_grad_other")[0]
-    pair_w_mine = weight_grad(pair_grad_mine, ffn_pieces, True, 2 * block, "pair_grad_mine")[0]
-    pair_sum = to_z(pair_w_mine, pair_w_other)
-
-    own, send = rows_call(
-        two_out_kernel,
-        2 * block,
-        [hid_mine, hid_other],
-        [down_mine, down_other],
-        [(half, jnp.bfloat16), (half, jnp.bfloat16)],
-        2 * rows * features * 2 * planes * unit,
-        "down",
-    )
-    output = from_tree(low(middle + collect(own, send)))
+    gate_other = unit_grad(dgate_o, ffn_pieces, "gate_grad_other", parts[0])
+    down_own = unit_grad(hid_m, grad_pieces, "down_grad_mine", gate_other)
+    parts[1] = after(parts[1], down_own)
+    own, got, outgoing = collect_core(parts)
+    down_total = low(wide(after(down_own, outgoing)) + wide(swap_x(down_other)))
+    down_sum = to_row(down_total)
+    up_other = unit_grad(dup_o, ffn_pieces, "up_grad_other", down_total)
+    gate_own = unit_grad(dgate_m, ffn_pieces, "gate_grad_mine", up_other)
+    normed_ffn_grad = collect_col(after(own, gate_own), got, outgoing)
 
     def norm_back(grad, ratio, normed, gain):
         scaled = grad * gain
@@ -947,81 +1042,126 @@
 
     middle_back, gain_ffn_part = norm_back(normed_ffn_grad, ratio_ffn, normed_ffn, gain_ffn_own)
     middle_grad = wide(cotangent) + middle_back
-    middle_pieces = spread(low(middle_grad))
+    middle_low = low(middle_grad)
+    middle_pieces = spread(middle_low)
+    up_own = unit_grad(dup_m, ffn_pieces, "up_grad_mine", middle_low)
+    gate_total = low(wide(after(gate_own, up_own)) + wide(swap_x(gate_other)))
+    gate_sum = to_row(gate_total)
+    where = jnp.stack([y, x, c]).astype(jnp.int32)
+
+    def unit_halves(total):
+        kept = jnp.concatenate([total[:, :quarter], total[:, half : half + quarter]], axis=1)
+        sent = jnp.concatenate([total[:, quarter:half], total[:, half + quarter :]], axis=1)
+        return kept, sent
+
+    def unit_parts(kept, sent):
+        both = jnp.stack([kept, swap_col(sent)])
+        over = swap_x(both)
+        return [both, swap_core(both), over, swap_core(over)]
+
+    out_parts = rows_call(
+        functools.partial(sum_out_kernel, 2),
+        2 * block,
+        [after(hid_m, gate_total), hid_o],
+        [down_mine, down_far],
+        [(quarter, jnp.bfloat16)] * 4,
+        2 * rows * features * 2 * planes * unit,
+        "down",
+    )
     attn_grad = rows_call(
         attn_grad_kernel,
         2 * block,
-        middle_pieces,
-        [w_mix],
+        [after(middle_pieces[0], out_parts[0]), *middle_pieces[1:]],
+        [m_near, m_far],
         [(groups * 2 * HEAD, jnp.bfloat16)],
         2 * rows * features * groups * 2 * HEAD,
         "attn_grad",
     )[0]
-    mix_grad = weight_grad(attn, middle_pieces, True, groups * 2 * HEAD, "mix_grad")[0]
+    out_parts[1] = after(out_parts[1], attn_grad)
+    out_own, out_got, out_outgoing = collect_core(out_parts)
     qkv_grad = attend_back(
-        qkv, attn, attn_grad, label_col, label_rows, lse, cosine, sine, trunk, leaf_begin, block
-    )
-    own, send = rows_call(
+        qkv, attn, after(attn_grad, out_outgoing), label_col, label_rows, lse, cosine, sine,
+        TRUNK, LEAF_BEGIN, block,
+    )
+    output = low(after(middle, qkv_grad) + collect_col(out_own, out_got, out_outgoing))
+    up_total = low(wide(after(up_own, output)) + wide(swap_x(up_other)))
+    up_sum = to_row(up_total)
+    parts = rows_call(
         project_back_kernel,
         2 * block,
-        [qkv_grad],
-        [w_project],
-        [(half, jnp.bfloat16), (half, jnp.bfloat16)],
+        [after(qkv_grad, up_total)],
+        [w_near, w_far],
+        [(quarter, jnp.bfloat16)] * 4,
         2 * rows * features * groups * 4 * HEAD,
         "project_back",
     )
-    normed_attn_grad = collect(own, send)
-    project_grad = weight_grad(normed_attn, [qkv_grad], True, 2 * block, "project_grad")[0]
+    output_tree = lax.all_to_all(output, "row", 0, 0, tiled=True)
+    home_kept, home_sent = unit_halves(
+        jnp.concatenate([after(down_sum, parts[0]), gate_sum])
+    )
+    project_grad = weight_grad(
+        normed_attn, [after(qkv_grad, home_sent)], 2 * block, "project_grad", split=groups
+    )
+    parts[1] = after(parts[1], project_grad)
+    own, got, outgoing = collect_core(parts)
+    mix_grads = weight_grad(
+        attn,
+        [after(middle_pieces[0], outgoing), *middle_pieces[1:]],
+        groups * 2 * HEAD,
+        "mix_grad",
+        joined=False,
+    )
+
+    project_parts = project_grad.reshape(groups, 2, 2, 2, share, 4 * HEAD)
+    mix_parts = jnp.stack([m.reshape(groups, 2, HEAD, quarter) for m in mix_grads], axis=1)
+    mix_parts = mix_parts.reshape(groups, 2, 2, 2, HEAD, quarter)
+
+    def of_x(index):
+        return jnp.concatenate([take(project_parts, index, 3), take(mix_parts, index, 3)], axis=3)
+
+    attn_sent = of_x(1 - x)
+    attn_kept = of_x(after(x, attn_sent))
+    home_parts = unit_parts(home_kept, home_sent)
+    home_parts[0] = after(home_parts[0], attn_kept)
+    down_out = ffn_home(where, home_parts, 0, unit, False, "down_home")
+    gate_out = ffn_home(where, home_parts, 1, unit, True, "gate_home")
+    normed_attn_grad = collect_col(after(own, down_out, gate_out), got, outgoing)
     normed_attn_own = wide(block_in) * ratio_attn
     input_back, gain_attn_part = norm_back(
         normed_attn_grad, ratio_attn, normed_attn_own, gain_attn_own
     )
-    input_grad = from_tree(low(middle_grad + input_back))
-
-    def ffn_home(total):
-        parts = total.reshape(-1, unit, 2, 2, quarter)
-        cols = in_order(y, parts[:, :, :, 0], swap_col(parts[:, :, :, 1]))
-        both = in_order(x, cols, swap_x(cols))
-        both = jnp.where(c == 0, both, both[:, :, :, :, ::-1])
-        whole = in_order(c, both, swap_core(both))
-        whole = jnp.transpose(whole, (3, 2, 0, 1, 4, 5, 6))
-        return wide(whole.reshape(-1, 8 * unit, half))
-
-    down_out = ffn_home(down_sum)[0]
-    pair_out = ffn_home(pair_sum)
-    gate_out = pair_out[0].T
-    up_out = pair_out[1].T
-
-    def attn_home(parts):
-        kept = take(parts, x, 3)
-        total = low(wide(kept) + wide(swap_x(take(parts, 1 - x, 3))))
-        mine = total[:, 0]
-        other = swap_core(total[:, 1])
-        planes_all = in_order(c, mine, other).reshape((planes,) + mine.shape[1:])
-        summed = lax.psum_scatter(planes_all, "row", scatter_dimension=0, tiled=False)
-        cols = in_order(y, summed[0], swap_col(summed[1]))
-        both = in_order(x, cols, swap_x(cols))
-        return in_order(c, both, swap_core(both))
-
-    mix_parts = mix_grad.reshape(groups, 2, HEAD, 2, 2, quarter)
-    mix_home = attn_home(jnp.transpose(mix_parts, (0, 3, 4, 1, 2, 5)))
+    input_low = low(middle_grad + input_back)
+    input_tree = lax.all_to_all(input_low, "row", 0, 0, tiled=True)
+    up_kept, up_sent = unit_halves(after(up_sum, input_low))
+    attn_total = low(wide(after(attn_kept, up_sent)) + wide(swap_x(attn_sent)))
+    by_plane = in_order(c, attn_total[:, 0], swap_core(attn_total[:, 1]))
+    by_plane = by_plane.reshape((planes,) + by_plane.shape[2:])
+    attn_sum = lax.psum_scatter(by_plane, "row", scatter_dimension=0, tiled=False)
+    output, output_sent = of_core(after(output_tree, by_plane))
+    output = by_feature(output, output_sent)
+    up_parts = unit_parts(up_kept, up_sent)
+    up_parts[0] = after(up_parts[0], output)
+    up_out = ffn_home(where, up_parts, 0, unit, True, "up_home")
+    input_grad = by_feature(*of_core(after(input_tree, up_out)))
+
+    home = in_order(y, attn_sum[0], swap_col(attn_sum[1]))
+    home = in_order(x, home, swap_x(home))
+    home = in_order(c, home, swap_core(home))
+    mix_home = home[:, :, :, share:]
     out_out = wide(jnp.transpose(mix_home, (2, 1, 3, 0, 4)).reshape(groups * 2 * HEAD, half))
-    project_parts = project_grad.reshape(2, 2, 2, share, groups, 4 * HEAD)
-    project_home = attn_home(jnp.transpose(project_parts, (4, 0, 1, 2, 3, 5)))
-    project_home = jnp.transpose(project_home, (0, 1, 3, 2, 4)).reshape(half, groups, 4 * HEAD)
+    project_home = jnp.transpose(home[:, :, :, :share], (0, 1, 3, 2, 4))
+    project_home = project_home.reshape(half, groups, 4 * HEAD)
     query_out = wide(project_home[:, :, : 2 * HEAD].reshape(half, groups * 2 * HEAD))
     key_out = wide(project_home[:, :, 2 * HEAD : 3 * HEAD].reshape(half, groups * HEAD))
     value_out = wide(project_home[:, :, 3 * HEAD :].reshape(half, groups * HEAD))
 
-    def gain_home(part):
-        filled = lax.dynamic_update_slice(
-            jnp.zeros((half,), jnp.float32), part, (c * quarter,)
-        )
-        return filled
-
-    gain_attn_out, gain_ffn_out = lax.psum(
-        (gain_home(gain_attn_part), gain_home(gain_ffn_part)), ("dp", "row")
-    )
+    gains = jnp.stack([gain_attn_part, gain_ffn_part])
+    gains = gains + shift(gains, ROW_SECOND)
+    gains = gains + shift(gains, ROW_SWAP)
+    gains = gains + swap_x(gains)
+    gains = in_order(c, gains, swap_core(gains), 1)
+    gain_attn_out = gains[0].reshape(half)
+    gain_ffn_out = gains[1].reshape(half)
     return (
         output,
         input_grad,

time: 1590 us -> 1420 us (0.89)
  local copies, waits for them, and re-layouts: 222 us -> 57.3 us
  waiting for transfers between devices: 646 us -> 564 us
  blocking collectives: 34.7 us -> 111 us
  other arithmetic: 177 us -> 128 us
  Pallas kernels: 428 us -> 472 us
    all_to_all x0 -> x1, blocking collectives: none -> 111 us  [tree_body(): output_tree = lax.all_to_all(output, 'row', 0, 0, tiled=True)]
    unnamed x121 -> x98, local copies, waits for them, and re-layouts: 72.7 us -> 18.2 us
    all_gather x4 -> x5, waiting for transfers between devices: 89.9 us -> 48.9 us  [the longest x1 48.8 us: tree_body(): project_all = lax.all_gather(project_mine, 'row', axis=0)]
    slice x7 -> x11, local copies, waits for them, and re-layouts: 45.9 us -> 6.88 us  [the longest x2 2.27 us: unit_halves(): total[:, :quarter]]
    pallas_call x6 -> x11, Pallas kernels: 121 us -> 157 us  [the longest x8 133 us: weight_grad(): pl.pallas_call(functools.partial(weight_grad_kernel, len(bs), split), gri...]
    psum x1 -> x0, blocking collectives: 34.7 us -> none  [tree_body(): lax.psum((gain_home(gain_attn_part), gain_home(gain_ffn_part)), ('dp', 'r...]
    another operation x38 -> x17, other arithmetic: 41.7 us -> 17.1 us  [in_order(): return jnp.stack([first, second], axis=axis)]
    ppermute x20 -> x17, waiting for transfers between devices: 305 us -> 282 us  [swap_col(): return lax.ppermute(a, 'col', COL_SWAP)]
  transfers between devices with their start and end apart: 73 -> 80, of which waited for: 28 -> 35; matrix products, arithmetic and copies ran while one was open for 19% -> 11% of each run, Pallas kernels for 19% -> 30%
where the time goes in v2:
time: 1420 us; the launch traced here: 1410 us
  waiting for transfers between devices  564 us (40%)
  Pallas kernels  472 us (33%)
  other arithmetic  128 us (9%)
  blocking collectives  111 us (8%)
  starting transfers between devices  59.1 us (4%)
  local copies, waits for them, and re-layouts  57.3 us (4%)
  between operations  15.1 us (1%)
    ppermute x17, waiting for transfers between devices, swap_col(): return lax.ppermute(a, 'col', COL_SWAP)  282 us
    pallas_call x8, Pallas kernels, rows_call(): pl.pallas_call(fn, grid=(rows // block,), in_specs=in_specs, out_specs=[p...  226 us
    ppermute x13, waiting for transfers between devices, swap_x(): return lax.ppermute(a, 'dp', X_SWAP)  175 us
    pallas_call x8, Pallas kernels, weight_grad(): pl.pallas_call(functools.partial(weight_grad_kernel, len(bs), split), gri...  133 us
    all_to_all x1, blocking collectives, tree_body(): output_tree = lax.all_to_all(output, 'row', 0, 0, tiled=True)  111 us
    convert_element_type x12, other arithmetic, low(): return a.astype(jnp.bfloat16)  57.5 us
    pallas_call x1, Pallas kernels, attend_back(): pl.pallas_call(functools.partial(attend_back_kernel, trunk, leaf_begin, b...  55.6 us
    all_gather x1, waiting for transfers between devices, tree_body(): project_all = lax.all_gather(project_mine, 'row', axis=0)  48.8 us
  transfers between devices with their start and end apart: 80, of which 35 were waited for; matrix products, arithmetic and copies ran while one was open for 11% of the time, Pallas kernels for 30%

profile of v2, /device:TPU:0, one launch (start us, length us, event | category | flops | bytes accessed | tf_op | source)
XLA Modules:
  0.0 1407.5 jit_solution(13836127598761957691)
XLA Ops:
  53.3 17.3 %collective-permute-done.2 = bf16[896,1024]{1,0:T(8,128)(2,1)} collective-permute-done((bf16[896,1024]{1,0:T(8,128)(2,1)}, bf16[896,1024]{1,0:T(8,128)(2,1)}, u32[]{:S(2)}, u32[]{:S(2)}) %collective-permute-start.2) | collective-permute-done | bytes 1835040 | tf_op jit(solution)/shard_map/ppermute | solution.py:332
  77.1 48.8 %all-gather.14.cloned.1.call-done = bf16[8,256,512]{2,1,0:T(8,128)(2,1)} async-done(((bf16[2,256,512]{2,1,0:T(8,128)(2,1)}), bf16[8,256,512]{2,1,0:T(8,128)(2,1)}) %all-gather.14.cloned.1.call-update) | async-done | bytes 2097168 | tf_op jit(solution)/shard_map/all_gather | solution.py:900
  139.7 56.0 %collective-permute-done.5.x1 = bf16[2560,512]{1,0:T(8,128)(2,1)} collective-permute-done((bf16[2560,512]{1,0:T(8,128)(2,1)}, bf16[2560,512]{1,0:T(8,128)(2,1)}, u32[]{:S(2)}, u32[]{:S(2)}) %collective-permute-start.5) | collective-permute-done | bytes 2621472 | tf_op jit(solution)/shard_map/ppermute | solution.py:332
  213.8 20.3 %project.1 = (bf16[2560,2048]{1,0:T(8,128)(2,1)}, bf16[2560,1024]{1,0:T(8,128)(2,1)}, f32[2560,1]{1,0:T(8,128)}) custom-call(bf16[2560,512]{1,0:T(8,128)(2,1)} %bitcast.6.x0, bf16[2560,512]{1,0:T(8,128)(2,1)} %collective-permute-done.5.x1, bf16[2560,512]{1,0:T(8,128)(2,1)} %collective-permute-done.6.x2, bf16[2560,512]{1,0:T(8,128)(2,1)} %collective-permute-done.7.x3, ...), custom_call_target="tpu_custom_call" | custom-call | flops 1342177280 | bytes 4131072 | tf_op jit(solution)/shard_map/project/pallas_call | solution.py:372
  239.5 34.4 %attend.1 = (bf16[2560,512]{1,0:T(8,128)(2,1)}, f32[2,10,1,512]{3,2,1,0:T(1,128)}) custom-call(bf16[2560,1024]{1,0:T(8,128)(2,1)} %get-tuple-element.102.q_ref.k_ref.v_ref, bf16[2560,1024]{1,0:T(8,128)(2,1)} %get-tuple-element.102.q_ref.k_ref.v_ref, bf16[2560,1024]{1,0:T(8,128)(2,1)} %get-tuple-element.102.q_ref.k_ref.v_ref, s32[2560,1]{1,0:T(8,128)} %copy.74.lab_ref, ...), custom_call_target="tpu_custom_call" | custom-call | flops 3355443200 | bytes 1638400 | tf_op jit(solution)/shard_map/attend/pallas_call | solution.py:585
  283.0 20.5 %all-to-all-done.1 = bf16[4,640,512]{2,1,0:T(8,128)(2,1)S(1)} async-done(((bf16[4,640,512]{2,1,0:T(8,128)(2,1)}), bf16[4,640,512]{2,1,0:T(8,128)(2,1)S(1)}, u32[]{:S(2)}, u32[]{:S(2)}) %all-to-all-start.1) | async-done | bytes 2621472 | tf_op jit(solution)/shard_map/all_to_all | solution.py:976
  312.2 55.9 %collective-permute-done.15 = bf16[2560,512]{1,0:T(8,128)(2,1)} collective-permute-done((bf16[2560,512]{1,0:T(8,128)(2,1)}, bf16[2560,512]{1,0:T(8,128)(2,1)}, u32[]{:S(2)}, u32[]{:S(2)}) %collective-permute-start.15) | collective-permute-done | bytes 2621472 | tf_op jit(solution)/shard_map/ppermute | solution.py:332
  378.2 24.6 %collective-permute-done.19.refs_6_ = bf16[1024,2048]{1,0:T(8,128)(2,1)} collective-permute-done((bf16[1024,2048]{1,0:T(8,128)(2,1)}, bf16[1024,2048]{1,0:T(8,128)(2,1)}, u32[]{:S(2)}, u32[]{:S(2)}) %collective-permute-start.19) | collective-permute-done | bytes 4194336 | tf_op jit(solution)/shard_map/ppermute | solution.py:328
  405.0 55.2 %collective-permute-done.20.refs_1_.refs_2_ = bf16[2560,512]{1,0:T(8,128)(2,1)} collective-permute-done((bf16[2560,512]{1,0:T(8,128)(2,1)S(1)}, bf16[2560,512]{1,0:T(8,128)(2,1)}, u32[]{:S(2)}, u32[]{:S(2)}) %collective-permute-start.20) | collective-permute-done | bytes 2621472 | tf_op jit(solution)/shard_map/ppermute | solution.py:332
  469.3 28.1 %collective-permute-done.25.refs_7_ = bf16[1024,2048]{1,0:T(8,128)(2,1)} collective-permute-done((bf16[1024,2048]{1,0:T(8,128)(2,1)}, bf16[1024,2048]{1,0:T(8,128)(2,1)}, u32[]{:S(2)}, u32[]{:S(2)}) %collective-permute-start.25) | collective-permute-done | bytes 4194336 | tf_op jit(solution)/shard_map/ppermute | solution.py:328
  497.3 53.1 %gate_up.1 = (bf16[2560,1024]{1,0:T(8,128)(2,1)}, bf16[2560,1024]{1,0:T(8,128)(2,1)}, bf16[2560,1024]{1,0:T(8,128)(2,1)}, bf16[2560,1024]{1,0:T(8,128)(2,1)}) custom-call(bf16[2560,512]{1,0:T(8,128)(2,1)} %copy-done.1, bf16[2560,512]{1,0:T(8,128)(2,1)} %collective-permute-done.20.refs_1_.refs_2_, bf16[2560,512]{1,0:T(8,128)(2,1)} %collective-permute-done.24.refs_2_.refs_3_, ...), custom_call_target="tpu_custom_call" | custom-call | flops 5368709120 | bytes 6029312 | tf_op jit(solution)/shard_map/gate_up/pallas_call | solution.py:372
  550.6 33.9 %collective-permute-done.27.refs_9_.refs_3_ = bf16[1024,2048]{1,0:T(8,128)(2,1)} collective-permute-done((bf16[1024,2048]{1,0:T(8,128)(2,1)}, bf16[1024,2048]{1,0:T(8,128)(2,1)}, u32[]{:S(2)}, u32[]{:S(2)}) %collective-permute-start.27) | collective-permute-done | bytes 4194336 | tf_op jit(solution)/shard_map/ppermute | solution.py:328
  586.9 36.9 %hidden.1 = (bf16[2560,1024]{1,0:T(8,128)(2,1)}, bf16[2560,1024]{1,0:T(8,128)(2,1)}, bf16[2560,1024]{1,0:T(8,128)(2,1)}, bf16[2560,1024]{1,0:T(8,128)(2,1)}, bf1...) custom-call(bf16[2560,512]{1,0:T(8,128)(2,1)} %bitcast.188, ...), custom_call_target="tpu_custom_call" | custom-call | flops 2684354560 | bytes 8912896 | tf_op jit(solution)/shard_map/hidden/pallas_call | solution.py:372
  623.8 17.4 %down_grad_other.1 = bf16[1024,2048]{1,0:T(8,128)(2,1)} custom-call(bf16[2560,1024]{1,0:T(8,128)(2,1)} %get-tuple-element.128.refs_0_.refs_1_, bf16[2560,512]{1,0:T(8,128)(2,1)} %bitcast.189, bf16[2560,512]{1,0:T(8,128)(2,1)} %collective-permute-done.21.refs_1_.refs_2_, bf16[2560,512]{1,0:T(8,128)(2,1)} %copy-done.4, bf16[2560,512]{1,0:T(8,128)(2,1)} %copy-done.5), custom_call_target="tpu_custom_call" | custom-call | flops 1342177280 | bytes 2490368 | tf_op jit(solution)/shard_map/down_grad_other/pallas_call | solution.py:779
  642.7 52.7 %pair_back.1 = (bf16[2560,512]{1,0:T(8,128)(2,1)}, bf16[2560,512]{1,0:T(8,128)(2,1)}, bf16[2560,512]{1,0:T(8,128)(2,1)}, bf16[2560,512]{1,0:T(8,128)(2,1)}) custom-call(bf16[2560,1024]{1,0:T(8,128)(2,1)} %get-tuple-element.142.refs_0_, bf16[2560,1024]{1,0:T(8,128)(2,1)} %get-tuple-element.145.refs_1_.refs_0_, ...), custom_call_target="tpu_custom_call" | custom-call | flops 5368709120 | bytes 6029312 | tf_op jit(solution)/shard_map/pair_back/pallas_call | solution.py:372
  695.5 17.3 %gate_grad_other.1 = bf16[1024,2048]{1,0:T(8,128)(2,1)} custom-call(bf16[2560,1024]{1,0:T(8,128)(2,1)} %get-tuple-element.135.refs_2_.refs_0_, bf16[2560,512]{1,0:T(8,128)(2,1)} %copy-done.1, bf16[2560,512]{1,0:T(8,128)(2,1)} %collective-permute-done.20.refs_1_.refs_2_, bf16[2560,512]{1,0:T(8,128)(2,1)} %collective-permute-done.24.refs_2_.refs_3_, ...), custom_call_target="tpu_custom_call" | custom-call | flops 1342177280 | bytes 2490368 | tf_op jit(solution)/shard_map/gate_grad_other/pallas_call | solution.py:779
  712.8 17.7 %down_grad_mine.1 = bf16[1024,2048]{1,0:T(8,128)(2,1)} custom-call(bf16[2560,1024]{1,0:T(8,128)(2,1)} %get-tuple-element.147.refs_0_, bf16[2560,512]{1,0:T(8,128)(2,1)} %bitcast.190, bf16[2560,512]{1,0:T(8,128)(2,1)} %collective-permute-done.21.refs_1_.refs_2_, bf16[2560,512]{1,0:T(8,128)(2,1)} %copy-done.4, bf16[2560,512]{1,0:T(8,128)(2,1)} %copy-done.5), custom_call_target="tpu_custom_call" | custom-call | flops 1342177280 | bytes 2490368 | tf_op jit(solution)/shard_map/down_grad_mine/pallas_call | solution.py:779
  741.8 18.3 %up_grad_other.1 = bf16[1024,2048]{1,0:T(8,128)(2,1)} custom-call(bf16[2560,1024]{1,0:T(8,128)(2,1)} %get-tuple-element.141.refs_3_.refs_0_, bf16[2560,512]{1,0:T(8,128)(2,1)} %copy-done.1, bf16[2560,512]{1,0:T(8,128)(2,1)} %collective-permute-done.20.refs_1_.refs_2_, bf16[2560,512]{1,0:T(8,128)(2,1)} %collective-permute-done.24.refs_2_.refs_3_, ...), custom_call_target="tpu_custom_call" | custom-call | flops 1342177280 | bytes 2490368 | tf_op jit(solution)/shard_map/up_grad_other/pallas_call | solution.py:779
  760.1 17.5 %gate_grad_mine.1 = bf16[1024,2048]{1,0:T(8,128)(2,1)} custom-call(bf16[2560,1024]{1,0:T(8,128)(2,1)} %get-tuple-element.142.refs_0_, bf16[2560,512]{1,0:T(8,128)(2,1)} %copy-done.1, bf16[2560,512]{1,0:T(8,128)(2,1)} %collective-permute-done.20.refs_1_.refs_2_, bf16[2560,512]{1,0:T(8,128)(2,1)} %collective-permute-done.24.refs_2_.refs_3_, ...), custom_call_target="tpu_custom_call" | custom-call | flops 1342177280 | bytes 2490368 | tf_op jit(solution)/shard_map/gate_grad_mine/pallas_call | solution.py:779
  777.6 21.5 %collective-permute-done.31 = bf16[2560,512]{1,0:T(8,128)(2,1)} collective-permute-done((bf16[2560,512]{1,0:T(8,128)(2,1)}, bf16[2560,512]{1,0:T(8,128)(2,1)}, u32[]{:S(2)}, u32[]{:S(2)}) %collective-permute-start.31) | collective-permute-done | bytes 2621472 | tf_op jit(solution)/shard_map/ppermute | solution.py:332
  815.2 17.7 %up_grad_mine.1 = bf16[1024,2048]{1,0:T(8,128)(2,1)} custom-call(bf16[2560,1024]{1,0:T(8,128)(2,1)} %get-tuple-element.145.refs_1_.refs_0_, bf16[2560,512]{1,0:T(8,128)(2,1)} %copy-done.1, bf16[2560,512]{1,0:T(8,128)(2,1)} %collective-permute-done.20.refs_1_.refs_2_, bf16[2560,512]{1,0:T(8,128)(2,1)} %collective-permute-done.24.refs_2_.refs_3_, ...), custom_call_target="tpu_custom_call" | custom-call | flops 1342177280 | bytes 2490368 | tf_op jit(solution)/shard_map/up_grad_mine/pallas_call | solution.py:779
  840.4 33.2 %collective-permute-done.36.h1.refs_2_ = bf16[2560,512]{1,0:T(8,128)(2,1)} collective-permute-done((bf16[2560,512]{1,0:T(8,128)(2,1)}, bf16[2560,512]{1,0:T(8,128)(2,1)}, u32[]{:S(2)}, u32[]{:S(2)}) %collective-permute-start.36) | collective-permute-done | bytes 2621472 | tf_op jit(solution)/shard_map/ppermute | solution.py:332
  873.6 27.5 %down.1 = (bf16[2560,512]{1,0:T(8,128)(2,1)}, bf16[2560,512]{1,0:T(8,128)(2,1)}, bf16[2560,512]{1,0:T(8,128)(2,1)}, bf16[2560,512]{1,0:T(8,128)(2,1)}) custom-call(bf16[2560,1024]{1,0:T(8,128)(2,1)} %get-tuple-element.147.refs_0_, bf16[2560,1024]{1,0:T(8,128)(2,1)} %get-tuple-element.128.refs_0_.refs_1_, ...), custom_call_target="tpu_custom_call" | custom-call | flops 2684354560 | bytes 3670016 | tf_op jit(solution)/shard_map/down/pallas_call | solution.py:372
  921.3 55.6 %attend_back.1.d_ref.refs_1_ = bf16[2560,1024]{1,0:T(8,128)(2,1)} custom-call(bf16[2560,1024]{1,0:T(8,128)(2,1)} %get-tuple-element.102.q_ref.k_ref.v_ref, bf16[2560,1024]{1,0:T(8,128)(2,1)} %get-tuple-element.102.q_ref.k_ref.v_ref, bf16[2560,1024]{1,0:T(8,128)(2,1)} %get-tuple-element.102.q_ref.k_ref.v_ref, ...), custom_call_target="tpu_custom_call" | custom-call | flops 8388608000 | bytes 3276800 | tf_op jit(solution)/shard_map/attend_back/pallas_call | solution.py:608
  1000.6 15.8 %project_back.1 = (bf16[2560,512]{1,0:T(8,128)(2,1)}, bf16[2560,512]{1,0:T(8,128)(2,1)}, bf16[2560,512]{1,0:T(8,128)(2,1)}, bf16[2560,512]{1,0:T(8,128)(2,1)}) custom-call(bf16[2560,1024]{1,0:T(8,128)(2,1)} %attend_back.1.d_ref.refs_1_, bf16[2,1024,512]{2,1,0:T(8,128)(2,1)} %bitcast.194, bf16[2,1024,512]{2,1,0:T(8,128)(2,1)} %bitcast.25.far_ref), custom_call_target="tpu_custom_call" | custom-call | flops 1342177280 | bytes 2490368 | tf_op jit(solution)/shard_map/project_back/pallas_call | solution.py:372
  1020.5 24.6 %collective-permute-done.44 = bf16[512,1024]{1,0:T(8,128)(2,1)S(1)} collective-permute-done((bf16[512,1024]{1,0:T(8,128)(2,1)S(1)}, bf16[512,1024]{1,0:T(8,128)(2,1)S(1)}, u32[]{:S(2)}, u32[]{:S(2)}) %collective-permute-start.44) | collective-permute-done | bytes 1048608 | tf_op jit(solution)/shard_map/ppermute | solution.py:332
  1045.9 16.1 %project_grad.1 = bf16[2,2048,512]{2,1,0:T(8,128)(2,1)} custom-call(bf16[2560,2048]{1,0:T(8,128)(2,1)} %get-tuple-element.157.refs_0_, bf16[2560,1024]{1,0:T(8,128)(2,1)} %attend_back.1.d_ref.refs_1_), custom_call_target="tpu_custom_call" | custom-call | flops 1342177280 | bytes 2490368 | tf_op jit(solution)/shard_map/project_grad/pallas_call | solution.py:779
  1067.0 25.9 %collective-permute-done.46.refs_2_ = bf16[2,512,1024]{2,1,0:T(8,128)(2,1)} collective-permute-done((bf16[2,512,1024]{2,1,0:T(8,128)(2,1)S(1)}, bf16[2,512,1024]{2,1,0:T(8,128)(2,1)}, u32[]{:S(2)}, u32[]{:S(2)}) %collective-permute-start.46) | collective-permute-done | bytes 2097184 | tf_op jit(solution)/shard_map/ppermute | solution.py:328
  1152.0 29.7 %collective-permute-done.53 = bf16[2,2,2,384,512]{4,3,2,1,0:T(8,128)(2,1)} collective-permute-done((bf16[2,2,2,384,512]{4,3,2,1,0:T(8,128)(2,1)}, bf16[2,2,2,384,512]{4,3,2,1,0:T(8,128)(2,1)}, u32[]{:S(2)}, u32[]{:S(2)}) %collective-permute-start.53) | collective-permute-done | bytes 3145760 | tf_op jit(solution)/shard_map/ppermute | solution.py:328
  1192.0 111.5 %all_to_all.47 = bf16[4,640,512]{2,1,0:T(8,128)(2,1)} all-to-all(bf16[4,640,512]{2,1,0:T(8,128)(2,1)S(1)} %bitcast.203), channel_id=1, replica_groups=mesh['dp'=4,'row'=4,'col'=2] {'row'}, dimensions={0} | all-to-all | bytes 5242880 | tf_op jit(solution)/shard_map/all_to_all | solution.py:1098
  1308.9 12.6 collective-permute-done.56
  1327.8 19.3 %collective-permute-done.58.refs_2_ = bf16[2,256,1024]{2,1,0:T(8,128)(2,1)} collective-permute-done((bf16[2,256,1024]{2,1,0:T(8,128)(2,1)}, bf16[2,256,1024]{2,1,0:T(8,128)(2,1)}, u32[]{:S(2)}, u32[]{:S(2)}) %collective-permute-start.58) | collective-permute-done | bytes 1048608 | tf_op jit(solution)/shard_map/ppermute | solution.py:328
  (385 shorter events, 355.5 us)
Async XLA Ops:
  38.9 98.5 %all-to-all-start = ((bf16[4,640,512]{2,1,0:T(8,128)(2,1)}), bf16[4,640,512]{2,1,0:T(8,128)(2,1)}, u32[]{:S(2)}, u32[]{:S(2)}) async-start(bf16[4,640,512]{2,1,0:T(8,128)(2,1)} %bitcast.5), calls=%async_computation | async-start | bytes 5242880 | tf_op jit(solution)/shard_map/all_to_all | solution.py:897
  43.9 82.1 %all-gather.14.cloned.1.call-start = ((), (), s32[]{:S(2)}) async-start(), calls=%async_computation.15 | async-start | bytes 2621440 | tf_op jit(solution)/shard_map/all_gather | solution.py:900
  46.5 155.5 %all-gather.16.cloned.1.call-start = ((), (), s32[]{:S(2)}) async-start(), calls=%async_computation.16 | async-start | bytes 1310720 | tf_op jit(solution)/shard_map/all_gather | solution.py:939
  137.4 173.2 %all-gather.10.cloned.1.call-start = ((), (), s32[]{:S(2)}) async-start(), calls=%async_computation.9 | async-start | bytes 5242880 | tf_op jit(solution)/shard_map/all_gather | solution.py:940
  137.4 58.2 %collective-permute-start.5 = (bf16[2560,512]{1,0:T(8,128)(2,1)}, bf16[2560,512]{1,0:T(8,128)(2,1)}, u32[]{:S(2)}, u32[]{:S(2)}) collective-permute-start(bf16[2560,512]{1,0:T(8,128)(2,1)} %bitcast.6.x0), channel_id=1, source_target_pairs={{0,1},{1,0},{2,3},{3,2},{4,5},{5,4},{6,7},{7,6},{8,9},{9,8},{10,11... | collective-permute-start | bytes 7864328 | tf_op jit(solution)/shard_map/ppermute | solution.py:332
  138.1 57.6 %collective-permute-start.8 = (bf16[4,2,256,512]{3,2,1,0:T(8,128)(2,1)}, bf16[4,2,256,512]{3,2,1,0:T(8,128)(2,1)S(1)}, u32[]{:S(2)}, u32[]{:S(2)}) collective-permute-start(bf16[4,2,256,512]{3,2,1,0:T(8,128)(2,1)} %bitcast.225), channel_id=1, source_target_pairs={{0,16},{16,0},{8,24},{24,8},{1,17},{17,1},{9,25},{25,9},{2,18},{18... | collective-permute-start | bytes 6291464 | tf_op jit(solution)/shard_map/ppermute | solution.py:328
  139.7 74.1 %collective-permute-start.6 = (bf16[2560,512]{1,0:T(8,128)(2,1)}, bf16[2560,512]{1,0:T(8,128)(2,1)}, u32[]{:S(2)}, u32[]{:S(2)}) collective-permute-start(bf16[2560,512]{1,0:T(8,128)(2,1)} %bitcast.6.x0), channel_id=1, source_target_pairs={{0,8},{8,0},{16,24},{24,16},{1,9},{9,1},{17,25},{25,17},{2,10},{10... | collective-permute-start | bytes 7864328 | tf_op jit(solution)/shard_map/ppermute | solution.py:324
  210.1 93.4 %all-to-all-start.1 = ((bf16[4,640,512]{2,1,0:T(8,128)(2,1)}), bf16[4,640,512]{2,1,0:T(8,128)(2,1)S(1)}, u32[]{:S(2)}, u32[]{:S(2)}) async-start(bf16[4,640,512]{2,1,0:T(8,128)(2,1)} %bitcast.198), calls=%async_computation.1 | async-start | bytes 5242880 | tf_op jit(solution)/shard_map/all_to_all | solution.py:976
  213.8 164.4 %all-gather.8.cloned.1.call-start = ((), (), s32[]{:S(2)}) async-start(), calls=%async_computation.8 | async-start | bytes 5242880 | tf_op jit(solution)/shard_map/all_gather | solution.py:941
  237.5 224.0 %all-gather.12.cloned.1.call-start = ((), (), s32[]{:S(2)}) async-start(), calls=%async_computation.10 | async-start | bytes 5242880 | tf_op jit(solution)/shard_map/all_gather | solution.py:942
  309.2 58.9 %collective-permute-start.15 = (bf16[2560,512]{1,0:T(8,128)(2,1)}, bf16[2560,512]{1,0:T(8,128)(2,1)}, u32[]{:S(2)}, u32[]{:S(2)}) collective-permute-start(bf16[2560,512]{1,0:T(8,128)(2,1)} %add_convert_fusion.8), channel_id=1, source_target_pairs={{0,1},{1,0},{2,3},{3,2},{4,5},{5,4},{6,7},{7,6},{8,9},{9,8},{10,11... | collective-permute-start | bytes 7864328 | tf_op jit(solution)/shard_map/ppermute | solution.py:332
  310.6 92.2 %collective-permute-start.19 = (bf16[1024,2048]{1,0:T(8,128)(2,1)}, bf16[1024,2048]{1,0:T(8,128)(2,1)}, u32[]{:S(2)}, u32[]{:S(2)}) collective-permute-start(bf16[1024,2048]{1,0:T(8,128)(2,1)} %all-gather.10.cloned.1.call-done.refs_4_), channel_id=1, source_target_pairs={{0,16},{16,0},{8,24},{24,8},{1,17},{17,1},{9,25},{25,9},{2,18},{18... | collective-permute-start | bytes 12582920 | tf_op jit(solution)/shard_map/ppermute | solution.py:328
  312.1 704.3 %reduce-scatter.5.cloned.1.call-start = ((), (), s32[]{:S(2)}) async-start(), calls=%async_computation.11 | async-start | bytes 5242880 | tf_op jit(solution)/shard_map/reduce_scatter | solution.py:1016
  403.5 93.8 %collective-permute-start.25 = (bf16[1024,2048]{1,0:T(8,128)(2,1)}, bf16[1024,2048]{1,0:T(8,128)(2,1)}, u32[]{:S(2)}, u32[]{:S(2)}) collective-permute-start(bf16[1024,2048]{1,0:T(8,128)(2,1)} %all-gather.8.cloned.1.call-done.refs_5_), channel_id=1, source_target_pairs={{0,16},{16,0},{8,24},{24,8},{1,17},{17,1},{9,25},{25,9},{2,18},{18... | collective-permute-start | bytes 12582920 | tf_op jit(solution)/shard_map/ppermute | solution.py:328
  460.7 89.8 %collective-permute-start.21 = (bf16[2560,512]{1,0:T(8,128)(2,1)}, bf16[2560,512]{1,0:T(8,128)(2,1)}, u32[]{:S(2)}, u32[]{:S(2)}) collective-permute-start(bf16[2560,512]{1,0:T(8,128)(2,1)} %bitcast.186), channel_id=1, source_target_pairs={{0,1},{1,0},{2,3},{3,2},{4,5},{5,4},{6,7},{7,6},{8,9},{9,8},{10,11... | collective-permute-start | bytes 7864328 | tf_op jit(solution)/shard_map/ppermute | solution.py:332
  461.5 123.0 %collective-permute-start.27 = (bf16[1024,2048]{1,0:T(8,128)(2,1)}, bf16[1024,2048]{1,0:T(8,128)(2,1)}, u32[]{:S(2)}, u32[]{:S(2)}) collective-permute-start(bf16[1024,2048]{1,0:T(8,128)(2,1)} %all-gather.12.cloned.1.call-done.refs_8_.refs_2_), channel_id=1, source_target_pairs={{0,16},{16,0},{8,24},{24,8},{1,17},{17,1},{9,25},{25,9},{2,18},{18... | collective-permute-start | bytes 12582920 | tf_op jit(solution)/shard_map/ppermute | solution.py:328
  469.1 115.4 %collective-permute-start.23 = (bf16[2560,512]{1,0:T(8,128)(2,1)}, bf16[2560,512]{1,0:T(8,128)(2,1)S(1)}, u32[]{:S(2)}, u32[]{:S(2)}) collective-permute-start(bf16[2560,512]{1,0:T(8,128)(2,1)} %bitcast.187), channel_id=1, source_target_pairs={{0,8},{8,0},{16,24},{24,16},{1,9},{9,1},{17,25},{25,17},{2,10},{10... | collective-permute-start | bytes 7864328 | tf_op jit(solution)/shard_map/ppermute | solution.py:324
  641.2 94.3 %collective-permute-start.29 = (bf16[1024,2048]{1,0:T(8,128)(2,1)}, bf16[1024,2048]{1,0:T(8,128)(2,1)S(1)}, u32[]{:S(2)}, u32[]{:S(2)}) collective-permute-start(bf16[1024,2048]{1,0:T(8,128)(2,1)} %down_grad_other.1), channel_id=1, source_target_pairs={{0,16},{16,0},{8,24},{24,8},{1,17},{17,1},{9,25},{25,9},{2,18},{18... | collective-permute-start | bytes 12582920 | tf_op jit(solution)/shard_map/ppermute | solution.py:328
  739.4 278.4 %reduce-scatter.7.cloned.1.call-start = ((), (), s32[]{:S(2)}) async-start(), calls=%async_computation.12 | async-start | bytes 5242880 | tf_op jit(solution)/shard_map/reduce_scatter | solution.py:1016
  740.0 59.2 %collective-permute-start.31 = (bf16[2560,512]{1,0:T(8,128)(2,1)}, bf16[2560,512]{1,0:T(8,128)(2,1)}, u32[]{:S(2)}, u32[]{:S(2)}) collective-permute-start(bf16[2560,512]{1,0:T(8,128)(2,1)} %add_convert_fusion.7), channel_id=1, source_target_pairs={{0,1},{1,0},{2,3},{3,2},{4,5},{5,4},{6,7},{7,6},{8,9},{9,8},{10,11... | collective-permute-start | bytes 7864328 | tf_op jit(solution)/shard_map/ppermute | solution.py:332
  741.2 92.6 %collective-permute-start.35 = (bf16[1024,2048]{1,0:T(8,128)(2,1)}, bf16[1024,2048]{1,0:T(8,128)(2,1)}, u32[]{:S(2)}, u32[]{:S(2)}) collective-permute-start(bf16[1024,2048]{1,0:T(8,128)(2,1)} %gate_grad_other.1), channel_id=1, source_target_pairs={{0,16},{16,0},{8,24},{24,8},{1,17},{17,1},{9,25},{25,9},{2,18},{18... | collective-permute-start | bytes 12582920 | tf_op jit(solution)/shard_map/ppermute | solution.py:328
  814.0 59.5 %collective-permute-start.36 = (bf16[2560,512]{1,0:T(8,128)(2,1)}, bf16[2560,512]{1,0:T(8,128)(2,1)}, u32[]{:S(2)}, u32[]{:S(2)}) collective-permute-start(bf16[2560,512]{1,0:T(8,128)(2,1)} %get-tuple-element.166.h0.refs_1_), channel_id=1, source_target_pairs={{0,1},{1,0},{2,3},{3,2},{4,5},{5,4},{6,7},{7,6},{8,9},{9,8},{10,11... | collective-permute-start | bytes 7864328 | tf_op jit(solution)/shard_map/ppermute | solution.py:332
  840.3 308.8 %reduce-scatter.9.cloned.1.call-start = ((), (), s32[]{:S(2)}) async-start(), calls=%async_computation.13 | async-start | bytes 5242880 | tf_op jit(solution)/shard_map/reduce_scatter | solution.py:1016
  840.3 61.9 %collective-permute-start.37 = (bf16[2560,512]{1,0:T(8,128)(2,1)}, bf16[2560,512]{1,0:T(8,128)(2,1)S(1)}, u32[]{:S(2)}, u32[]{:S(2)}) collective-permute-start(bf16[2560,512]{1,0:T(8,128)(2,1)} %get-tuple-element.166.h0.refs_1_), channel_id=1, source_target_pairs={{0,8},{8,0},{16,24},{24,16},{1,9},{9,1},{17,25},{25,17},{2,10},{10... | collective-permute-start | bytes 7864328 | tf_op jit(solution)/shard_map/ppermute | solution.py:324
  901.6 92.9 %collective-permute-start.42 = (bf16[1024,2048]{1,0:T(8,128)(2,1)}, bf16[1024,2048]{1,0:T(8,128)(2,1)}, u32[]{:S(2)}, u32[]{:S(2)}) collective-permute-start(bf16[1024,2048]{1,0:T(8,128)(2,1)} %up_grad_other.1), channel_id=1, source_target_pairs={{0,16},{16,0},{8,24},{24,8},{1,17},{17,1},{9,25},{25,9},{2,18},{18... | collective-permute-start | bytes 12582920 | tf_op jit(solution)/shard_map/ppermute | solution.py:328
  902.2 74.7 %collective-permute-start.40 = (bf16[2560,512]{1,0:T(8,128)(2,1)}, bf16[2560,512]{1,0:T(8,128)(2,1)}, u32[]{:S(2)}, u32[]{:S(2)}) collective-permute-start(bf16[2560,512]{1,0:T(8,128)(2,1)} %get-tuple-element.156), channel_id=1, source_target_pairs={{0,8},{8,0},{16,24},{24,16},{1,9},{9,1},{17,25},{25,17},{2,10},{10... | collective-permute-start | bytes 7864328 | tf_op jit(solution)/shard_map/ppermute | solution.py:324
  920.5 59.6 %collective-permute-start.41 = (bf16[2560,512]{1,0:T(8,128)(2,1)}, bf16[2560,512]{1,0:T(8,128)(2,1)}, u32[]{:S(2)}, u32[]{:S(2)}) collective-permute-start(bf16[2560,512]{1,0:T(8,128)(2,1)} %add_convert_fusion.6), channel_id=1, source_target_pairs={{0,1},{1,0},{2,3},{3,2},{4,5},{5,4},{6,7},{7,6},{8,9},{9,8},{10,11... | collective-permute-start | bytes 7864328 | tf_op jit(solution)/shard_map/ppermute | solution.py:332
  1000.6 324.6 %reduce-scatter.11.cloned.1.call-start = ((), (), s32[]{:S(2)}) async-start(), calls=%async_computation.14 | async-start | bytes 3932160 | tf_op jit(solution)/shard_map/reduce_scatter | solution.py:1139
  1045.9 87.9 %collective-permute-start.48 = (bf16[2560,512]{1,0:T(8,128)(2,1)}, bf16[2560,512]{1,0:T(8,128)(2,1)}, u32[]{:S(2)}, u32[]{:S(2)}) collective-permute-start(bf16[2560,512]{1,0:T(8,128)(2,1)} %get-tuple-element.175), channel_id=1, source_target_pairs={{0,8},{8,0},{16,24},{24,16},{1,9},{9,1},{17,25},{25,17},{2,10},{10... | collective-permute-start | bytes 7864328 | tf_op jit(solution)/shard_map/ppermute | solution.py:324
  1066.0 67.8 %collective-permute-start.49 = (bf16[2560,512]{1,0:T(8,128)(2,1)}, bf16[2560,512]{1,0:T(8,128)(2,1)}, u32[]{:S(2)}, u32[]{:S(2)}) collective-permute-start(bf16[2560,512]{1,0:T(8,128)(2,1)} %add_convert_fusion.4), channel_id=1, source_target_pairs={{0,1},{1,0},{2,3},{3,2},{4,5},{5,4},{6,7},{7,6},{8,9},{9,8},{10,11... | collective-permute-start | bytes 7864328 | tf_op jit(solution)/shard_map/ppermute | solution.py:332
  1110.9 70.8 %collective-permute-start.53 = (bf16[2,2,2,384,512]{4,3,2,1,0:T(8,128)(2,1)}, bf16[2,2,2,384,512]{4,3,2,1,0:T(8,128)(2,1)}, u32[]{:S(2)}, u32[]{:S(2)}) collective-permute-start(bf16[2,2,2,384,512]{4,3,2,1,0:T(8,128)(2,1)} %pad_maximum_fusion), channel_id=1, source_target_pairs={{0,16},{16,0},{8,24},{24,8},{1,17},{17,1},{9,25},{25,9},{2,18},{18... | collective-permute-start | bytes 9437192 | tf_op jit(solution)/shard_map/ppermute | solution.py:328
  1303.5 63.7 %all-to-all-start.3 = ((bf16[4,640,512]{2,1,0:T(8,128)(2,1)}), bf16[4,640,512]{2,1,0:T(8,128)(2,1)S(1)}, u32[]{:S(2)}, u32[]{:S(2)}) async-start(bf16[4,640,512]{2,1,0:T(8,128)(2,1)} %bitcast.64), calls=%async_computation.6 | async-start | bytes 5242880 | tf_op jit(solution)/shard_map/all_to_all | solution.py:1134
  (92 other events, 1582.6 us)
Sparse Core Ops, SparseCore 0:
  46.9 79.0 all-gather.13
  137.5 28.2 all-gather.15
  167.4 123.5 all-gather.9
  292.4 79.5 all-gather.7
  373.4 79.2 all-gather.11
  739.5 74.6 reduce-scatter.4
  840.4 74.0 reduce-scatter.6
  1000.7 74.0 reduce-scatter.8
  1190.4 99.2 reduce-scatter.10

commit v3 on v2

--- a/solution.py
+++ b/solution.py
@@ -640,9 +640,20 @@
 
 
 def sum_out_kernel(count, *refs):
-    a_refs, w_refs = refs[:count], refs[count : 2 * count]
-    acc = sum(mxu(a[...], w[...], NN) for a, w in zip(a_refs, w_refs))
-    quarters_out(acc, refs[2 * count :])
+    a_refs = refs[:count]
+    w_refs, out_refs = refs[count:-4], refs[-4:]
+    acc = None
+    left = list(a_refs)
+    at = 0
+    for w in w_refs:
+        depth = w.shape[0]
+        part = mxu(left[0][:, at : at + depth], w[...], NN)
+        acc = part if acc is None else acc + part
+        at += depth
+        if at == left[0].shape[1]:
+            left.pop(0)
+            at = 0
+    quarters_out(acc, out_refs)
 
 
 def project_back_kernel(d_ref, near_ref, far_ref, *out_refs):
@@ -665,43 +676,101 @@
 
 
 def gate_up_kernel(*refs):
-    x_refs, w_refs, out_refs = refs[:4], refs[4:8], refs[8:12]
-    xs_ref = refs[12]
+    x_refs, w_refs, out_refs = refs[:4], refs[4:10], refs[10:14]
+    xs_ref = refs[14]
     width = x_refs[0].shape[1]
     for i, x in enumerate(x_refs):
         xs_ref[:, i * width : (i + 1) * width] = x[...]
     normed = xs_ref[...]
-    for w_ref, out_ref in zip(w_refs, out_refs):
-        unit = 512
-        for at in range(0, w_ref.shape[0], unit):
-            cols = slice(at, at + unit)
-            out_ref[:, cols] = low(mxu(normed, w_ref[cols, :], NT))
+    outs = list(out_refs)
+    at = 0
+    for w_ref in w_refs:
+        for start in range(0, w_ref.shape[0], 512):
+            size = min(512, w_ref.shape[0] - start)
+            product = mxu(normed, w_ref[start : start + size, :], NT)
+            outs[0][:, at : at + size] = low(product)
+            at += size
+        if at == outs[0].shape[1]:
+            outs.pop(0)
+            at = 0
 
 
 def hidden_kernel(*refs):
-    g_refs, gate_refs, up_refs, w_refs = refs[:4], refs[4:6], refs[6:8], refs[8:10]
-    out_refs = refs[10:16]
-    gs_ref = refs[16]
+    g_refs, gate_refs, up_refs, w_refs = refs[:4], refs[4:6], refs[6:8], refs[8:11]
+    out_refs = refs[11:17]
+    gs_ref = refs[17]
     width = g_refs[0].shape[1]
     for i, g in enumerate(g_refs):
         gs_ref[:, i * width : (i + 1) * width] = g[...]
     grads = gs_ref[...]
-    for side in range(2):
-        w_ref = w_refs[side]
+    unit = 256
+    places = [(0, w_refs[0], i, i) for i in range(0, w_refs[0].shape[0], unit)]
+    places += [(1, w_refs[1], i, i) for i in range(0, w_refs[1].shape[0], unit)]
+    first = w_refs[1].shape[0]
+    places += [(1, w_refs[2], i, first + i) for i in range(0, w_refs[2].shape[0], unit)]
+    for side, w_ref, row, at in places:
         dgate_ref, dup_ref, hid_ref = out_refs[3 * side : 3 * side + 3]
-        unit = 256
-        for at in range(0, w_ref.shape[0], unit):
-            cols = slice(at, at + unit)
-            gate = wide(gate_refs[side][:, cols])
-            upper = wide(up_refs[side][:, cols])
-            hidden_grad = mxu(grads, w_ref[cols, :], NT)
-            sigma = jax.nn.sigmoid(gate)
-            silu_value = gate * sigma
-            hid_ref[:, cols] = low(silu_value * upper)
-            dgate_ref[:, cols] = low(
-                hidden_grad * upper * sigma * (1.0 + gate * (1.0 - sigma))
-            )
-            dup_ref[:, cols] = low(hidden_grad * silu_value)
+        cols = slice(at, at + unit)
+        gate = wide(gate_refs[side][:, cols])
+        upper = wide(up_refs[side][:, cols])
+        hidden_grad = mxu(grads, w_ref[row : row + unit, :], NT)
+        sigma = jax.nn.sigmoid(gate)
+        silu_value = gate * sigma
+        hid_ref[:, cols] = low(silu_value * upper)
+        dgate_ref[:, cols] = low(hidden_grad * upper * sigma * (1.0 + gate * (1.0 - sigma)))
+        dup_ref[:, cols] = low(hidden_grad * silu_value)
+
+
+def pass_kernel(where_ref, in_ref, out_ref):
+    out_ref[...] = in_ref[...]
+
+
+def next_blocks(gathered, z, planes):
+    rows, width = gathered.shape
+    unit = rows // planes
+    return pl.pallas_call(
+        pass_kernel,
+        grid_spec=pltpu.PrefetchScalarGridSpec(
+            num_scalar_prefetch=1,
+            grid=(planes - 1,),
+            in_specs=[pl.BlockSpec((unit, width), lambda i, w: (lax.rem(w[0] + 1 + i, planes), 0))],
+            out_specs=pl.BlockSpec((unit, width), lambda i, w: (i, 0)),
+        ),
+        out_shape=jax.ShapeDtypeStruct((rows - unit, width), gathered.dtype),
+        compiler_params=pltpu.CompilerParams(vmem_limit_bytes=VMEM_LIMIT),
+        cost_estimate=cost(0, 4 * rows * width),
+        name="next_blocks",
+    )(z.reshape(1), gathered)
+
+
+def turned_grad_kernel(count, where_ref, *refs):
+    weight_grad_kernel(count, 0, *refs)
+
+
+def turned_grad(a, bs, z, planes, name):
+    rows, m = a.shape
+    n = sum(b.shape[1] for b in bs)
+    unit = m // planes
+    in_specs = [
+        pl.BlockSpec((rows, unit), lambda i, w: (0, lax.rem(i + planes - w[0], planes)))
+    ]
+    for b in bs:
+        in_specs.append(
+            pl.BlockSpec(b.shape, lambda i, w: (0, 0), pipeline_mode=pl.Buffered(1))
+        )
+    return pl.pallas_call(
+        functools.partial(turned_grad_kernel, len(bs)),
+        grid_spec=pltpu.PrefetchScalarGridSpec(
+            num_scalar_prefetch=1,
+            grid=(planes,),
+            in_specs=in_specs,
+            out_specs=pl.BlockSpec((unit, n), lambda i, w: (i, 0)),
+        ),
+        out_shape=jax.ShapeDtypeStruct((m, n), jnp.bfloat16),
+        compiler_params=pltpu.CompilerParams(vmem_limit_bytes=VMEM_LIMIT),
+        cost_estimate=cost(2 * rows * m * n, 2 * (rows * m + rows * n + m * n)),
+        name=name,
+    )(z.reshape(1), a, *bs)
 
 
 def ffn_home_kernel(turned, where_ref, *refs):
@@ -879,23 +948,24 @@
     def by_core(a):
         return jnp.where(c == 0, a, jnp.concatenate([a[:, quarter:], a[:, :quarter]], axis=1))
 
-    def hidden_piece(j):
-        at = ((2 * j + c) * 2 + x) * unit
+    def four(kept, got):
+        return jnp.concatenate(
+            [kept[:, :quarter], got[:, :quarter], kept[:, quarter:], got[:, quarter:]], axis=1
+        )
+
+    project_sent = project_piece(1 - y)
+    project_mine = jnp.stack([project_piece(y), swap_col(project_sent)])
+    trees = to_trees(tokens)
+    block_in = lax.all_to_all(trees, "row", 0, 0, tiled=True)
+    def hidden_piece(j, xh):
+        at = ((2 * j + c) * 2 + xh) * unit
         return [
             by_core(lax.dynamic_slice_in_dim(w_gate, at, unit, 1).T),
             by_core(lax.dynamic_slice_in_dim(w_up, at, unit, 1).T),
             by_core(lax.dynamic_slice_in_dim(w_down, at, unit, 0)),
         ]
 
-    def four(kept, got):
-        return jnp.concatenate(
-            [kept[:, :quarter], got[:, :quarter], kept[:, quarter:], got[:, quarter:]], axis=1
-        )
-
-    project_sent = project_piece(1 - y)
-    project_mine = jnp.stack([project_piece(y), swap_col(project_sent)])
-    block_in = lax.all_to_all(to_trees(tokens), "row", 0, 0, tiled=True)
-    sent = jnp.concatenate([*hidden_piece(1 - y), jnp.tile(mix_piece(1 - y), (1, 2))])
+    sent = jnp.concatenate([*hidden_piece(1 - y, x), jnp.tile(mix_piece(1 - y), (1, 2))])
     got = swap_col(after(sent, project_sent))
     project_all = lax.all_gather(project_mine, "row", axis=0)
 
@@ -909,11 +979,17 @@
     label_col = marks[0][:, None]
     label_rows = jnp.pad(marks, ((0, 4), (0, 0)))
 
-    hidden_kept = hidden_piece(y)
     hidden_mine = [
-        four(kept, got[i * unit : (i + 1) * unit]) for i, kept in enumerate(hidden_kept)
+        four(kept, got[i * unit : (i + 1) * unit])
+        for i, kept in enumerate(hidden_piece(y, x))
     ]
     mix_mine = jnp.stack([mix_piece(y), got[3 * unit :, :quarter]])
+    near_sent = jnp.concatenate(hidden_piece(1 - y, 1 - x))
+    near_got = swap_col(after(near_sent, mix_mine))
+    hidden_near = [
+        four(kept, near_got[i * unit : (i + 1) * unit])
+        for i, kept in enumerate(hidden_piece(y, 1 - x))
+    ]
 
     def gain_order(gain):
         kept = gain.reshape(2, quarter)
@@ -927,10 +1003,10 @@
 
     (
         project_all, block_in, mix_mine, gate_piece, up_piece, down_piece,
-        cosine, sine, label_col, label_rows, gain_attn_all,
+        gate_near, up_near, down_near, cosine, sine, label_col, label_rows, gain_attn_all,
     ) = lax.optimization_barrier(
         (
-            project_all, block_in, mix_mine, *hidden_mine,
+            project_all, block_in, mix_mine, *hidden_mine, *hidden_near,
             cosine, sine, label_col, label_rows, gain_attn_all,
         )
     )
@@ -940,7 +1016,10 @@
     gate_mine = lax.all_gather(gate_piece, "row", axis=0, tiled=True)
     up_mine = lax.all_gather(after(up_piece, mix_all), "row", axis=0, tiled=True)
     down_mine = lax.all_gather(after(down_piece, gate_mine), "row", axis=0, tiled=True)
-    gate_far, up_far, down_far = (swap_x(u) for u in (gate_mine, up_mine, down_mine))
+    gate_next, up_next, down_next = (
+        next_blocks(u, z, planes) for u in (gate_mine, up_mine, down_mine)
+    )
+    gate_far, up_far, down_far = (swap_x(u) for u in (gate_next, up_next, down_next))
 
     def of_core_pairs(mine, other):
         both = in_order(x, mine, other, 2)
@@ -974,19 +1053,21 @@
         "mix",
     )
     cotangent = lax.all_to_all(to_trees(out_grad), "row", 0, 0, tiled=True)
-    parts[1] = after(parts[1], cotangent)
+    parts[1] = after(parts[1], cotangent, gate_next)
     own, got, outgoing = collect_core(parts)
     middle = wide(block_in) + collect_col(own, got, outgoing)
     square = small_sum(jnp.sum(middle * middle, axis=1))
     ratio_ffn = lax.rsqrt(square / features + EPSILON)[:, None]
     normed_ffn = middle * ratio_ffn
-    ffn_pieces = spread(after(low(normed_ffn * gain_ffn_own), up_mine, gate_far))
+    ffn_near = after(low(normed_ffn * gain_ffn_own), up_next, gate_far)
+    ffn_across = swap_col(ffn_near)
+    ffn_pieces = [ffn_near, ffn_across, swap_core(ffn_near), swap_core(ffn_across)]
     grad_near, grad_across = cotangent, swap_col(after(cotangent, ffn_pieces[1]))
     gate_m, up_m, gate_o, up_o = rows_call(
         gate_up_kernel,
         block,
         ffn_pieces,
-        [gate_mine, up_mine, gate_far, up_far],
+        [gate_mine, up_mine, gate_near, gate_far, up_near, up_far],
         [(planes * unit, jnp.bfloat16)] * 4,
         2 * rows * features * 4 * planes * unit,
         "gate_up",
@@ -1002,7 +1083,7 @@
         hidden_kernel,
         block,
         [*grad_pieces, gate_m, gate_o, up_m, up_o],
-        [down_mine, down_far],
+        [down_mine, down_near, down_far],
         [(planes * unit, jnp.bfloat16)] * 6,
         2 * rows * features * 2 * planes * unit,
         "hidden",
@@ -1015,23 +1096,23 @@
     def to_row(total):
         return lax.psum_scatter(total, "row", scatter_dimension=0, tiled=True)
 
-    down_other = weight_grad(hid_o, grad_pieces, 2 * block, "down_grad_other")
+    down_other = turned_grad(hid_o, grad_pieces, z, planes, "down_grad_other")
     parts = rows_call(
         functools.partial(sum_out_kernel, 4),
         2 * block,
         [after(dgate_m, down_other), dup_m, dgate_o, dup_o],
-        [gate_mine, up_mine, gate_far, up_far],
+        [gate_mine, up_mine, gate_near, gate_far, up_near, up_far],
         [(quarter, jnp.bfloat16)] * 4,
         2 * rows * features * 4 * planes * unit,
         "pair_back",
     )
-    gate_other = unit_grad(dgate_o, ffn_pieces, "gate_grad_other", parts[0])
+    gate_other = turned_grad(after(dgate_o, parts[0]), ffn_pieces, z, planes, "gate_grad_other")
     down_own = unit_grad(hid_m, grad_pieces, "down_grad_mine", gate_other)
     parts[1] = after(parts[1], down_own)
     own, got, outgoing = collect_core(parts)
     down_total = low(wide(after(down_own, outgoing)) + wide(swap_x(down_other)))
     down_sum = to_row(down_total)
-    up_other = unit_grad(dup_o, ffn_pieces, "up_grad_other", down_total)
+    up_other = turned_grad(after(dup_o, down_total), ffn_pieces, z, planes, "up_grad_other")
     gate_own = unit_grad(dgate_m, ffn_pieces, "gate_grad_mine", up_other)
     normed_ffn_grad = collect_col(after(own, gate_own), got, outgoing)
 
@@ -1043,7 +1124,6 @@
     middle_back, gain_ffn_part = norm_back(normed_ffn_grad, ratio_ffn, normed_ffn, gain_ffn_own)
     middle_grad = wide(cotangent) + middle_back
     middle_low = low(middle_grad)
-    middle_pieces = spread(middle_low)
     up_own = unit_grad(dup_m, ffn_pieces, "up_grad_mine", middle_low)
     gate_total = low(wide(after(gate_own, up_own)) + wide(swap_x(gate_other)))
     gate_sum = to_row(gate_total)
@@ -1054,24 +1134,26 @@
         sent = jnp.concatenate([total[:, quarter:half], total[:, half + quarter :]], axis=1)
         return kept, sent
 
-    def unit_parts(kept, sent):
-        both = jnp.stack([kept, swap_col(sent)])
-        over = swap_x(both)
+    def unit_parts(kept, sent, first, second):
+        both = jnp.stack([kept, after(swap_col(sent), first)])
+        over = after(swap_x(both), second)
         return [both, swap_core(both), over, swap_core(over)]
 
     out_parts = rows_call(
         functools.partial(sum_out_kernel, 2),
         2 * block,
         [after(hid_m, gate_total), hid_o],
-        [down_mine, down_far],
+        [down_mine, down_near, down_far],
         [(quarter, jnp.bfloat16)] * 4,
         2 * rows * features * 2 * planes * unit,
         "down",
     )
+    middle_across = after(swap_col(middle_low), out_parts[0])
+    middle_pieces = [middle_low, middle_across, swap_core(middle_low), swap_core(middle_across)]
     attn_grad = rows_call(
         attn_grad_kernel,
         2 * block,
-        [after(middle_pieces[0], out_parts[0]), *middle_pieces[1:]],
+        middle_pieces,
         [m_near, m_far],
         [(groups * 2 * HEAD, jnp.bfloat16)],
         2 * rows * features * groups * 2 * HEAD,
@@ -1096,17 +1178,13 @@
         "project_back",
     )
     output_tree = lax.all_to_all(output, "row", 0, 0, tiled=True)
-    home_kept, home_sent = unit_halves(
-        jnp.concatenate([after(down_sum, parts[0]), gate_sum])
-    )
+    own, got, outgoing = collect_core(parts)
     project_grad = weight_grad(
-        normed_attn, [after(qkv_grad, home_sent)], 2 * block, "project_grad", split=groups
-    )
-    parts[1] = after(parts[1], project_grad)
-    own, got, outgoing = collect_core(parts)
+        normed_attn, [after(qkv_grad, outgoing)], 2 * block, "project_grad", split=groups
+    )
     mix_grads = weight_grad(
         attn,
-        [after(middle_pieces[0], outgoing), *middle_pieces[1:]],
+        [after(middle_pieces[0], project_grad), *middle_pieces[1:]],
         groups * 2 * HEAD,
         "mix_grad",
         joined=False,
@@ -1121,26 +1199,27 @@
 
     attn_sent = of_x(1 - x)
     attn_kept = of_x(after(x, attn_sent))
-    home_parts = unit_parts(home_kept, home_sent)
-    home_parts[0] = after(home_parts[0], attn_kept)
-    down_out = ffn_home(where, home_parts, 0, unit, False, "down_home")
-    gate_out = ffn_home(where, home_parts, 1, unit, True, "gate_home")
-    normed_attn_grad = collect_col(after(own, down_out, gate_out), got, outgoing)
+    normed_attn_grad = collect_col(after(own, attn_kept), got, outgoing)
     normed_attn_own = wide(block_in) * ratio_attn
     input_back, gain_attn_part = norm_back(
         normed_attn_grad, ratio_attn, normed_attn_own, gain_attn_own
     )
     input_low = low(middle_grad + input_back)
     input_tree = lax.all_to_all(input_low, "row", 0, 0, tiled=True)
-    up_kept, up_sent = unit_halves(after(up_sum, input_low))
-    attn_total = low(wide(after(attn_kept, up_sent)) + wide(swap_x(attn_sent)))
+    home_kept, home_sent = unit_halves(
+        jnp.concatenate([after(down_sum, input_low), gate_sum])
+    )
+    output, output_sent = of_core(after(output_tree, home_sent))
+    attn_total = low(wide(after(attn_kept, output_sent)) + wide(swap_x(attn_sent)))
     by_plane = in_order(c, attn_total[:, 0], swap_core(attn_total[:, 1]))
     by_plane = by_plane.reshape((planes,) + by_plane.shape[2:])
     attn_sum = lax.psum_scatter(by_plane, "row", scatter_dimension=0, tiled=False)
-    output, output_sent = of_core(after(output_tree, by_plane))
-    output = by_feature(output, output_sent)
-    up_parts = unit_parts(up_kept, up_sent)
-    up_parts[0] = after(up_parts[0], output)
+    output = by_feature(after(output, by_plane), output_sent)
+    up_kept, up_sent = unit_halves(after(up_sum, output))
+    home_parts = unit_parts(home_kept, home_sent, attn_total, up_sent)
+    down_out = ffn_home(where, home_parts, 0, unit, False, "down_home")
+    gate_out = ffn_home(where, home_parts, 1, unit, True, "gate_home")
+    up_parts = unit_parts(up_kept, up_sent, home_parts[0], gate_out)
     up_out = ffn_home(where, up_parts, 0, unit, True, "up_home")
     input_grad = by_feature(*of_core(after(input_tree, up_out)))
 

time: 1420 us -> 1330 us (0.937)
  blocking collectives: 111 us -> 0 us
  waiting for transfers between devices: 564 us -> 537 us
  local copies, waits for them, and re-layouts: 57.3 us -> 76.2 us
    all_to_all x1 -> x0, blocking collectives: 111 us -> none  [tree_body(): output_tree = lax.all_to_all(output, 'row', 0, 0, tiled=True)]
    pallas_call x0 -> x6, Pallas kernels: none -> 65.2 us  [the longest x3 51.6 us: turned_grad(): pl.pallas_call(functools.partial(turned_grad_kernel, len(bs)), grid_spec=...]
    pallas_call x8 -> x5, Pallas kernels: 133 us -> 80.1 us  [weight_grad(): pl.pallas_call(functools.partial(weight_grad_kernel, len(bs), split), gri...]
    all_to_all x1 -> x2, waiting for transfers between devices: 11.4 us -> 56.5 us  [the longest x1 45.3 us: tree_body(): output_tree = lax.all_to_all(output, 'row', 0, 0, tiled=True)]
    ppermute x13, waiting for transfers between devices: 175 us -> 142 us  [swap_x(): return lax.ppermute(a, 'dp', X_SWAP)]
    ppermute x17 -> x18, waiting for transfers between devices: 282 us -> 256 us  [swap_col(): return lax.ppermute(a, 'col', COL_SWAP)]
    all_gather x1, waiting for transfers between devices: 48.8 us -> 23.9 us  [tree_body(): project_all = lax.all_gather(project_mine, 'row', axis=0)]
  transfers between devices with their start and end apart: 80 -> 82, of which waited for: 35 -> 33; matrix products, arithmetic and copies ran while one was open for 11% -> 14% of each run, Pallas kernels for 30% -> 29%
where the time goes in v3:
time: 1330 us; the launch traced here: 1320 us
  waiting for transfers between devices  537 us (40%)
  Pallas kernels  485 us (36%)
  other arithmetic  135 us (10%)
  local copies, waits for them, and re-layouts  76.2 us (6%)
  starting transfers between devices  72.4 us (5%)
  between operations  15.3 us (1%)
    ppermute x18, waiting for transfers between devices, swap_col(): return lax.ppermute(a, 'col', COL_SWAP)  256 us
    pallas_call x8, Pallas kernels, rows_call(): pl.pallas_call(fn, grid=(rows // block,), in_specs=in_specs, out_specs=[p...  226 us
    ppermute x13, waiting for transfers between devices, swap_x(): return lax.ppermute(a, 'dp', X_SWAP)  142 us
    pallas_call x5, Pallas kernels, weight_grad(): pl.pallas_call(functools.partial(weight_grad_kernel, len(bs), split), gri...  80.1 us
    convert_element_type x12, other arithmetic, low(): return a.astype(jnp.bfloat16)  56.3 us
    pallas_call x1, Pallas kernels, attend_back(): pl.pallas_call(functools.partial(attend_back_kernel, trunk, leaf_begin, b...  56 us
    pallas_call x3, Pallas kernels, turned_grad(): pl.pallas_call(functools.partial(turned_grad_kernel, len(bs)), grid_spec=...  51.6 us
    all_to_all x1, waiting for transfers between devices, tree_body(): output_tree = lax.all_to_all(output, 'row', 0, 0, tiled=True)  45.3 us
  transfers between devices with their start and end apart: 82, of which 33 were waited for; matrix products, arithmetic and copies ran while one was open for 14% of the time, Pallas kernels for 29%

profile of v3, /device:TPU:0, one launch (start us, length us, event | category | flops | bytes accessed | tf_op | source)
XLA Modules:
  0.0 1320.7 jit_solution(3766843921423153793)
XLA Ops:
  62.3 13.0 collective-permute-done.2
  95.1 18.0 %collective-permute-done.3 = bf16[768,1024]{1,0:T(8,128)(2,1)} collective-permute-done((bf16[768,1024]{1,0:T(8,128)(2,1)}, bf16[768,1024]{1,0:T(8,128)(2,1)}, u32[]{:S(2)}, u32[]{:S(2)}) %collective-permute-start.3) | collective-permute-done | bytes 1572896 | tf_op jit(solution)/shard_map/ppermute | solution.py:332
  117.9 23.9 %all-gather.14.cloned.1.call-done = bf16[8,256,512]{2,1,0:T(8,128)(2,1)} async-done(((bf16[2,256,512]{2,1,0:T(8,128)(2,1)}), bf16[8,256,512]{2,1,0:T(8,128)(2,1)}) %all-gather.14.cloned.1.call-update) | async-done | bytes 2097168 | tf_op jit(solution)/shard_map/all_gather | solution.py:970
  155.6 55.8 %collective-permute-done.6.x1 = bf16[2560,512]{1,0:T(8,128)(2,1)} collective-permute-done((bf16[2560,512]{1,0:T(8,128)(2,1)S(1)}, bf16[2560,512]{1,0:T(8,128)(2,1)}, u32[]{:S(2)}, u32[]{:S(2)}) %collective-permute-start.6) | collective-permute-done | bytes 2621472 | tf_op jit(solution)/shard_map/ppermute | solution.py:332
  231.5 20.2 %project.1 = (bf16[2560,2048]{1,0:T(8,128)(2,1)}, bf16[2560,1024]{1,0:T(8,128)(2,1)}, f32[2560,1]{1,0:T(8,128)}) custom-call(bf16[2560,512]{1,0:T(8,128)(2,1)} %bitcast.192, bf16[2560,512]{1,0:T(8,128)(2,1)} %collective-permute-done.6.x1, bf16[2560,512]{1,0:T(8,128)(2,1)} %collective-permute-done.7.x2, bf16[2560,512]{1,0:T(8,128)(2,1)} %collective-permute-done.8.x3, ...), custom_call_target="tpu_custom_call" | custom-call | flops 1342177280 | bytes 4131072 | tf_op jit(solution)/shard_map/project/pallas_call | solution.py:372
  256.2 34.4 %attend.1 = (bf16[2560,512]{1,0:T(8,128)(2,1)}, f32[2,10,1,512]{3,2,1,0:T(1,128)}) custom-call(bf16[2560,1024]{1,0:T(8,128)(2,1)} %get-tuple-element.109.q_ref.k_ref.v_ref, bf16[2560,1024]{1,0:T(8,128)(2,1)} %get-tuple-element.109.q_ref.k_ref.v_ref, bf16[2560,1024]{1,0:T(8,128)(2,1)} %get-tuple-element.109.q_ref.k_ref.v_ref, s32[2560,1]{1,0:T(8,128)} %copy.90.lab_ref, ...), custom_call_target="tpu_custom_call" | custom-call | flops 3355443200 | bytes 1638400 | tf_op jit(solution)/shard_map/attend/pallas_call | solution.py:585
  305.7 17.6 %all-to-all-done.1 = bf16[4,640,512]{2,1,0:T(8,128)(2,1)} async-done(((bf16[4,640,512]{2,1,0:T(8,128)(2,1)}), bf16[4,640,512]{2,1,0:T(8,128)(2,1)}, u32[]{:S(2)}, u32[]{:S(2)}) %all-to-all-start.1) | async-done | bytes 2621472 | tf_op jit(solution)/shard_map/all_to_all | solution.py:1055
  329.9 55.3 %collective-permute-done.16 = bf16[2560,512]{1,0:T(8,128)(2,1)S(1)} collective-permute-done((bf16[2560,512]{1,0:T(8,128)(2,1)S(1)}, bf16[2560,512]{1,0:T(8,128)(2,1)S(1)}, u32[]{:S(2)}, u32[]{:S(2)}) %collective-permute-start.16) | collective-permute-done | bytes 2621472 | tf_op jit(solution)/shard_map/ppermute | solution.py:332
  400.0 57.1 %collective-permute-done.21.refs_1_.refs_2_ = bf16[2560,512]{1,0:T(8,128)(2,1)S(1)} collective-permute-done((bf16[2560,512]{1,0:T(8,128)(2,1)}, bf16[2560,512]{1,0:T(8,128)(2,1)S(1)}, u32[]{:S(2)}, u32[]{:S(2)}) %collective-permute-start.21) | collective-permute-done | bytes 2621472 | tf_op jit(solution)/shard_map/ppermute | solution.py:332
  458.3 11.9 all-gather.12.cloned.1.call-done.in_ref.refs_8_.refs_2_
  476.2 53.0 %gate_up.1 = (bf16[2560,1024]{1,0:T(8,128)(2,1)}, bf16[2560,1024]{1,0:T(8,128)(2,1)}, bf16[2560,1024]{1,0:T(8,128)(2,1)}, bf16[2560,1024]{1,0:T(8,128)(2,1)}) custom-call(bf16[2560,512]{1,0:T(8,128)(2,1)} %multiply_convert_fusion.refs_0_.refs_1_, bf16[2560,512]{1,0:T(8,128)(2,1)} %copy-done.4, bf16[2560,512]{1,0:T(8,128)(2,1)} %collective-permute-done.25.refs_2_.refs_3_, ...), custom_call_target="tpu_custom_call" | custom-call | flops 5368709120 | bytes 6029312 | tf_op jit(solution)/shard_map/gate_up/pallas_call | solution.py:372
  529.7 15.1 %collective-permute-done.28.refs_10_.refs_4_ = bf16[768,2048]{1,0:T(8,128)(2,1)} collective-permute-done((bf16[768,2048]{1,0:T(8,128)(2,1)}, bf16[768,2048]{1,0:T(8,128)(2,1)}, u32[]{:S(2)}, u32[]{:S(2)}) %collective-permute-start.28) | collective-permute-done | bytes 3145760 | tf_op jit(solution)/shard_map/ppermute | solution.py:328
  547.2 37.0 %hidden.1 = (bf16[2560,1024]{1,0:T(8,128)(2,1)}, bf16[2560,1024]{1,0:T(8,128)(2,1)}, bf16[2560,1024]{1,0:T(8,128)(2,1)}, bf16[2560,1024]{1,0:T(8,128)(2,1)}, bf1...) custom-call(bf16[2560,512]{1,0:T(8,128)(2,1)} %bitcast.39.refs_0_.refs_1_, ...), custom_call_target="tpu_custom_call" | custom-call | flops 2684354560 | bytes 8912896 | tf_op jit(solution)/shard_map/hidden/pallas_call | solution.py:372
  584.2 17.1 %down_grad_other.1 = bf16[1024,2048]{1,0:T(8,128)(2,1)} custom-call(s32[1]{0:T(128)} %bitcast.40.where_ref, bf16[2560,1024]{1,0:T(8,128)(2,1)} %get-tuple-element.138.refs_0_.refs_1_, bf16[2560,512]{1,0:T(8,128)(2,1)} %bitcast.39.refs_0_.refs_1_, bf16[2560,512]{1,0:T(8,128)(2,1)} %collective-permute-done.22.refs_1_.refs_2_, bf16[2560,512]{1,0:T(8,128)(2,1)} %copy-done.5, ...), custom_call_target="tpu_custom_call" | custom-call | flops 1342177280 | bytes 2490368 | tf_op jit(solution)/shard_map/down_grad_other/pallas_call | solution.py:761
  601.3 53.1 %pair_back.1 = (bf16[2560,512]{1,0:T(8,128)(2,1)}, bf16[2560,512]{1,0:T(8,128)(2,1)}, bf16[2560,512]{1,0:T(8,128)(2,1)}, bf16[2560,512]{1,0:T(8,128)(2,1)}) custom-call(bf16[2560,1024]{1,0:T(8,128)(2,1)} %get-tuple-element.152.refs_0_, bf16[2560,1024]{1,0:T(8,128)(2,1)} %get-tuple-element.155.refs_1_.refs_0_, ...), custom_call_target="tpu_custom_call" | custom-call | flops 5368709120 | bytes 6029312 | tf_op jit(solution)/shard_map/pair_back/pallas_call | solution.py:372
  656.0 17.1 %gate_grad_other.1 = bf16[1024,2048]{1,0:T(8,128)(2,1)} custom-call(s32[1]{0:T(128)} %bitcast.40.where_ref, bf16[2560,1024]{1,0:T(8,128)(2,1)} %get-tuple-element.145.refs_2_.refs_0_, bf16[2560,512]{1,0:T(8,128)(2,1)} %multiply_convert_fusion.refs_0_.refs_1_, bf16[2560,512]{1,0:T(8,128)(2,1)} %copy-done.4, ...), custom_call_target="tpu_custom_call" | custom-call | flops 1342177280 | bytes 2490368 | tf_op jit(solution)/shard_map/gate_grad_other/pallas_call | solution.py:761
  673.1 17.6 %down_grad_mine.1 = bf16[1024,2048]{1,0:T(8,128)(2,1)} custom-call(bf16[2560,1024]{1,0:T(8,128)(2,1)} %get-tuple-element.157.refs_0_, bf16[2560,512]{1,0:T(8,128)(2,1)} %bitcast.39.refs_0_.refs_1_, bf16[2560,512]{1,0:T(8,128)(2,1)} %collective-permute-done.22.refs_1_.refs_2_, bf16[2560,512]{1,0:T(8,128)(2,1)} %copy-done.5, bf16[2560,512]{1,0:T(8,128)(2,1)} %copy-done.6), custom_call_target="tpu_custom_call" | custom-call | flops 1342177280 | bytes 2490368 | tf_op jit(solution)/shard_map/down_grad_mine/pallas_call | solution.py:848
  697.9 50.2 %collective-permute-done.30 = bf16[1024,2048]{1,0:T(8,128)(2,1)S(1)} collective-permute-done((bf16[1024,2048]{1,0:T(8,128)(2,1)}, bf16[1024,2048]{1,0:T(8,128)(2,1)S(1)}, u32[]{:S(2)}, u32[]{:S(2)}) %collective-permute-start.30) | collective-permute-done | bytes 4194336 | tf_op jit(solution)/shard_map/ppermute | solution.py:328
  752.1 17.3 %up_grad_other.1 = bf16[1024,2048]{1,0:T(8,128)(2,1)} custom-call(s32[1]{0:T(128)} %bitcast.40.where_ref, bf16[2560,1024]{1,0:T(8,128)(2,1)} %get-tuple-element.151.refs_3_.refs_0_, bf16[2560,512]{1,0:T(8,128)(2,1)} %multiply_convert_fusion.refs_0_.refs_1_, bf16[2560,512]{1,0:T(8,128)(2,1)} %copy-done.4, ...), custom_call_target="tpu_custom_call" | custom-call | flops 1342177280 | bytes 2490368 | tf_op jit(solution)/shard_map/up_grad_other/pallas_call | solution.py:761
  769.4 17.5 %gate_grad_mine.1 = bf16[1024,2048]{1,0:T(8,128)(2,1)} custom-call(bf16[2560,1024]{1,0:T(8,128)(2,1)} %get-tuple-element.152.refs_0_, bf16[2560,512]{1,0:T(8,128)(2,1)} %multiply_convert_fusion.refs_0_.refs_1_, bf16[2560,512]{1,0:T(8,128)(2,1)} %copy-done.4, bf16[2560,512]{1,0:T(8,128)(2,1)} %collective-permute-done.25.refs_2_.refs_3_, ...), custom_call_target="tpu_custom_call" | custom-call | flops 1342177280 | bytes 2490368 | tf_op jit(solution)/shard_map/gate_grad_mine/pallas_call | solution.py:848
  805.7 17.7 %up_grad_mine.1 = bf16[1024,2048]{1,0:T(8,128)(2,1)} custom-call(bf16[2560,1024]{1,0:T(8,128)(2,1)} %get-tuple-element.155.refs_1_.refs_0_, bf16[2560,512]{1,0:T(8,128)(2,1)} %multiply_convert_fusion.refs_0_.refs_1_, bf16[2560,512]{1,0:T(8,128)(2,1)} %copy-done.4, bf16[2560,512]{1,0:T(8,128)(2,1)} %collective-permute-done.25.refs_2_.refs_3_, ...), custom_call_target="tpu_custom_call" | custom-call | flops 1342177280 | bytes 2490368 | tf_op jit(solution)/shard_map/up_grad_mine/pallas_call | solution.py:848
  823.4 14.3 %collective-permute-done.37 = bf16[1024,2048]{1,0:T(8,128)(2,1)} collective-permute-done((bf16[1024,2048]{1,0:T(8,128)(2,1)}, bf16[1024,2048]{1,0:T(8,128)(2,1)}, u32[]{:S(2)}, u32[]{:S(2)}) %collective-permute-start.37) | collective-permute-done | bytes 4194336 | tf_op jit(solution)/shard_map/ppermute | solution.py:328
  844.1 27.5 %down.1 = (bf16[2560,512]{1,0:T(8,128)(2,1)}, bf16[2560,512]{1,0:T(8,128)(2,1)}, bf16[2560,512]{1,0:T(8,128)(2,1)}, bf16[2560,512]{1,0:T(8,128)(2,1)}) custom-call(bf16[2560,1024]{1,0:T(8,128)(2,1)} %get-tuple-element.157.refs_0_, bf16[2560,1024]{1,0:T(8,128)(2,1)} %get-tuple-element.138.refs_0_.refs_1_, ...), custom_call_target="tpu_custom_call" | custom-call | flops 2684354560 | bytes 3670016 | tf_op jit(solution)/shard_map/down/pallas_call | solution.py:372
  897.3 56.0 %attend_back.1.d_ref.refs_1_ = bf16[2560,1024]{1,0:T(8,128)(2,1)} custom-call(bf16[2560,1024]{1,0:T(8,128)(2,1)} %get-tuple-element.109.q_ref.k_ref.v_ref, bf16[2560,1024]{1,0:T(8,128)(2,1)} %get-tuple-element.109.q_ref.k_ref.v_ref, bf16[2560,1024]{1,0:T(8,128)(2,1)} %get-tuple-element.109.q_ref.k_ref.v_ref, ...), custom_call_target="tpu_custom_call" | custom-call | flops 8388608000 | bytes 3276800 | tf_op jit(solution)/shard_map/attend_back/pallas_call | solution.py:608
  971.3 15.5 %project_back.1 = (bf16[2560,512]{1,0:T(8,128)(2,1)}, bf16[2560,512]{1,0:T(8,128)(2,1)}, bf16[2560,512]{1,0:T(8,128)(2,1)}, bf16[2560,512]{1,0:T(8,128)(2,1)}) custom-call(bf16[2560,1024]{1,0:T(8,128)(2,1)} %attend_back.1.d_ref.refs_1_, bf16[2,1024,512]{2,1,0:T(8,128)(2,1)} %bitcast.199, bf16[2,1024,512]{2,1,0:T(8,128)(2,1)} %bitcast.29.far_ref), custom_call_target="tpu_custom_call" | custom-call | flops 1342177280 | bytes 2490368 | tf_op jit(solution)/shard_map/project_back/pallas_call | solution.py:372
  1006.5 15.9 %project_grad.1 = bf16[2,2048,512]{2,1,0:T(8,128)(2,1)} custom-call(bf16[2560,2048]{1,0:T(8,128)(2,1)} %get-tuple-element.171.refs_0_, bf16[2560,1024]{1,0:T(8,128)(2,1)} %attend_back.1.d_ref.refs_1_), custom_call_target="tpu_custom_call" | custom-call | flops 1342177280 | bytes 2490368 | tf_op jit(solution)/shard_map/project_grad/pallas_call | solution.py:848
  1041.4 16.9 %collective-permute-done.46 = bf16[2560,512]{1,0:T(8,128)(2,1)} collective-permute-done((bf16[2560,512]{1,0:T(8,128)(2,1)}, bf16[2560,512]{1,0:T(8,128)(2,1)}, u32[]{:S(2)}, u32[]{:S(2)}) %collective-permute-start.46) | collective-permute-done | bytes 2621472 | tf_op jit(solution)/shard_map/ppermute | solution.py:332
  1081.1 45.3 %all-to-all-done.2 = bf16[4,640,512]{2,1,0:T(8,128)(2,1)} async-done(((bf16[4,640,512]{2,1,0:T(8,128)(2,1)}), bf16[4,640,512]{2,1,0:T(8,128)(2,1)}, u32[]{:S(2)}, u32[]{:S(2)}) %all-to-all-start.2) | async-done | bytes 2621472 | tf_op jit(solution)/shard_map/all_to_all | solution.py:1180
  1141.1 23.6 %collective-permute-done.54 = bf16[512,1024]{1,0:T(8,128)(2,1)S(1)} collective-permute-done((bf16[512,1024]{1,0:T(8,128)(2,1)S(1)}, bf16[512,1024]{1,0:T(8,128)(2,1)S(1)}, u32[]{:S(2)}, u32[]{:S(2)}) %collective-permute-start.54) | collective-permute-done | bytes 1048608 | tf_op jit(solution)/shard_map/ppermute | solution.py:332
  1176.2 35.8 %collective-permute-done.58.refs_2_ = bf16[2,512,1024]{2,1,0:T(8,128)(2,1)} collective-permute-done((bf16[2,512,1024]{2,1,0:T(8,128)(2,1)S(1)}, bf16[2,512,1024]{2,1,0:T(8,128)(2,1)}, u32[]{:S(2)}, u32[]{:S(2)}) %collective-permute-start.58) | collective-permute-done | bytes 2097184 | tf_op jit(solution)/shard_map/ppermute | solution.py:328
  1213.5 12.8 collective-permute-done.53
  1239.1 12.4 collective-permute-done.56.refs_2_
  (447 shorter events, 409.6 us)
Async XLA Ops:
  54.9 98.2 %all-to-all-start = ((bf16[4,640,512]{2,1,0:T(8,128)(2,1)}), bf16[4,640,512]{2,1,0:T(8,128)(2,1)S(1)}, u32[]{:S(2)}, u32[]{:S(2)}) async-start(bf16[4,640,512]{2,1,0:T(8,128)(2,1)} %bitcast.204), calls=%async_computation | async-start | bytes 5242880 | tf_op jit(solution)/shard_map/all_to_all | solution.py:959
  59.8 82.1 %all-gather.14.cloned.1.call-start = ((), (), s32[]{:S(2)}) async-start(), calls=%async_computation.15 | async-start | bytes 2621440 | tf_op jit(solution)/shard_map/all_gather | solution.py:970
  62.3 156.1 %all-gather.16.cloned.1.call-start = ((), (), s32[]{:S(2)}) async-start(), calls=%async_computation.16 | async-start | bytes 1310720 | tf_op jit(solution)/shard_map/all_gather | solution.py:1015
  153.2 148.2 %all-gather.8.cloned.1.call-start = ((), (), s32[]{:S(2)}) async-start(), calls=%async_computation.8 | async-start | bytes 5242880 | tf_op jit(solution)/shard_map/all_gather | solution.py:1016
  155.5 75.9 %collective-permute-start.7 = (bf16[2560,512]{1,0:T(8,128)(2,1)S(1)}, bf16[2560,512]{1,0:T(8,128)(2,1)}, u32[]{:S(2)}, u32[]{:S(2)}) collective-permute-start(bf16[2560,512]{1,0:T(8,128)(2,1)S(1)} %bitcast.191), channel_id=1, source_target_pairs={{0,8},{8,0},{16,24},{24,16},{1,9},{9,1},{17,25},{25,17},{2,10},{10... | collective-permute-start | bytes 7864328 | tf_op jit(solution)/shard_map/ppermute | solution.py:324
  226.8 96.5 %all-to-all-start.1 = ((bf16[4,640,512]{2,1,0:T(8,128)(2,1)}), bf16[4,640,512]{2,1,0:T(8,128)(2,1)}, u32[]{:S(2)}, u32[]{:S(2)}) async-start(bf16[4,640,512]{2,1,0:T(8,128)(2,1)} %bitcast.205), calls=%async_computation.1 | async-start | bytes 5242880 | tf_op jit(solution)/shard_map/all_to_all | solution.py:1055
  231.4 159.8 %all-gather.10.cloned.1.call-start = ((), (), s32[]{:S(2)}) async-start(), calls=%async_computation.9 | async-start | bytes 5242880 | tf_op jit(solution)/shard_map/all_gather | solution.py:1017
  300.7 169.5 %all-gather.12.cloned.1.call-start = ((), (), s32[]{:S(2)}) async-start(), calls=%async_computation.10 | async-start | bytes 5242880 | tf_op jit(solution)/shard_map/all_gather | solution.py:1018
  328.4 69.7 %collective-permute-start.20 = (bf16[768,2048]{1,0:T(8,128)(2,1)}, bf16[768,2048]{1,0:T(8,128)(2,1)}, u32[]{:S(2)}, u32[]{:S(2)}) collective-permute-start(bf16[768,2048]{1,0:T(8,128)(2,1)} %next_blocks.3), channel_id=1, source_target_pairs={{0,16},{16,0},{8,24},{24,8},{1,17},{17,1},{9,25},{25,9},{2,18},{18... | collective-permute-start | bytes 9437192 | tf_op jit(solution)/shard_map/ppermute | solution.py:328
  391.1 681.6 %reduce-scatter.5.cloned.1.call-start = ((), (), s32[]{:S(2)}) async-start(), calls=%async_computation.11 | async-start | bytes 5242880 | tf_op jit(solution)/shard_map/reduce_scatter | solution.py:1097
  398.1 59.0 %collective-permute-start.21 = (bf16[2560,512]{1,0:T(8,128)(2,1)}, bf16[2560,512]{1,0:T(8,128)(2,1)S(1)}, u32[]{:S(2)}, u32[]{:S(2)}) collective-permute-start(bf16[2560,512]{1,0:T(8,128)(2,1)} %multiply_convert_fusion.refs_0_.refs_1_), channel_id=1, source_target_pairs={{0,1},{1,0},{2,3},{3,2},{4,5},{5,4},{6,7},{7,6},{8,9},{9,8},{10,11... | collective-permute-start | bytes 7864328 | tf_op jit(solution)/shard_map/ppermute | solution.py:332
  398.5 77.6 %collective-permute-start.26 = (bf16[768,2048]{1,0:T(8,128)(2,1)}, bf16[768,2048]{1,0:T(8,128)(2,1)}, u32[]{:S(2)}, u32[]{:S(2)}) collective-permute-start(bf16[768,2048]{1,0:T(8,128)(2,1)} %next_blocks.4), channel_id=1, source_target_pairs={{0,16},{16,0},{8,24},{24,8},{1,17},{17,1},{9,25},{25,9},{2,18},{18... | collective-permute-start | bytes 9437192 | tf_op jit(solution)/shard_map/ppermute | solution.py:328
  457.6 71.6 %collective-permute-start.22 = (bf16[2560,512]{1,0:T(8,128)(2,1)}, bf16[2560,512]{1,0:T(8,128)(2,1)}, u32[]{:S(2)}, u32[]{:S(2)}) collective-permute-start(bf16[2560,512]{1,0:T(8,128)(2,1)} %bitcast.39.refs_0_.refs_1_), channel_id=1, source_target_pairs={{0,1},{1,0},{2,3},{3,2},{4,5},{5,4},{6,7},{7,6},{8,9},{9,8},{10,11... | collective-permute-start | bytes 7864328 | tf_op jit(solution)/shard_map/ppermute | solution.py:332
  474.6 70.2 %collective-permute-start.28 = (bf16[768,2048]{1,0:T(8,128)(2,1)}, bf16[768,2048]{1,0:T(8,128)(2,1)}, u32[]{:S(2)}, u32[]{:S(2)}) collective-permute-start(bf16[768,2048]{1,0:T(8,128)(2,1)} %next_blocks.5), channel_id=1, source_target_pairs={{0,16},{16,0},{8,24},{24,8},{1,17},{17,1},{9,25},{25,9},{2,18},{18... | collective-permute-start | bytes 9437192 | tf_op jit(solution)/shard_map/ppermute | solution.py:328
  476.1 68.7 %collective-permute-start.24 = (bf16[2560,512]{1,0:T(8,128)(2,1)}, bf16[2560,512]{1,0:T(8,128)(2,1)S(1)}, u32[]{:S(2)}, u32[]{:S(2)}) collective-permute-start(bf16[2560,512]{1,0:T(8,128)(2,1)} %bitcast.39.refs_0_.refs_1_), channel_id=1, source_target_pairs={{0,8},{8,0},{16,24},{24,16},{1,9},{9,1},{17,25},{25,17},{2,10},{10... | collective-permute-start | bytes 7864328 | tf_op jit(solution)/shard_map/ppermute | solution.py:324
  654.5 93.6 %collective-permute-start.30 = (bf16[1024,2048]{1,0:T(8,128)(2,1)}, bf16[1024,2048]{1,0:T(8,128)(2,1)S(1)}, u32[]{:S(2)}, u32[]{:S(2)}) collective-permute-start(bf16[1024,2048]{1,0:T(8,128)(2,1)} %down_grad_other.1), channel_id=1, source_target_pairs={{0,16},{16,0},{8,24},{24,8},{1,17},{17,1},{9,25},{25,9},{2,18},{18... | collective-permute-start | bytes 12582920 | tf_op jit(solution)/shard_map/ppermute | solution.py:328
  690.7 96.2 %collective-permute-start.31 = (bf16[2560,512]{1,0:T(8,128)(2,1)}, bf16[2560,512]{1,0:T(8,128)(2,1)}, u32[]{:S(2)}, u32[]{:S(2)}) collective-permute-start(bf16[2560,512]{1,0:T(8,128)(2,1)} %get-tuple-element.154), channel_id=1, source_target_pairs={{0,8},{8,0},{16,24},{24,16},{1,9},{9,1},{17,25},{25,17},{2,10},{10... | collective-permute-start | bytes 7864328 | tf_op jit(solution)/shard_map/ppermute | solution.py:324
  695.8 91.1 %collective-permute-start.32 = (bf16[2560,512]{1,0:T(8,128)(2,1)}, bf16[2560,512]{1,0:T(8,128)(2,1)}, u32[]{:S(2)}, u32[]{:S(2)}) collective-permute-start(bf16[2560,512]{1,0:T(8,128)(2,1)} %add_convert_fusion.7), channel_id=1, source_target_pairs={{0,1},{1,0},{2,3},{3,2},{4,5},{5,4},{6,7},{7,6},{8,9},{9,8},{10,11... | collective-permute-start | bytes 7864328 | tf_op jit(solution)/shard_map/ppermute | solution.py:332
  697.3 140.3 %collective-permute-start.37 = (bf16[1024,2048]{1,0:T(8,128)(2,1)}, bf16[1024,2048]{1,0:T(8,128)(2,1)}, u32[]{:S(2)}, u32[]{:S(2)}) collective-permute-start(bf16[1024,2048]{1,0:T(8,128)(2,1)} %gate_grad_other.1), channel_id=1, source_target_pairs={{0,16},{16,0},{8,24},{24,8},{1,17},{17,1},{9,25},{25,9},{2,18},{18... | collective-permute-start | bytes 12582920 | tf_op jit(solution)/shard_map/ppermute | solution.py:328
  752.0 323.0 %reduce-scatter.7.cloned.1.call-start = ((), (), s32[]{:S(2)}) async-start(), calls=%async_computation.12 | async-start | bytes 5242880 | tf_op jit(solution)/shard_map/reduce_scatter | solution.py:1097
  804.5 67.1 %collective-permute-start.36 = (bf16[2560,512]{1,0:T(8,128)(2,1)}, bf16[2560,512]{1,0:T(8,128)(2,1)}, u32[]{:S(2)}, u32[]{:S(2)}) collective-permute-start(bf16[2560,512]{1,0:T(8,128)(2,1)} %get-tuple-element.175.h0.refs_1_), channel_id=1, source_target_pairs={{0,1},{1,0},{2,3},{3,2},{4,5},{5,4},{6,7},{7,6},{8,9},{9,8},{10,11... | collective-permute-start | bytes 7864328 | tf_op jit(solution)/shard_map/ppermute | solution.py:332
  805.7 68.0 %collective-permute-start.38 = (bf16[2560,512]{1,0:T(8,128)(2,1)}, bf16[2560,512]{1,0:T(8,128)(2,1)}, u32[]{:S(2)}, u32[]{:S(2)}) collective-permute-start(bf16[2560,512]{1,0:T(8,128)(2,1)} %get-tuple-element.175.h0.refs_1_), channel_id=1, source_target_pairs={{0,8},{8,0},{16,24},{24,16},{1,9},{9,1},{17,25},{25,17},{2,10},{10... | collective-permute-start | bytes 7864328 | tf_op jit(solution)/shard_map/ppermute | solution.py:324
  872.2 92.9 %collective-permute-start.43 = (bf16[1024,2048]{1,0:T(8,128)(2,1)}, bf16[1024,2048]{1,0:T(8,128)(2,1)}, u32[]{:S(2)}, u32[]{:S(2)}) collective-permute-start(bf16[1024,2048]{1,0:T(8,128)(2,1)} %up_grad_other.1), channel_id=1, source_target_pairs={{0,16},{16,0},{8,24},{24,8},{1,17},{17,1},{9,25},{25,9},{2,18},{18... | collective-permute-start | bytes 12582920 | tf_op jit(solution)/shard_map/ppermute | solution.py:328
  873.7 79.6 %collective-permute-start.41 = (bf16[2560,512]{1,0:T(8,128)(2,1)}, bf16[2560,512]{1,0:T(8,128)(2,1)}, u32[]{:S(2)}, u32[]{:S(2)}) collective-permute-start(bf16[2560,512]{1,0:T(8,128)(2,1)} %get-tuple-element.166), channel_id=1, source_target_pairs={{0,8},{8,0},{16,24},{24,16},{1,9},{9,1},{17,25},{25,17},{2,10},{10... | collective-permute-start | bytes 7864328 | tf_op jit(solution)/shard_map/ppermute | solution.py:324
  895.7 59.2 %collective-permute-start.42 = (bf16[2560,512]{1,0:T(8,128)(2,1)}, bf16[2560,512]{1,0:T(8,128)(2,1)}, u32[]{:S(2)}, u32[]{:S(2)}) collective-permute-start(bf16[2560,512]{1,0:T(8,128)(2,1)} %add_convert_fusion.6), channel_id=1, source_target_pairs={{0,1},{1,0},{2,3},{3,2},{4,5},{5,4},{6,7},{7,6},{8,9},{9,8},{10,11... | collective-permute-start | bytes 7864328 | tf_op jit(solution)/shard_map/ppermute | solution.py:332
  897.2 277.7 %reduce-scatter.9.cloned.1.call-start = ((), (), s32[]{:S(2)}) async-start(), calls=%async_computation.13 | async-start | bytes 5242880 | tf_op jit(solution)/shard_map/reduce_scatter | solution.py:1097
  999.1 59.2 %collective-permute-start.46 = (bf16[2560,512]{1,0:T(8,128)(2,1)}, bf16[2560,512]{1,0:T(8,128)(2,1)}, u32[]{:S(2)}, u32[]{:S(2)}) collective-permute-start(bf16[2560,512]{1,0:T(8,128)(2,1)} %add_convert_fusion.4), channel_id=1, source_target_pairs={{0,1},{1,0},{2,3},{3,2},{4,5},{5,4},{6,7},{7,6},{8,9},{9,8},{10,11... | collective-permute-start | bytes 7864328 | tf_op jit(solution)/shard_map/ppermute | solution.py:332
  1001.7 124.7 %all-to-all-start.2 = ((bf16[4,640,512]{2,1,0:T(8,128)(2,1)}), bf16[4,640,512]{2,1,0:T(8,128)(2,1)}, u32[]{:S(2)}, u32[]{:S(2)}) async-start(bf16[4,640,512]{2,1,0:T(8,128)(2,1)} %bitcast.41), calls=%async_computation.2 | async-start | bytes 5242880 | tf_op jit(solution)/shard_map/all_to_all | solution.py:1180
  1006.5 221.5 %reduce-scatter.11.cloned.1.call-start = ((), (), s32[]{:S(2)}) async-start(), calls=%async_computation.14 | async-start | bytes 3932160 | tf_op jit(solution)/shard_map/reduce_scatter | solution.py:1216
  1037.8 92.0 %collective-permute-start.50 = (bf16[2,2,2,384,512]{4,3,2,1,0:T(8,128)(2,1)}, bf16[2,2,2,384,512]{4,3,2,1,0:T(8,128)(2,1)}, u32[]{:S(2)}, u32[]{:S(2)}) collective-permute-start(bf16[2,2,2,384,512]{4,3,2,1,0:T(8,128)(2,1)} %pad_maximum_fusion), channel_id=1, source_target_pairs={{0,16},{16,0},{8,24},{24,8},{1,17},{17,1},{9,25},{25,9},{2,18},{18... | collective-permute-start | bytes 9437192 | tf_op jit(solution)/shard_map/ppermute | solution.py:328
  1166.4 97.5 %all-to-all-start.3 = ((bf16[4,640,512]{2,1,0:T(8,128)(2,1)}), bf16[4,640,512]{2,1,0:T(8,128)(2,1)}, u32[]{:S(2)}, u32[]{:S(2)}) async-start(bf16[4,640,512]{2,1,0:T(8,128)(2,1)} %bitcast.203), calls=%async_computation.5 | async-start | bytes 5242880 | tf_op jit(solution)/shard_map/all_to_all | solution.py:1208
  1171.3 59.8 %collective-permute-start.57 = (bf16[2,512,1024]{2,1,0:T(8,128)(2,1)S(1)}, bf16[2,512,1024]{2,1,0:T(8,128)(2,1)}, u32[]{:S(2)}, u32[]{:S(2)}) collective-permute-start(bf16[2,512,1024]{2,1,0:T(8,128)(2,1)S(1)} %pad_maximum_fusion.6.refs_0_), channel_id=1, source_target_pairs={{0,8},{8,0},{16,24},{24,16},{1,9},{9,1},{17,25},{25,17},{2,10},{10... | collective-permute-start | bytes 6291464 | tf_op jit(solution)/shard_map/ppermute | solution.py:324
  (113 other events, 1907.9 us)
Sparse Core Ops, SparseCore 0:
  62.7 79.0 all-gather.13
  153.3 28.3 all-gather.15
  183.9 108.5 all-gather.7
  300.8 87.2 all-gather.9
  391.3 78.8 all-gather.11
  752.1 75.3 reduce-scatter.4
  897.4 74.4 reduce-scatter.6
  1000.7 120.6 reduce-scatter.8
  1138.4 85.5 reduce-scatter.10

commit v4 on v3

--- a/solution.py
+++ b/solution.py
@@ -1210,21 +1210,24 @@
         jnp.concatenate([after(down_sum, input_low), gate_sum])
     )
     output, output_sent = of_core(after(output_tree, home_sent))
-    attn_total = low(wide(after(attn_kept, output_sent)) + wide(swap_x(attn_sent)))
+    home_both = jnp.stack([home_kept, after(swap_col(home_sent), output_sent)])
+    home_over = swap_x(home_both)
+    attn_total = low(wide(after(attn_kept, home_both)) + wide(swap_x(attn_sent)))
     by_plane = in_order(c, attn_total[:, 0], swap_core(attn_total[:, 1]))
     by_plane = by_plane.reshape((planes,) + by_plane.shape[2:])
     attn_sum = lax.psum_scatter(by_plane, "row", scatter_dimension=0, tiled=False)
     output = by_feature(after(output, by_plane), output_sent)
     up_kept, up_sent = unit_halves(after(up_sum, output))
-    home_parts = unit_parts(home_kept, home_sent, attn_total, up_sent)
+    home_over = after(home_over, up_sent)
+    home_parts = [home_both, swap_core(home_both), home_over, swap_core(home_over)]
     down_out = ffn_home(where, home_parts, 0, unit, False, "down_home")
     gate_out = ffn_home(where, home_parts, 1, unit, True, "gate_home")
-    up_parts = unit_parts(up_kept, up_sent, home_parts[0], gate_out)
+    attn_sum = after(attn_sum, down_out, gate_out)
+    home = in_order(y, attn_sum[0], swap_col(attn_sum[1]))
+    up_parts = unit_parts(up_kept, up_sent, gate_out, home)
     up_out = ffn_home(where, up_parts, 0, unit, True, "up_home")
+    home = in_order(x, home, after(swap_x(home), up_out))
     input_grad = by_feature(*of_core(after(input_tree, up_out)))
-
-    home = in_order(y, attn_sum[0], swap_col(attn_sum[1]))
-    home = in_order(x, home, swap_x(home))
     home = in_order(c, home, swap_core(home))
     mix_home = home[:, :, :, share:]
     out_out = wide(jnp.transpose(mix_home, (2, 1, 3, 0, 4)).reshape(groups * 2 * HEAD, half))

time: 1330 us -> 1310 us (0.985)
  waiting for transfers between devices: 537 us -> 515 us
    ppermute x18, waiting for transfers between devices: 256 us -> 230 us  [swap_col(): return lax.ppermute(a, 'col', COL_SWAP)]
  transfers between devices with their start and end apart: 82 -> 82, of which waited for: 33 -> 36; matrix products, arithmetic and copies ran while one was open for 14% -> 15% of each run, Pallas kernels for 29% -> 29%
where the time goes in v4:
time: 1310 us; the launch traced here: 1300 us
  waiting for transfers between devices  515 us (39%)
  Pallas kernels  484 us (37%)
  other arithmetic  143 us (11%)
  local copies, waits for them, and re-layouts  74.2 us (6%)
  starting transfers between devices  70.7 us (5%)
  between operations  15.2 us (1%)
    ppermute x18, waiting for transfers between devices, swap_col(): return lax.ppermute(a, 'col', COL_SWAP)  230 us
    pallas_call x8, Pallas kernels, rows_call(): pl.pallas_call(fn, grid=(rows // block,), in_specs=in_specs, out_specs=[p...  226 us
    ppermute x13, waiting for transfers between devices, swap_x(): return lax.ppermute(a, 'dp', X_SWAP)  140 us
    pallas_call x5, Pallas kernels, weight_grad(): pl.pallas_call(functools.partial(weight_grad_kernel, len(bs), split), gri...  79.7 us
    convert_element_type x12, other arithmetic, low(): return a.astype(jnp.bfloat16)  61.4 us
    pallas_call x1, Pallas kernels, attend_back(): pl.pallas_call(functools.partial(attend_back_kernel, trunk, leaf_begin, b...  55.6 us
    pallas_call x3, Pallas kernels, turned_grad(): pl.pallas_call(functools.partial(turned_grad_kernel, len(bs)), grid_spec=...  51.5 us
    all_to_all x1, waiting for transfers between devices, tree_body(): output_tree = lax.all_to_all(output, 'row', 0, 0, tiled=True)  44.8 us
  transfers between devices with their start and end apart: 82, of which 36 were waited for; matrix products, arithmetic and copies ran while one was open for 15% of the time, Pallas kernels for 29%

profile of v4, /device:TPU:0, one launch (start us, length us, event | category | flops | bytes accessed | tf_op | source)
XLA Modules:
  0.0 1301.3 jit_solution(10353821927717033626)
XLA Ops:
  62.3 13.0 %collective-permute-done.2 = bf16[896,1024]{1,0:T(8,128)(2,1)} collective-permute-done((bf16[896,1024]{1,0:T(8,128)(2,1)}, bf16[896,1024]{1,0:T(8,128)(2,1)}, u32[]{:S(2)}, u32[]{:S(2)}) %collective-permute-start.2) | collective-permute-done | bytes 1835040 | tf_op jit(solution)/shard_map/ppermute | solution.py:332
  95.0 18.0 %collective-permute-done.3 = bf16[768,1024]{1,0:T(8,128)(2,1)} collective-permute-done((bf16[768,1024]{1,0:T(8,128)(2,1)}, bf16[768,1024]{1,0:T(8,128)(2,1)}, u32[]{:S(2)}, u32[]{:S(2)}) %collective-permute-start.3) | collective-permute-done | bytes 1572896 | tf_op jit(solution)/shard_map/ppermute | solution.py:332
  117.9 23.9 %all-gather.14.cloned.1.call-done = bf16[8,256,512]{2,1,0:T(8,128)(2,1)} async-done(((bf16[2,256,512]{2,1,0:T(8,128)(2,1)}), bf16[8,256,512]{2,1,0:T(8,128)(2,1)}) %all-gather.14.cloned.1.call-update) | async-done | bytes 2097168 | tf_op jit(solution)/shard_map/all_gather | solution.py:970
  141.8 11.3 all-to-all-done
  155.8 55.8 %collective-permute-done.6.x1 = bf16[2560,512]{1,0:T(8,128)(2,1)} collective-permute-done((bf16[2560,512]{1,0:T(8,128)(2,1)S(1)}, bf16[2560,512]{1,0:T(8,128)(2,1)}, u32[]{:S(2)}, u32[]{:S(2)}) %collective-permute-start.6) | collective-permute-done | bytes 2621472 | tf_op jit(solution)/shard_map/ppermute | solution.py:332
  231.7 20.3 %project.1 = (bf16[2560,2048]{1,0:T(8,128)(2,1)}, bf16[2560,1024]{1,0:T(8,128)(2,1)}, f32[2560,1]{1,0:T(8,128)}) custom-call(bf16[2560,512]{1,0:T(8,128)(2,1)} %bitcast.194, bf16[2560,512]{1,0:T(8,128)(2,1)} %collective-permute-done.6.x1, bf16[2560,512]{1,0:T(8,128)(2,1)} %collective-permute-done.7.x2, bf16[2560,512]{1,0:T(8,128)(2,1)} %collective-permute-done.8.x3, ...), custom_call_target="tpu_custom_call" | custom-call | flops 1342177280 | bytes 4131072 | tf_op jit(solution)/shard_map/project/pallas_call | solution.py:372
  256.4 34.4 %attend.1 = (bf16[2560,512]{1,0:T(8,128)(2,1)}, f32[2,10,1,512]{3,2,1,0:T(1,128)}) custom-call(bf16[2560,1024]{1,0:T(8,128)(2,1)} %get-tuple-element.111.q_ref.k_ref.v_ref, bf16[2560,1024]{1,0:T(8,128)(2,1)} %get-tuple-element.111.q_ref.k_ref.v_ref, bf16[2560,1024]{1,0:T(8,128)(2,1)} %get-tuple-element.111.q_ref.k_ref.v_ref, s32[2560,1]{1,0:T(8,128)} %copy.90.lab_ref, ...), custom_call_target="tpu_custom_call" | custom-call | flops 3355443200 | bytes 1638400 | tf_op jit(solution)/shard_map/attend/pallas_call | solution.py:585
  305.9 17.6 %all-to-all-done.1 = bf16[4,640,512]{2,1,0:T(8,128)(2,1)} async-done(((bf16[4,640,512]{2,1,0:T(8,128)(2,1)}), bf16[4,640,512]{2,1,0:T(8,128)(2,1)}, u32[]{:S(2)}, u32[]{:S(2)}) %all-to-all-start.1) | async-done | bytes 2621472 | tf_op jit(solution)/shard_map/all_to_all | solution.py:1055
  330.1 55.5 %collective-permute-done.16 = bf16[2560,512]{1,0:T(8,128)(2,1)S(1)} collective-permute-done((bf16[2560,512]{1,0:T(8,128)(2,1)S(1)}, bf16[2560,512]{1,0:T(8,128)(2,1)S(1)}, u32[]{:S(2)}, u32[]{:S(2)}) %collective-permute-start.16) | collective-permute-done | bytes 2621472 | tf_op jit(solution)/shard_map/ppermute | solution.py:332
  401.1 56.2 %collective-permute-done.21.refs_1_.refs_2_ = bf16[2560,512]{1,0:T(8,128)(2,1)S(1)} collective-permute-done((bf16[2560,512]{1,0:T(8,128)(2,1)}, bf16[2560,512]{1,0:T(8,128)(2,1)S(1)}, u32[]{:S(2)}, u32[]{:S(2)}) %collective-permute-start.21) | collective-permute-done | bytes 2621472 | tf_op jit(solution)/shard_map/ppermute | solution.py:332
  459.2 11.3 all-gather.12.cloned.1.call-done.in_ref.refs_8_.refs_2_
  476.4 53.0 %gate_up.1 = (bf16[2560,1024]{1,0:T(8,128)(2,1)}, bf16[2560,1024]{1,0:T(8,128)(2,1)}, bf16[2560,1024]{1,0:T(8,128)(2,1)}, bf16[2560,1024]{1,0:T(8,128)(2,1)}) custom-call(bf16[2560,512]{1,0:T(8,128)(2,1)} %multiply_convert_fusion.refs_0_.refs_1_, bf16[2560,512]{1,0:T(8,128)(2,1)} %copy-done.4, bf16[2560,512]{1,0:T(8,128)(2,1)} %collective-permute-done.25.refs_2_.refs_3_, ...), custom_call_target="tpu_custom_call" | custom-call | flops 5368709120 | bytes 6029312 | tf_op jit(solution)/shard_map/gate_up/pallas_call | solution.py:372
  530.0 15.1 %collective-permute-done.28.refs_10_.refs_4_ = bf16[768,2048]{1,0:T(8,128)(2,1)} collective-permute-done((bf16[768,2048]{1,0:T(8,128)(2,1)}, bf16[768,2048]{1,0:T(8,128)(2,1)}, u32[]{:S(2)}, u32[]{:S(2)}) %collective-permute-start.28) | collective-permute-done | bytes 3145760 | tf_op jit(solution)/shard_map/ppermute | solution.py:328
  547.4 37.0 %hidden.1 = (bf16[2560,1024]{1,0:T(8,128)(2,1)}, bf16[2560,1024]{1,0:T(8,128)(2,1)}, bf16[2560,1024]{1,0:T(8,128)(2,1)}, bf16[2560,1024]{1,0:T(8,128)(2,1)}, bf1...) custom-call(bf16[2560,512]{1,0:T(8,128)(2,1)} %bitcast.39.refs_0_.refs_1_, ...), custom_call_target="tpu_custom_call" | custom-call | flops 2684354560 | bytes 8912896 | tf_op jit(solution)/shard_map/hidden/pallas_call | solution.py:372
  584.3 17.1 %down_grad_other.1 = bf16[1024,2048]{1,0:T(8,128)(2,1)} custom-call(s32[1]{0:T(128)} %bitcast.40.where_ref, bf16[2560,1024]{1,0:T(8,128)(2,1)} %get-tuple-element.140.refs_0_.refs_1_, bf16[2560,512]{1,0:T(8,128)(2,1)} %bitcast.39.refs_0_.refs_1_, bf16[2560,512]{1,0:T(8,128)(2,1)} %collective-permute-done.22.refs_1_.refs_2_, bf16[2560,512]{1,0:T(8,128)(2,1)} %copy-done.5, ...), custom_call_target="tpu_custom_call" | custom-call | flops 1342177280 | bytes 2490368 | tf_op jit(solution)/shard_map/down_grad_other/pallas_call | solution.py:761
  601.5 52.8 %pair_back.1 = (bf16[2560,512]{1,0:T(8,128)(2,1)}, bf16[2560,512]{1,0:T(8,128)(2,1)}, bf16[2560,512]{1,0:T(8,128)(2,1)}, bf16[2560,512]{1,0:T(8,128)(2,1)}) custom-call(bf16[2560,1024]{1,0:T(8,128)(2,1)} %get-tuple-element.154.refs_0_, bf16[2560,1024]{1,0:T(8,128)(2,1)} %get-tuple-element.157.refs_1_.refs_0_, ...), custom_call_target="tpu_custom_call" | custom-call | flops 5368709120 | bytes 6029312 | tf_op jit(solution)/shard_map/pair_back/pallas_call | solution.py:372
  655.9 17.1 %gate_grad_other.1 = bf16[1024,2048]{1,0:T(8,128)(2,1)} custom-call(s32[1]{0:T(128)} %bitcast.40.where_ref, bf16[2560,1024]{1,0:T(8,128)(2,1)} %get-tuple-element.147.refs_2_.refs_0_, bf16[2560,512]{1,0:T(8,128)(2,1)} %multiply_convert_fusion.refs_0_.refs_1_, bf16[2560,512]{1,0:T(8,128)(2,1)} %copy-done.4, ...), custom_call_target="tpu_custom_call" | custom-call | flops 1342177280 | bytes 2490368 | tf_op jit(solution)/shard_map/gate_grad_other/pallas_call | solution.py:761
  673.0 17.7 %down_grad_mine.1 = bf16[1024,2048]{1,0:T(8,128)(2,1)} custom-call(bf16[2560,1024]{1,0:T(8,128)(2,1)} %get-tuple-element.159.refs_0_, bf16[2560,512]{1,0:T(8,128)(2,1)} %bitcast.39.refs_0_.refs_1_, bf16[2560,512]{1,0:T(8,128)(2,1)} %collective-permute-done.22.refs_1_.refs_2_, bf16[2560,512]{1,0:T(8,128)(2,1)} %copy-done.5, bf16[2560,512]{1,0:T(8,128)(2,1)} %copy-done.6), custom_call_target="tpu_custom_call" | custom-call | flops 1342177280 | bytes 2490368 | tf_op jit(solution)/shard_map/down_grad_mine/pallas_call | solution.py:848
  697.9 50.1 %collective-permute-done.30 = bf16[1024,2048]{1,0:T(8,128)(2,1)S(1)} collective-permute-done((bf16[1024,2048]{1,0:T(8,128)(2,1)}, bf16[1024,2048]{1,0:T(8,128)(2,1)S(1)}, u32[]{:S(2)}, u32[]{:S(2)}) %collective-permute-start.30) | collective-permute-done | bytes 4194336 | tf_op jit(solution)/shard_map/ppermute | solution.py:328
  751.9 17.2 %up_grad_other.1 = bf16[1024,2048]{1,0:T(8,128)(2,1)} custom-call(s32[1]{0:T(128)} %bitcast.40.where_ref, bf16[2560,1024]{1,0:T(8,128)(2,1)} %get-tuple-element.153.refs_3_.refs_0_, bf16[2560,512]{1,0:T(8,128)(2,1)} %multiply_convert_fusion.refs_0_.refs_1_, bf16[2560,512]{1,0:T(8,128)(2,1)} %copy-done.4, ...), custom_call_target="tpu_custom_call" | custom-call | flops 1342177280 | bytes 2490368 | tf_op jit(solution)/shard_map/up_grad_other/pallas_call | solution.py:761
  769.2 17.4 %gate_grad_mine.1 = bf16[1024,2048]{1,0:T(8,128)(2,1)} custom-call(bf16[2560,1024]{1,0:T(8,128)(2,1)} %get-tuple-element.154.refs_0_, bf16[2560,512]{1,0:T(8,128)(2,1)} %multiply_convert_fusion.refs_0_.refs_1_, bf16[2560,512]{1,0:T(8,128)(2,1)} %copy-done.4, bf16[2560,512]{1,0:T(8,128)(2,1)} %collective-permute-done.25.refs_2_.refs_3_, ...), custom_call_target="tpu_custom_call" | custom-call | flops 1342177280 | bytes 2490368 | tf_op jit(solution)/shard_map/gate_grad_mine/pallas_call | solution.py:848
  806.7 17.4 %up_grad_mine.1 = bf16[1024,2048]{1,0:T(8,128)(2,1)} custom-call(bf16[2560,1024]{1,0:T(8,128)(2,1)} %get-tuple-element.157.refs_1_.refs_0_, bf16[2560,512]{1,0:T(8,128)(2,1)} %multiply_convert_fusion.refs_0_.refs_1_, bf16[2560,512]{1,0:T(8,128)(2,1)} %copy-done.4, bf16[2560,512]{1,0:T(8,128)(2,1)} %collective-permute-done.25.refs_2_.refs_3_, ...), custom_call_target="tpu_custom_call" | custom-call | flops 1342177280 | bytes 2490368 | tf_op jit(solution)/shard_map/up_grad_mine/pallas_call | solution.py:848
  824.1 13.4 %collective-permute-done.37 = bf16[1024,2048]{1,0:T(8,128)(2,1)} collective-permute-done((bf16[1024,2048]{1,0:T(8,128)(2,1)}, bf16[1024,2048]{1,0:T(8,128)(2,1)}, u32[]{:S(2)}, u32[]{:S(2)}) %collective-permute-start.37) | collective-permute-done | bytes 4194336 | tf_op jit(solution)/shard_map/ppermute | solution.py:328
  845.3 27.6 %down.1 = (bf16[2560,512]{1,0:T(8,128)(2,1)}, bf16[2560,512]{1,0:T(8,128)(2,1)}, bf16[2560,512]{1,0:T(8,128)(2,1)}, bf16[2560,512]{1,0:T(8,128)(2,1)}) custom-call(bf16[2560,1024]{1,0:T(8,128)(2,1)} %get-tuple-element.159.refs_0_, bf16[2560,1024]{1,0:T(8,128)(2,1)} %get-tuple-element.140.refs_0_.refs_1_, ...), custom_call_target="tpu_custom_call" | custom-call | flops 2684354560 | bytes 3670016 | tf_op jit(solution)/shard_map/down/pallas_call | solution.py:372
  882.7 10.4 attn_grad.1.do_ref
  899.5 55.6 %attend_back.1.d_ref.refs_1_ = bf16[2560,1024]{1,0:T(8,128)(2,1)} custom-call(bf16[2560,1024]{1,0:T(8,128)(2,1)} %get-tuple-element.111.q_ref.k_ref.v_ref, bf16[2560,1024]{1,0:T(8,128)(2,1)} %get-tuple-element.111.q_ref.k_ref.v_ref, bf16[2560,1024]{1,0:T(8,128)(2,1)} %get-tuple-element.111.q_ref.k_ref.v_ref, ...), custom_call_target="tpu_custom_call" | custom-call | flops 8388608000 | bytes 3276800 | tf_op jit(solution)/shard_map/attend_back/pallas_call | solution.py:608
  972.5 15.9 %project_back.1 = (bf16[2560,512]{1,0:T(8,128)(2,1)}, bf16[2560,512]{1,0:T(8,128)(2,1)}, bf16[2560,512]{1,0:T(8,128)(2,1)}, bf16[2560,512]{1,0:T(8,128)(2,1)}) custom-call(bf16[2560,1024]{1,0:T(8,128)(2,1)} %attend_back.1.d_ref.refs_1_, bf16[2,1024,512]{2,1,0:T(8,128)(2,1)} %bitcast.201, bf16[2,1024,512]{2,1,0:T(8,128)(2,1)} %bitcast.29.far_ref), custom_call_target="tpu_custom_call" | custom-call | flops 1342177280 | bytes 2490368 | tf_op jit(solution)/shard_map/project_back/pallas_call | solution.py:372
  1007.8 15.9 %project_grad.1 = bf16[2,2048,512]{2,1,0:T(8,128)(2,1)} custom-call(bf16[2560,2048]{1,0:T(8,128)(2,1)} %get-tuple-element.173.refs_0_, bf16[2560,1024]{1,0:T(8,128)(2,1)} %attend_back.1.d_ref.refs_1_), custom_call_target="tpu_custom_call" | custom-call | flops 1342177280 | bytes 2490368 | tf_op jit(solution)/shard_map/project_grad/pallas_call | solution.py:848
  1023.8 11.2 mix_grad.1
  1045.8 14.2 %collective-permute-done.46 = bf16[2560,512]{1,0:T(8,128)(2,1)} collective-permute-done((bf16[2560,512]{1,0:T(8,128)(2,1)}, bf16[2560,512]{1,0:T(8,128)(2,1)}, u32[]{:S(2)}, u32[]{:S(2)}) %collective-permute-start.46) | collective-permute-done | bytes 2621472 | tf_op jit(solution)/shard_map/ppermute | solution.py:332
  1083.8 44.8 %all-to-all-done.2 = bf16[4,640,512]{2,1,0:T(8,128)(2,1)S(1)} async-done(((bf16[4,640,512]{2,1,0:T(8,128)(2,1)}), bf16[4,640,512]{2,1,0:T(8,128)(2,1)S(1)}, u32[]{:S(2)}, u32[]{:S(2)}) %all-to-all-start.2) | async-done | bytes 2621472 | tf_op jit(solution)/shard_map/all_to_all | solution.py:1180
  1152.9 41.1 %collective-permute-done.56.refs_2_ = bf16[2,512,1024]{2,1,0:T(8,128)(2,1)} collective-permute-done((bf16[2,512,1024]{2,1,0:T(8,128)(2,1)S(1)}, bf16[2,512,1024]{2,1,0:T(8,128)(2,1)}, u32[]{:S(2)}, u32[]{:S(2)}) %collective-permute-start.56) | collective-permute-done | bytes 2097184 | tf_op jit(solution)/shard_map/ppermute | solution.py:328
  (437 shorter events, 406.6 us)
Async XLA Ops:
  54.9 98.2 %all-to-all-start = ((bf16[4,640,512]{2,1,0:T(8,128)(2,1)}), bf16[4,640,512]{2,1,0:T(8,128)(2,1)S(1)}, u32[]{:S(2)}, u32[]{:S(2)}) async-start(bf16[4,640,512]{2,1,0:T(8,128)(2,1)} %bitcast.207), calls=%async_computation | async-start | bytes 5242880 | tf_op jit(solution)/shard_map/all_to_all | solution.py:959
  59.7 82.1 %all-gather.14.cloned.1.call-start = ((), (), s32[]{:S(2)}) async-start(), calls=%async_computation.15 | async-start | bytes 2621440 | tf_op jit(solution)/shard_map/all_gather | solution.py:970
  62.2 156.5 %all-gather.16.cloned.1.call-start = ((), (), s32[]{:S(2)}) async-start(), calls=%async_computation.16 | async-start | bytes 1310720 | tf_op jit(solution)/shard_map/all_gather | solution.py:1015
  153.1 148.4 %all-gather.8.cloned.1.call-start = ((), (), s32[]{:S(2)}) async-start(), calls=%async_computation.8 | async-start | bytes 5242880 | tf_op jit(solution)/shard_map/all_gather | solution.py:1016
  155.7 75.9 %collective-permute-start.7 = (bf16[2560,512]{1,0:T(8,128)(2,1)S(1)}, bf16[2560,512]{1,0:T(8,128)(2,1)}, u32[]{:S(2)}, u32[]{:S(2)}) collective-permute-start(bf16[2560,512]{1,0:T(8,128)(2,1)S(1)} %bitcast.193), channel_id=1, source_target_pairs={{0,8},{8,0},{16,24},{24,16},{1,9},{9,1},{17,25},{25,17},{2,10},{10... | collective-permute-start | bytes 7864328 | tf_op jit(solution)/shard_map/ppermute | solution.py:324
  227.1 96.5 %all-to-all-start.1 = ((bf16[4,640,512]{2,1,0:T(8,128)(2,1)}), bf16[4,640,512]{2,1,0:T(8,128)(2,1)}, u32[]{:S(2)}, u32[]{:S(2)}) async-start(bf16[4,640,512]{2,1,0:T(8,128)(2,1)} %bitcast.208), calls=%async_computation.1 | async-start | bytes 5242880 | tf_op jit(solution)/shard_map/all_to_all | solution.py:1055
  231.6 159.9 %all-gather.10.cloned.1.call-start = ((), (), s32[]{:S(2)}) async-start(), calls=%async_computation.9 | async-start | bytes 5242880 | tf_op jit(solution)/shard_map/all_gather | solution.py:1017
  300.9 169.6 %all-gather.12.cloned.1.call-start = ((), (), s32[]{:S(2)}) async-start(), calls=%async_computation.10 | async-start | bytes 5242880 | tf_op jit(solution)/shard_map/all_gather | solution.py:1018
  327.0 58.6 %collective-permute-start.16 = (bf16[2560,512]{1,0:T(8,128)(2,1)S(1)}, bf16[2560,512]{1,0:T(8,128)(2,1)S(1)}, u32[]{:S(2)}, u32[]{:S(2)}) collective-permute-start(bf16[2560,512]{1,0:T(8,128)(2,1)S(1)} %add_convert_fusion.8), channel_id=1, source_target_pairs={{0,1},{1,0},{2,3},{3,2},{4,5},{5,4},{6,7},{7,6},{8,9},{9,8},{10,11... | collective-permute-start | bytes 7864328 | tf_op jit(solution)/shard_map/ppermute | solution.py:332
  328.6 69.8 %collective-permute-start.20 = (bf16[768,2048]{1,0:T(8,128)(2,1)}, bf16[768,2048]{1,0:T(8,128)(2,1)}, u32[]{:S(2)}, u32[]{:S(2)}) collective-permute-start(bf16[768,2048]{1,0:T(8,128)(2,1)} %next_blocks.3), channel_id=1, source_target_pairs={{0,16},{16,0},{8,24},{24,8},{1,17},{17,1},{9,25},{25,9},{2,18},{18... | collective-permute-start | bytes 9437192 | tf_op jit(solution)/shard_map/ppermute | solution.py:328
  391.5 682.9 %reduce-scatter.5.cloned.1.call-start = ((), (), s32[]{:S(2)}) async-start(), calls=%async_computation.11 | async-start | bytes 5242880 | tf_op jit(solution)/shard_map/reduce_scatter | solution.py:1097
  398.4 59.0 %collective-permute-start.21 = (bf16[2560,512]{1,0:T(8,128)(2,1)}, bf16[2560,512]{1,0:T(8,128)(2,1)S(1)}, u32[]{:S(2)}, u32[]{:S(2)}) collective-permute-start(bf16[2560,512]{1,0:T(8,128)(2,1)} %multiply_convert_fusion.refs_0_.refs_1_), channel_id=1, source_target_pairs={{0,1},{1,0},{2,3},{3,2},{4,5},{5,4},{6,7},{7,6},{8,9},{9,8},{10,11... | collective-permute-start | bytes 7864328 | tf_op jit(solution)/shard_map/ppermute | solution.py:332
  399.7 76.7 %collective-permute-start.26 = (bf16[768,2048]{1,0:T(8,128)(2,1)}, bf16[768,2048]{1,0:T(8,128)(2,1)}, u32[]{:S(2)}, u32[]{:S(2)}) collective-permute-start(bf16[768,2048]{1,0:T(8,128)(2,1)} %next_blocks.4), channel_id=1, source_target_pairs={{0,16},{16,0},{8,24},{24,8},{1,17},{17,1},{9,25},{25,9},{2,18},{18... | collective-permute-start | bytes 9437192 | tf_op jit(solution)/shard_map/ppermute | solution.py:328
  457.9 71.5 %collective-permute-start.22 = (bf16[2560,512]{1,0:T(8,128)(2,1)}, bf16[2560,512]{1,0:T(8,128)(2,1)}, u32[]{:S(2)}, u32[]{:S(2)}) collective-permute-start(bf16[2560,512]{1,0:T(8,128)(2,1)} %bitcast.39.refs_0_.refs_1_), channel_id=1, source_target_pairs={{0,1},{1,0},{2,3},{3,2},{4,5},{5,4},{6,7},{7,6},{8,9},{9,8},{10,11... | collective-permute-start | bytes 7864328 | tf_op jit(solution)/shard_map/ppermute | solution.py:332
  474.9 70.2 %collective-permute-start.28 = (bf16[768,2048]{1,0:T(8,128)(2,1)}, bf16[768,2048]{1,0:T(8,128)(2,1)}, u32[]{:S(2)}, u32[]{:S(2)}) collective-permute-start(bf16[768,2048]{1,0:T(8,128)(2,1)} %next_blocks.5), channel_id=1, source_target_pairs={{0,16},{16,0},{8,24},{24,8},{1,17},{17,1},{9,25},{25,9},{2,18},{18... | collective-permute-start | bytes 9437192 | tf_op jit(solution)/shard_map/ppermute | solution.py:328
  476.4 68.7 %collective-permute-start.24 = (bf16[2560,512]{1,0:T(8,128)(2,1)}, bf16[2560,512]{1,0:T(8,128)(2,1)S(1)}, u32[]{:S(2)}, u32[]{:S(2)}) collective-permute-start(bf16[2560,512]{1,0:T(8,128)(2,1)} %bitcast.39.refs_0_.refs_1_), channel_id=1, source_target_pairs={{0,8},{8,0},{16,24},{24,16},{1,9},{9,1},{17,25},{25,17},{2,10},{10... | collective-permute-start | bytes 7864328 | tf_op jit(solution)/shard_map/ppermute | solution.py:324
  654.4 93.6 %collective-permute-start.30 = (bf16[1024,2048]{1,0:T(8,128)(2,1)}, bf16[1024,2048]{1,0:T(8,128)(2,1)S(1)}, u32[]{:S(2)}, u32[]{:S(2)}) collective-permute-start(bf16[1024,2048]{1,0:T(8,128)(2,1)} %down_grad_other.1), channel_id=1, source_target_pairs={{0,16},{16,0},{8,24},{24,8},{1,17},{17,1},{9,25},{25,9},{2,18},{18... | collective-permute-start | bytes 12582920 | tf_op jit(solution)/shard_map/ppermute | solution.py:328
  690.8 95.8 %collective-permute-start.31 = (bf16[2560,512]{1,0:T(8,128)(2,1)}, bf16[2560,512]{1,0:T(8,128)(2,1)}, u32[]{:S(2)}, u32[]{:S(2)}) collective-permute-start(bf16[2560,512]{1,0:T(8,128)(2,1)} %get-tuple-element.156), channel_id=1, source_target_pairs={{0,8},{8,0},{16,24},{24,16},{1,9},{9,1},{17,25},{25,17},{2,10},{10... | collective-permute-start | bytes 7864328 | tf_op jit(solution)/shard_map/ppermute | solution.py:324
  695.9 90.6 %collective-permute-start.32 = (bf16[2560,512]{1,0:T(8,128)(2,1)}, bf16[2560,512]{1,0:T(8,128)(2,1)}, u32[]{:S(2)}, u32[]{:S(2)}) collective-permute-start(bf16[2560,512]{1,0:T(8,128)(2,1)} %add_convert_fusion.7), channel_id=1, source_target_pairs={{0,1},{1,0},{2,3},{3,2},{4,5},{5,4},{6,7},{7,6},{8,9},{9,8},{10,11... | collective-permute-start | bytes 7864328 | tf_op jit(solution)/shard_map/ppermute | solution.py:332
  697.4 140.2 %collective-permute-start.37 = (bf16[1024,2048]{1,0:T(8,128)(2,1)}, bf16[1024,2048]{1,0:T(8,128)(2,1)}, u32[]{:S(2)}, u32[]{:S(2)}) collective-permute-start(bf16[1024,2048]{1,0:T(8,128)(2,1)} %gate_grad_other.1), channel_id=1, source_target_pairs={{0,16},{16,0},{8,24},{24,8},{1,17},{17,1},{9,25},{25,9},{2,18},{18... | collective-permute-start | bytes 12582920 | tf_op jit(solution)/shard_map/ppermute | solution.py:328
  793.2 283.5 %reduce-scatter.7.cloned.1.call-start = ((), (), s32[]{:S(2)}) async-start(), calls=%async_computation.12 | async-start | bytes 5242880 | tf_op jit(solution)/shard_map/reduce_scatter | solution.py:1097
  804.9 68.0 %collective-permute-start.36 = (bf16[2560,512]{1,0:T(8,128)(2,1)S(1)}, bf16[2560,512]{1,0:T(8,128)(2,1)}, u32[]{:S(2)}, u32[]{:S(2)}) collective-permute-start(bf16[2560,512]{1,0:T(8,128)(2,1)S(1)} %get-tuple-element.177.h0.refs_1_), channel_id=1, source_target_pairs={{0,1},{1,0},{2,3},{3,2},{4,5},{5,4},{6,7},{7,6},{8,9},{9,8},{10,11... | collective-permute-start | bytes 7864328 | tf_op jit(solution)/shard_map/ppermute | solution.py:332
  806.7 68.3 %collective-permute-start.38 = (bf16[2560,512]{1,0:T(8,128)(2,1)S(1)}, bf16[2560,512]{1,0:T(8,128)(2,1)}, u32[]{:S(2)}, u32[]{:S(2)}) collective-permute-start(bf16[2560,512]{1,0:T(8,128)(2,1)S(1)} %get-tuple-element.177.h0.refs_1_), channel_id=1, source_target_pairs={{0,8},{8,0},{16,24},{24,16},{1,9},{9,1},{17,25},{25,17},{2,10},{10... | collective-permute-start | bytes 7864328 | tf_op jit(solution)/shard_map/ppermute | solution.py:324
  873.5 92.9 %collective-permute-start.43 = (bf16[1024,2048]{1,0:T(8,128)(2,1)}, bf16[1024,2048]{1,0:T(8,128)(2,1)}, u32[]{:S(2)}, u32[]{:S(2)}) collective-permute-start(bf16[1024,2048]{1,0:T(8,128)(2,1)} %up_grad_other.1), channel_id=1, source_target_pairs={{0,16},{16,0},{8,24},{24,8},{1,17},{17,1},{9,25},{25,9},{2,18},{18... | collective-permute-start | bytes 12582920 | tf_op jit(solution)/shard_map/ppermute | solution.py:328
  875.0 80.1 %collective-permute-start.41 = (bf16[2560,512]{1,0:T(8,128)(2,1)}, bf16[2560,512]{1,0:T(8,128)(2,1)}, u32[]{:S(2)}, u32[]{:S(2)}) collective-permute-start(bf16[2560,512]{1,0:T(8,128)(2,1)} %get-tuple-element.168), channel_id=1, source_target_pairs={{0,8},{8,0},{16,24},{24,16},{1,9},{9,1},{17,25},{25,17},{2,10},{10... | collective-permute-start | bytes 7864328 | tf_op jit(solution)/shard_map/ppermute | solution.py:324
  897.9 59.2 %collective-permute-start.42 = (bf16[2560,512]{1,0:T(8,128)(2,1)}, bf16[2560,512]{1,0:T(8,128)(2,1)}, u32[]{:S(2)}, u32[]{:S(2)}) collective-permute-start(bf16[2560,512]{1,0:T(8,128)(2,1)} %add_convert_fusion.6), channel_id=1, source_target_pairs={{0,1},{1,0},{2,3},{3,2},{4,5},{5,4},{6,7},{7,6},{8,9},{9,8},{10,11... | collective-permute-start | bytes 7864328 | tf_op jit(solution)/shard_map/ppermute | solution.py:332
  1000.8 59.2 %collective-permute-start.46 = (bf16[2560,512]{1,0:T(8,128)(2,1)}, bf16[2560,512]{1,0:T(8,128)(2,1)}, u32[]{:S(2)}, u32[]{:S(2)}) collective-permute-start(bf16[2560,512]{1,0:T(8,128)(2,1)} %add_convert_fusion.4), channel_id=1, source_target_pairs={{0,1},{1,0},{2,3},{3,2},{4,5},{5,4},{6,7},{7,6},{8,9},{9,8},{10,11... | collective-permute-start | bytes 7864328 | tf_op jit(solution)/shard_map/ppermute | solution.py:332
  1003.4 125.2 %all-to-all-start.2 = ((bf16[4,640,512]{2,1,0:T(8,128)(2,1)}), bf16[4,640,512]{2,1,0:T(8,128)(2,1)S(1)}, u32[]{:S(2)}, u32[]{:S(2)}) async-start(bf16[4,640,512]{2,1,0:T(8,128)(2,1)} %bitcast.209), calls=%async_computation.2 | async-start | bytes 5242880 | tf_op jit(solution)/shard_map/all_to_all | solution.py:1180
  1007.0 144.5 %reduce-scatter.9.cloned.1.call-start = ((), (), s32[]{:S(2)}) async-start(), calls=%async_computation.13 | async-start | bytes 5242880 | tf_op jit(solution)/shard_map/reduce_scatter | solution.py:1097
  1007.8 214.3 %reduce-scatter.11.cloned.1.call-start = ((), (), s32[]{:S(2)}) async-start(), calls=%async_computation.14 | async-start | bytes 3932160 | tf_op jit(solution)/shard_map/reduce_scatter | solution.py:1218
  1066.6 70.6 %collective-permute-start.51 = (bf16[2,2,2,384,512]{4,3,2,1,0:T(8,128)(2,1)}, bf16[2,2,2,384,512]{4,3,2,1,0:T(8,128)(2,1)}, u32[]{:S(2)}, u32[]{:S(2)}) collective-permute-start(bf16[2,2,2,384,512]{4,3,2,1,0:T(8,128)(2,1)} %pad_maximum_fusion), channel_id=1, source_target_pairs={{0,16},{16,0},{8,24},{24,8},{1,17},{17,1},{9,25},{25,9},{2,18},{18... | collective-permute-start | bytes 9437192 | tf_op jit(solution)/shard_map/ppermute | solution.py:328
  1194.1 66.0 %all-to-all-start.3 = ((bf16[4,640,512]{2,1,0:T(8,128)(2,1)}), bf16[4,640,512]{2,1,0:T(8,128)(2,1)}, u32[]{:S(2)}, u32[]{:S(2)}) async-start(bf16[4,640,512]{2,1,0:T(8,128)(2,1)} %bitcast.205), calls=%async_computation.5 | async-start | bytes 5242880 | tf_op jit(solution)/shard_map/all_to_all | solution.py:1208
  (108 other events, 1800.3 us)
Sparse Core Ops, SparseCore 0:
  62.7 79.0 all-gather.13
  153.2 28.3 all-gather.15
  183.8 108.1 all-gather.7
  301.1 86.9 all-gather.9
  391.6 78.8 all-gather.11
  793.3 75.3 reduce-scatter.4
  899.6 74.4 reduce-scatter.6
  1010.8 120.6 reduce-scatter.8
  1146.0 58.5 reduce-scatter.10

commit v5 on v4

--- a/solution.py
+++ b/solution.py
@@ -1110,11 +1110,11 @@
     down_own = unit_grad(hid_m, grad_pieces, "down_grad_mine", gate_other)
     parts[1] = after(parts[1], down_own)
     own, got, outgoing = collect_core(parts)
-    down_total = low(wide(after(down_own, outgoing)) + wide(swap_x(down_other)))
+    up_other = turned_grad(after(dup_o, outgoing), ffn_pieces, z, planes, "up_grad_other")
+    gate_own = unit_grad(dgate_m, ffn_pieces, "gate_grad_mine", up_other)
+    down_total = low(wide(after(down_own, gate_own)) + wide(swap_x(down_other)))
     down_sum = to_row(down_total)
-    up_other = turned_grad(after(dup_o, down_total), ffn_pieces, z, planes, "up_grad_other")
-    gate_own = unit_grad(dgate_m, ffn_pieces, "gate_grad_mine", up_other)
-    normed_ffn_grad = collect_col(after(own, gate_own), got, outgoing)
+    normed_ffn_grad = collect_col(after(own, down_total), got, outgoing)
 
     def norm_back(grad, ratio, normed, gain):
         scaled = grad * gain
@@ -1125,8 +1125,6 @@
     middle_grad = wide(cotangent) + middle_back
     middle_low = low(middle_grad)
     up_own = unit_grad(dup_m, ffn_pieces, "up_grad_mine", middle_low)
-    gate_total = low(wide(after(gate_own, up_own)) + wide(swap_x(gate_other)))
-    gate_sum = to_row(gate_total)
     where = jnp.stack([y, x, c]).astype(jnp.int32)
 
     def unit_halves(total):
@@ -1142,7 +1140,7 @@
     out_parts = rows_call(
         functools.partial(sum_out_kernel, 2),
         2 * block,
-        [after(hid_m, gate_total), hid_o],
+        [after(hid_m, up_own), hid_o],
         [down_mine, down_near, down_far],
         [(quarter, jnp.bfloat16)] * 4,
         2 * rows * features * 2 * planes * unit,
@@ -1159,7 +1157,9 @@
         2 * rows * features * groups * 2 * HEAD,
         "attn_grad",
     )[0]
-    out_parts[1] = after(out_parts[1], attn_grad)
+    gate_total = low(wide(after(gate_own, attn_grad)) + wide(swap_x(gate_other)))
+    gate_sum = to_row(gate_total)
+    out_parts[1] = after(out_parts[1], gate_total)
     out_own, out_got, out_outgoing = collect_core(out_parts)
     qkv_grad = attend_back(
         qkv, attn, after(attn_grad, out_outgoing), label_col, label_rows, lse, cosine, sine,

time: 1310 us -> 1300 us (level)
    ppermute x13, waiting for transfers between devices: 140 us -> 123 us  [swap_x(): return lax.ppermute(a, 'dp', X_SWAP)]
  transfers between devices with their start and end apart: 82 -> 82, of which waited for: 36 -> 36; matrix products, arithmetic and copies ran while one was open for 15% -> 14% of each run, Pallas kernels for 29% -> 29%
where the time goes in v5:
time: 1300 us; the launch traced here: 1290 us
  waiting for transfers between devices  508 us (39%)
  Pallas kernels  485 us (37%)
  other arithmetic  142 us (11%)
  local copies, waits for them, and re-layouts  72.6 us (6%)
  starting transfers between devices  68.8 us (5%)
  between operations  15.2 us (1%)
    ppermute x18, waiting for transfers between devices, swap_col(): return lax.ppermute(a, 'col', COL_SWAP)  240 us
    pallas_call x8, Pallas kernels, rows_call(): pl.pallas_call(fn, grid=(rows // block,), in_specs=in_specs, out_specs=[p...  226 us
    ppermute x13, waiting for transfers between devices, swap_x(): return lax.ppermute(a, 'dp', X_SWAP)  123 us
    pallas_call x5, Pallas kernels, weight_grad(): pl.pallas_call(functools.partial(weight_grad_kernel, len(bs), split), gri...  80.1 us
    convert_element_type x12, other arithmetic, low(): return a.astype(jnp.bfloat16)  59 us
    pallas_call x1, Pallas kernels, attend_back(): pl.pallas_call(functools.partial(attend_back_kernel, trunk, leaf_begin, b...  55.7 us
    pallas_call x3, Pallas kernels, turned_grad(): pl.pallas_call(functools.partial(turned_grad_kernel, len(bs)), grid_spec=...  51.8 us
    all_to_all x1, waiting for transfers between devices, tree_body(): output_tree = lax.all_to_all(output, 'row', 0, 0, tiled=True)  45.2 us
  transfers between devices with their start and end apart: 82, of which 36 were waited for; matrix products, arithmetic and copies ran while one was open for 14% of the time, Pallas kernels for 29%

profile of v5, /device:TPU:0, one launch (start us, length us, event | category | flops | bytes accessed | tf_op | source)
XLA Modules:
  0.0 1291.5 jit_solution(10881744212225336725)
XLA Ops:
  62.3 13.1 %collective-permute-done.2 = bf16[896,1024]{1,0:T(8,128)(2,1)} collective-permute-done((bf16[896,1024]{1,0:T(8,128)(2,1)}, bf16[896,1024]{1,0:T(8,128)(2,1)}, u32[]{:S(2)}, u32[]{:S(2)}) %collective-permute-start.2) | collective-permute-done | bytes 1835040 | tf_op jit(solution)/shard_map/ppermute | solution.py:332
  95.0 18.0 %collective-permute-done.3 = bf16[768,1024]{1,0:T(8,128)(2,1)} collective-permute-done((bf16[768,1024]{1,0:T(8,128)(2,1)}, bf16[768,1024]{1,0:T(8,128)(2,1)}, u32[]{:S(2)}, u32[]{:S(2)}) %collective-permute-start.3) | collective-permute-done | bytes 1572896 | tf_op jit(solution)/shard_map/ppermute | solution.py:332
  117.9 23.9 %all-gather.14.cloned.1.call-done = bf16[8,256,512]{2,1,0:T(8,128)(2,1)} async-done(((bf16[2,256,512]{2,1,0:T(8,128)(2,1)}), bf16[8,256,512]{2,1,0:T(8,128)(2,1)}) %all-gather.14.cloned.1.call-update) | async-done | bytes 2097168 | tf_op jit(solution)/shard_map/all_gather | solution.py:970
  141.8 11.3 all-to-all-done
  155.8 55.8 %collective-permute-done.6.x1 = bf16[2560,512]{1,0:T(8,128)(2,1)} collective-permute-done((bf16[2560,512]{1,0:T(8,128)(2,1)S(1)}, bf16[2560,512]{1,0:T(8,128)(2,1)}, u32[]{:S(2)}, u32[]{:S(2)}) %collective-permute-start.6) | collective-permute-done | bytes 2621472 | tf_op jit(solution)/shard_map/ppermute | solution.py:332
  231.7 20.2 %project.1 = (bf16[2560,2048]{1,0:T(8,128)(2,1)}, bf16[2560,1024]{1,0:T(8,128)(2,1)}, f32[2560,1]{1,0:T(8,128)}) custom-call(bf16[2560,512]{1,0:T(8,128)(2,1)} %bitcast.192, bf16[2560,512]{1,0:T(8,128)(2,1)} %collective-permute-done.6.x1, bf16[2560,512]{1,0:T(8,128)(2,1)} %collective-permute-done.7.x2, bf16[2560,512]{1,0:T(8,128)(2,1)} %collective-permute-done.8.x3, ...), custom_call_target="tpu_custom_call" | custom-call | flops 1342177280 | bytes 4131072 | tf_op jit(solution)/shard_map/project/pallas_call | solution.py:372
  256.4 34.4 %attend.1 = (bf16[2560,512]{1,0:T(8,128)(2,1)}, f32[2,10,1,512]{3,2,1,0:T(1,128)}) custom-call(bf16[2560,1024]{1,0:T(8,128)(2,1)} %get-tuple-element.111.q_ref.k_ref.v_ref, bf16[2560,1024]{1,0:T(8,128)(2,1)} %get-tuple-element.111.q_ref.k_ref.v_ref, bf16[2560,1024]{1,0:T(8,128)(2,1)} %get-tuple-element.111.q_ref.k_ref.v_ref, s32[2560,1]{1,0:T(8,128)} %copy.90.lab_ref, ...), custom_call_target="tpu_custom_call" | custom-call | flops 3355443200 | bytes 1638400 | tf_op jit(solution)/shard_map/attend/pallas_call | solution.py:585
  305.9 17.6 %all-to-all-done.1 = bf16[4,640,512]{2,1,0:T(8,128)(2,1)} async-done(((bf16[4,640,512]{2,1,0:T(8,128)(2,1)}), bf16[4,640,512]{2,1,0:T(8,128)(2,1)}, u32[]{:S(2)}, u32[]{:S(2)}) %all-to-all-start.1) | async-done | bytes 2621472 | tf_op jit(solution)/shard_map/all_to_all | solution.py:1055
  330.1 55.5 %collective-permute-done.16 = bf16[2560,512]{1,0:T(8,128)(2,1)S(1)} collective-permute-done((bf16[2560,512]{1,0:T(8,128)(2,1)S(1)}, bf16[2560,512]{1,0:T(8,128)(2,1)S(1)}, u32[]{:S(2)}, u32[]{:S(2)}) %collective-permute-start.16) | collective-permute-done | bytes 2621472 | tf_op jit(solution)/shard_map/ppermute | solution.py:332
  401.2 56.3 %collective-permute-done.21.refs_1_.refs_2_ = bf16[2560,512]{1,0:T(8,128)(2,1)S(1)} collective-permute-done((bf16[2560,512]{1,0:T(8,128)(2,1)}, bf16[2560,512]{1,0:T(8,128)(2,1)S(1)}, u32[]{:S(2)}, u32[]{:S(2)}) %collective-permute-start.21) | collective-permute-done | bytes 2621472 | tf_op jit(solution)/shard_map/ppermute | solution.py:332
  459.2 11.3 all-gather.12.cloned.1.call-done.in_ref.refs_8_.refs_2_
  476.4 53.0 %gate_up.1 = (bf16[2560,1024]{1,0:T(8,128)(2,1)}, bf16[2560,1024]{1,0:T(8,128)(2,1)}, bf16[2560,1024]{1,0:T(8,128)(2,1)}, bf16[2560,1024]{1,0:T(8,128)(2,1)}) custom-call(bf16[2560,512]{1,0:T(8,128)(2,1)} %multiply_convert_fusion.refs_0_.refs_1_, bf16[2560,512]{1,0:T(8,128)(2,1)} %copy-done.4, bf16[2560,512]{1,0:T(8,128)(2,1)} %collective-permute-done.25.refs_2_.refs_3_, ...), custom_call_target="tpu_custom_call" | custom-call | flops 5368709120 | bytes 6029312 | tf_op jit(solution)/shard_map/gate_up/pallas_call | solution.py:372
  530.0 15.1 %collective-permute-done.28.refs_10_.refs_4_ = bf16[768,2048]{1,0:T(8,128)(2,1)} collective-permute-done((bf16[768,2048]{1,0:T(8,128)(2,1)}, bf16[768,2048]{1,0:T(8,128)(2,1)}, u32[]{:S(2)}, u32[]{:S(2)}) %collective-permute-start.28) | collective-permute-done | bytes 3145760 | tf_op jit(solution)/shard_map/ppermute | solution.py:328
  547.4 37.0 %hidden.1 = (bf16[2560,1024]{1,0:T(8,128)(2,1)}, bf16[2560,1024]{1,0:T(8,128)(2,1)}, bf16[2560,1024]{1,0:T(8,128)(2,1)}, bf16[2560,1024]{1,0:T(8,128)(2,1)}, bf1...) custom-call(bf16[2560,512]{1,0:T(8,128)(2,1)} %bitcast.39.refs_0_.refs_1_, ...), custom_call_target="tpu_custom_call" | custom-call | flops 2684354560 | bytes 8912896 | tf_op jit(solution)/shard_map/hidden/pallas_call | solution.py:372
  584.4 17.1 %down_grad_other.1 = bf16[1024,2048]{1,0:T(8,128)(2,1)} custom-call(s32[1]{0:T(128)} %bitcast.40.where_ref, bf16[2560,1024]{1,0:T(8,128)(2,1)} %get-tuple-element.140.refs_0_.refs_1_, bf16[2560,512]{1,0:T(8,128)(2,1)} %bitcast.39.refs_0_.refs_1_, bf16[2560,512]{1,0:T(8,128)(2,1)} %collective-permute-done.22.refs_1_.refs_2_, bf16[2560,512]{1,0:T(8,128)(2,1)} %copy-done.5, ...), custom_call_target="tpu_custom_call" | custom-call | flops 1342177280 | bytes 2490368 | tf_op jit(solution)/shard_map/down_grad_other/pallas_call | solution.py:761
  601.6 52.8 %pair_back.1 = (bf16[2560,512]{1,0:T(8,128)(2,1)}, bf16[2560,512]{1,0:T(8,128)(2,1)}, bf16[2560,512]{1,0:T(8,128)(2,1)}, bf16[2560,512]{1,0:T(8,128)(2,1)}) custom-call(bf16[2560,1024]{1,0:T(8,128)(2,1)} %get-tuple-element.153.refs_0_, bf16[2560,1024]{1,0:T(8,128)(2,1)} %get-tuple-element.157.refs_1_.refs_0_, ...), custom_call_target="tpu_custom_call" | custom-call | flops 5368709120 | bytes 6029312 | tf_op jit(solution)/shard_map/pair_back/pallas_call | solution.py:372
  656.0 17.2 %gate_grad_other.1 = bf16[1024,2048]{1,0:T(8,128)(2,1)} custom-call(s32[1]{0:T(128)} %bitcast.40.where_ref, bf16[2560,1024]{1,0:T(8,128)(2,1)} %get-tuple-element.147.refs_2_.refs_0_, bf16[2560,512]{1,0:T(8,128)(2,1)} %multiply_convert_fusion.refs_0_.refs_1_, bf16[2560,512]{1,0:T(8,128)(2,1)} %copy-done.4, ...), custom_call_target="tpu_custom_call" | custom-call | flops 1342177280 | bytes 2490368 | tf_op jit(solution)/shard_map/gate_grad_other/pallas_call | solution.py:761
  673.2 17.5 %down_grad_mine.1 = bf16[1024,2048]{1,0:T(8,128)(2,1)} custom-call(bf16[2560,1024]{1,0:T(8,128)(2,1)} %get-tuple-element.158.refs_0_, bf16[2560,512]{1,0:T(8,128)(2,1)} %bitcast.39.refs_0_.refs_1_, bf16[2560,512]{1,0:T(8,128)(2,1)} %collective-permute-done.22.refs_1_.refs_2_, bf16[2560,512]{1,0:T(8,128)(2,1)} %copy-done.5, bf16[2560,512]{1,0:T(8,128)(2,1)} %copy-done.6), custom_call_target="tpu_custom_call" | custom-call | flops 1342177280 | bytes 2490368 | tf_op jit(solution)/shard_map/down_grad_mine/pallas_call | solution.py:848
  694.5 17.5 %up_grad_other.1 = bf16[1024,2048]{1,0:T(8,128)(2,1)} custom-call(s32[1]{0:T(128)} %bitcast.40.where_ref, bf16[2560,1024]{1,0:T(8,128)(2,1)} %get-tuple-element.152.refs_3_.refs_0_, bf16[2560,512]{1,0:T(8,128)(2,1)} %multiply_convert_fusion.refs_0_.refs_1_, bf16[2560,512]{1,0:T(8,128)(2,1)} %copy-done.4, ...), custom_call_target="tpu_custom_call" | custom-call | flops 1342177280 | bytes 2490368 | tf_op jit(solution)/shard_map/up_grad_other/pallas_call | solution.py:761
  712.0 17.6 %gate_grad_mine.1 = bf16[1024,2048]{1,0:T(8,128)(2,1)} custom-call(bf16[2560,1024]{1,0:T(8,128)(2,1)} %get-tuple-element.153.refs_0_, bf16[2560,512]{1,0:T(8,128)(2,1)} %multiply_convert_fusion.refs_0_.refs_1_, bf16[2560,512]{1,0:T(8,128)(2,1)} %copy-done.4, bf16[2560,512]{1,0:T(8,128)(2,1)} %collective-permute-done.25.refs_2_.refs_3_, ...), custom_call_target="tpu_custom_call" | custom-call | flops 1342177280 | bytes 2490368 | tf_op jit(solution)/shard_map/gate_grad_mine/pallas_call | solution.py:848
  729.6 18.2 %collective-permute-done.30 = bf16[1024,2048]{1,0:T(8,128)(2,1)} collective-permute-done((bf16[1024,2048]{1,0:T(8,128)(2,1)}, bf16[1024,2048]{1,0:T(8,128)(2,1)}, u32[]{:S(2)}, u32[]{:S(2)}) %collective-permute-start.30) | collective-permute-done | bytes 4194336 | tf_op jit(solution)/shard_map/ppermute | solution.py:328
  776.4 17.4 %up_grad_mine.1 = bf16[1024,2048]{1,0:T(8,128)(2,1)} custom-call(bf16[2560,1024]{1,0:T(8,128)(2,1)} %get-tuple-element.157.refs_1_.refs_0_, bf16[2560,512]{1,0:T(8,128)(2,1)} %multiply_convert_fusion.refs_0_.refs_1_, bf16[2560,512]{1,0:T(8,128)(2,1)} %copy-done.4, bf16[2560,512]{1,0:T(8,128)(2,1)} %collective-permute-done.25.refs_2_.refs_3_, ...), custom_call_target="tpu_custom_call" | custom-call | flops 1342177280 | bytes 2490368 | tf_op jit(solution)/shard_map/up_grad_mine/pallas_call | solution.py:848
  793.8 27.6 %down.1 = (bf16[2560,512]{1,0:T(8,128)(2,1)}, bf16[2560,512]{1,0:T(8,128)(2,1)}, bf16[2560,512]{1,0:T(8,128)(2,1)}, bf16[2560,512]{1,0:T(8,128)(2,1)}) custom-call(bf16[2560,1024]{1,0:T(8,128)(2,1)} %get-tuple-element.158.refs_0_, bf16[2560,1024]{1,0:T(8,128)(2,1)} %get-tuple-element.140.refs_0_.refs_1_, ...), custom_call_target="tpu_custom_call" | custom-call | flops 2684354560 | bytes 3670016 | tf_op jit(solution)/shard_map/down/pallas_call | solution.py:372
  851.3 17.5 %collective-permute-done.39 = bf16[1024,2048]{1,0:T(8,128)(2,1)} collective-permute-done((bf16[1024,2048]{1,0:T(8,128)(2,1)}, bf16[1024,2048]{1,0:T(8,128)(2,1)}, u32[]{:S(2)}, u32[]{:S(2)}) %collective-permute-start.39) | collective-permute-done | bytes 4194336 | tf_op jit(solution)/shard_map/ppermute | solution.py:328
  880.5 55.7 %attend_back.1.d_ref.refs_1_ = bf16[2560,1024]{1,0:T(8,128)(2,1)} custom-call(bf16[2560,1024]{1,0:T(8,128)(2,1)} %get-tuple-element.111.q_ref.k_ref.v_ref, bf16[2560,1024]{1,0:T(8,128)(2,1)} %get-tuple-element.111.q_ref.k_ref.v_ref, bf16[2560,1024]{1,0:T(8,128)(2,1)} %get-tuple-element.111.q_ref.k_ref.v_ref, ...), custom_call_target="tpu_custom_call" | custom-call | flops 8388608000 | bytes 3276800 | tf_op jit(solution)/shard_map/attend_back/pallas_call | solution.py:608
  942.8 13.9 %collective-permute-done.43 = bf16[1024,2048]{1,0:T(8,128)(2,1)} collective-permute-done((bf16[1024,2048]{1,0:T(8,128)(2,1)}, bf16[1024,2048]{1,0:T(8,128)(2,1)}, u32[]{:S(2)}, u32[]{:S(2)}) %collective-permute-start.43) | collective-permute-done | bytes 4194336 | tf_op jit(solution)/shard_map/ppermute | solution.py:328
  962.8 15.8 %project_back.1 = (bf16[2560,512]{1,0:T(8,128)(2,1)}, bf16[2560,512]{1,0:T(8,128)(2,1)}, bf16[2560,512]{1,0:T(8,128)(2,1)}, bf16[2560,512]{1,0:T(8,128)(2,1)}) custom-call(bf16[2560,1024]{1,0:T(8,128)(2,1)} %attend_back.1.d_ref.refs_1_, bf16[2,1024,512]{2,1,0:T(8,128)(2,1)} %bitcast.199, bf16[2,1024,512]{2,1,0:T(8,128)(2,1)} %bitcast.29.far_ref), custom_call_target="tpu_custom_call" | custom-call | flops 1342177280 | bytes 2490368 | tf_op jit(solution)/shard_map/project_back/pallas_call | solution.py:372
  996.7 16.5 %project_grad.1 = bf16[2,2048,512]{2,1,0:T(8,128)(2,1)} custom-call(bf16[2560,2048]{1,0:T(8,128)(2,1)} %get-tuple-element.173.refs_0_, bf16[2560,1024]{1,0:T(8,128)(2,1)} %attend_back.1.d_ref.refs_1_), custom_call_target="tpu_custom_call" | custom-call | flops 1342177280 | bytes 2490368 | tf_op jit(solution)/shard_map/project_grad/pallas_call | solution.py:848
  1013.2 11.2 mix_grad.1
  1035.2 15.0 %collective-permute-done.46 = bf16[2560,512]{1,0:T(8,128)(2,1)} collective-permute-done((bf16[2560,512]{1,0:T(8,128)(2,1)}, bf16[2560,512]{1,0:T(8,128)(2,1)}, u32[]{:S(2)}, u32[]{:S(2)}) %collective-permute-start.46) | collective-permute-done | bytes 2621472 | tf_op jit(solution)/shard_map/ppermute | solution.py:332
  1073.4 45.2 %all-to-all-done.2 = bf16[4,640,512]{2,1,0:T(8,128)(2,1)S(1)} async-done(((bf16[4,640,512]{2,1,0:T(8,128)(2,1)}), bf16[4,640,512]{2,1,0:T(8,128)(2,1)S(1)}, u32[]{:S(2)}, u32[]{:S(2)}) %all-to-all-start.2) | async-done | bytes 2621472 | tf_op jit(solution)/shard_map/all_to_all | solution.py:1180
  1142.9 41.1 %collective-permute-done.56.refs_2_ = bf16[2,512,1024]{2,1,0:T(8,128)(2,1)} collective-permute-done((bf16[2,512,1024]{2,1,0:T(8,128)(2,1)S(1)}, bf16[2,512,1024]{2,1,0:T(8,128)(2,1)}, u32[]{:S(2)}, u32[]{:S(2)}) %collective-permute-start.56) | collective-permute-done | bytes 2097184 | tf_op jit(solution)/shard_map/ppermute | solution.py:328
  (438 shorter events, 418.9 us)
Async XLA Ops:
  54.8 98.2 %all-to-all-start = ((bf16[4,640,512]{2,1,0:T(8,128)(2,1)}), bf16[4,640,512]{2,1,0:T(8,128)(2,1)S(1)}, u32[]{:S(2)}, u32[]{:S(2)}) async-start(bf16[4,640,512]{2,1,0:T(8,128)(2,1)} %bitcast.205), calls=%async_computation | async-start | bytes 5242880 | tf_op jit(solution)/shard_map/all_to_all | solution.py:959
  59.7 82.1 %all-gather.14.cloned.1.call-start = ((), (), s32[]{:S(2)}) async-start(), calls=%async_computation.15 | async-start | bytes 2621440 | tf_op jit(solution)/shard_map/all_gather | solution.py:970
  62.2 156.5 %all-gather.16.cloned.1.call-start = ((), (), s32[]{:S(2)}) async-start(), calls=%async_computation.16 | async-start | bytes 1310720 | tf_op jit(solution)/shard_map/all_gather | solution.py:1015
  153.1 148.4 %all-gather.8.cloned.1.call-start = ((), (), s32[]{:S(2)}) async-start(), calls=%async_computation.8 | async-start | bytes 5242880 | tf_op jit(solution)/shard_map/all_gather | solution.py:1016
  153.6 58.0 %collective-permute-start.6 = (bf16[2560,512]{1,0:T(8,128)(2,1)S(1)}, bf16[2560,512]{1,0:T(8,128)(2,1)}, u32[]{:S(2)}, u32[]{:S(2)}) collective-permute-start(bf16[2560,512]{1,0:T(8,128)(2,1)S(1)} %bitcast.190), channel_id=1, source_target_pairs={{0,1},{1,0},{2,3},{3,2},{4,5},{5,4},{6,7},{7,6},{8,9},{9,8},{10,11... | collective-permute-start | bytes 7864328 | tf_op jit(solution)/shard_map/ppermute | solution.py:332
  155.7 76.0 %collective-permute-start.7 = (bf16[2560,512]{1,0:T(8,128)(2,1)S(1)}, bf16[2560,512]{1,0:T(8,128)(2,1)}, u32[]{:S(2)}, u32[]{:S(2)}) collective-permute-start(bf16[2560,512]{1,0:T(8,128)(2,1)S(1)} %bitcast.191), channel_id=1, source_target_pairs={{0,8},{8,0},{16,24},{24,16},{1,9},{9,1},{17,25},{25,17},{2,10},{10... | collective-permute-start | bytes 7864328 | tf_op jit(solution)/shard_map/ppermute | solution.py:324
  227.0 96.5 %all-to-all-start.1 = ((bf16[4,640,512]{2,1,0:T(8,128)(2,1)}), bf16[4,640,512]{2,1,0:T(8,128)(2,1)}, u32[]{:S(2)}, u32[]{:S(2)}) async-start(bf16[4,640,512]{2,1,0:T(8,128)(2,1)} %bitcast.206), calls=%async_computation.1 | async-start | bytes 5242880 | tf_op jit(solution)/shard_map/all_to_all | solution.py:1055
  231.7 159.9 %all-gather.10.cloned.1.call-start = ((), (), s32[]{:S(2)}) async-start(), calls=%async_computation.9 | async-start | bytes 5242880 | tf_op jit(solution)/shard_map/all_gather | solution.py:1017
  300.9 169.6 %all-gather.12.cloned.1.call-start = ((), (), s32[]{:S(2)}) async-start(), calls=%async_computation.10 | async-start | bytes 5242880 | tf_op jit(solution)/shard_map/all_gather | solution.py:1018
  327.0 58.6 %collective-permute-start.16 = (bf16[2560,512]{1,0:T(8,128)(2,1)S(1)}, bf16[2560,512]{1,0:T(8,128)(2,1)S(1)}, u32[]{:S(2)}, u32[]{:S(2)}) collective-permute-start(bf16[2560,512]{1,0:T(8,128)(2,1)S(1)} %add_convert_fusion.8), channel_id=1, source_target_pairs={{0,1},{1,0},{2,3},{3,2},{4,5},{5,4},{6,7},{7,6},{8,9},{9,8},{10,11... | collective-permute-start | bytes 7864328 | tf_op jit(solution)/shard_map/ppermute | solution.py:332
  328.6 69.8 %collective-permute-start.20 = (bf16[768,2048]{1,0:T(8,128)(2,1)}, bf16[768,2048]{1,0:T(8,128)(2,1)}, u32[]{:S(2)}, u32[]{:S(2)}) collective-permute-start(bf16[768,2048]{1,0:T(8,128)(2,1)} %next_blocks.3), channel_id=1, source_target_pairs={{0,16},{16,0},{8,24},{24,8},{1,17},{17,1},{9,25},{25,9},{2,18},{18... | collective-permute-start | bytes 9437192 | tf_op jit(solution)/shard_map/ppermute | solution.py:328
  391.5 672.9 %reduce-scatter.5.cloned.1.call-start = ((), (), s32[]{:S(2)}) async-start(), calls=%async_computation.11 | async-start | bytes 5242880 | tf_op jit(solution)/shard_map/reduce_scatter | solution.py:1097
  398.5 59.0 %collective-permute-start.21 = (bf16[2560,512]{1,0:T(8,128)(2,1)}, bf16[2560,512]{1,0:T(8,128)(2,1)S(1)}, u32[]{:S(2)}, u32[]{:S(2)}) collective-permute-start(bf16[2560,512]{1,0:T(8,128)(2,1)} %multiply_convert_fusion.refs_0_.refs_1_), channel_id=1, source_target_pairs={{0,1},{1,0},{2,3},{3,2},{4,5},{5,4},{6,7},{7,6},{8,9},{9,8},{10,11... | collective-permute-start | bytes 7864328 | tf_op jit(solution)/shard_map/ppermute | solution.py:332
  399.7 76.7 %collective-permute-start.26 = (bf16[768,2048]{1,0:T(8,128)(2,1)}, bf16[768,2048]{1,0:T(8,128)(2,1)}, u32[]{:S(2)}, u32[]{:S(2)}) collective-permute-start(bf16[768,2048]{1,0:T(8,128)(2,1)} %next_blocks.4), channel_id=1, source_target_pairs={{0,16},{16,0},{8,24},{24,8},{1,17},{17,1},{9,25},{25,9},{2,18},{18... | collective-permute-start | bytes 9437192 | tf_op jit(solution)/shard_map/ppermute | solution.py:328
  458.0 71.5 %collective-permute-start.22 = (bf16[2560,512]{1,0:T(8,128)(2,1)}, bf16[2560,512]{1,0:T(8,128)(2,1)}, u32[]{:S(2)}, u32[]{:S(2)}) collective-permute-start(bf16[2560,512]{1,0:T(8,128)(2,1)} %bitcast.39.refs_0_.refs_1_), channel_id=1, source_target_pairs={{0,1},{1,0},{2,3},{3,2},{4,5},{5,4},{6,7},{7,6},{8,9},{9,8},{10,11... | collective-permute-start | bytes 7864328 | tf_op jit(solution)/shard_map/ppermute | solution.py:332
  474.9 70.2 %collective-permute-start.28 = (bf16[768,2048]{1,0:T(8,128)(2,1)}, bf16[768,2048]{1,0:T(8,128)(2,1)}, u32[]{:S(2)}, u32[]{:S(2)}) collective-permute-start(bf16[768,2048]{1,0:T(8,128)(2,1)} %next_blocks.5), channel_id=1, source_target_pairs={{0,16},{16,0},{8,24},{24,8},{1,17},{17,1},{9,25},{25,9},{2,18},{18... | collective-permute-start | bytes 9437192 | tf_op jit(solution)/shard_map/ppermute | solution.py:328
  476.4 68.7 %collective-permute-start.24 = (bf16[2560,512]{1,0:T(8,128)(2,1)}, bf16[2560,512]{1,0:T(8,128)(2,1)S(1)}, u32[]{:S(2)}, u32[]{:S(2)}) collective-permute-start(bf16[2560,512]{1,0:T(8,128)(2,1)} %bitcast.39.refs_0_.refs_1_), channel_id=1, source_target_pairs={{0,8},{8,0},{16,24},{24,16},{1,9},{9,1},{17,25},{25,17},{2,10},{10... | collective-permute-start | bytes 7864328 | tf_op jit(solution)/shard_map/ppermute | solution.py:324
  654.5 93.3 %collective-permute-start.30 = (bf16[1024,2048]{1,0:T(8,128)(2,1)}, bf16[1024,2048]{1,0:T(8,128)(2,1)}, u32[]{:S(2)}, u32[]{:S(2)}) collective-permute-start(bf16[1024,2048]{1,0:T(8,128)(2,1)} %down_grad_other.1), channel_id=1, source_target_pairs={{0,16},{16,0},{8,24},{24,8},{1,17},{17,1},{9,25},{25,9},{2,18},{18... | collective-permute-start | bytes 12582920 | tf_op jit(solution)/shard_map/ppermute | solution.py:328
  690.6 63.6 %collective-permute-start.31 = (bf16[2560,512]{1,0:T(8,128)(2,1)}, bf16[2560,512]{1,0:T(8,128)(2,1)}, u32[]{:S(2)}, u32[]{:S(2)}) collective-permute-start(bf16[2560,512]{1,0:T(8,128)(2,1)} %get-tuple-element.156), channel_id=1, source_target_pairs={{0,8},{8,0},{16,24},{24,16},{1,9},{9,1},{17,25},{25,17},{2,10},{10... | collective-permute-start | bytes 7864328 | tf_op jit(solution)/shard_map/ppermute | solution.py:324
  693.0 61.2 %collective-permute-start.32 = (bf16[2560,512]{1,0:T(8,128)(2,1)}, bf16[2560,512]{1,0:T(8,128)(2,1)}, u32[]{:S(2)}, u32[]{:S(2)}) collective-permute-start(bf16[2560,512]{1,0:T(8,128)(2,1)} %add_convert_fusion.7), channel_id=1, source_target_pairs={{0,1},{1,0},{2,3},{3,2},{4,5},{5,4},{6,7},{7,6},{8,9},{9,8},{10,11... | collective-permute-start | bytes 7864328 | tf_op jit(solution)/shard_map/ppermute | solution.py:332
  762.2 304.6 %reduce-scatter.7.cloned.1.call-start = ((), (), s32[]{:S(2)}) async-start(), calls=%async_computation.12 | async-start | bytes 5242880 | tf_op jit(solution)/shard_map/reduce_scatter | solution.py:1097
  773.2 58.8 %collective-permute-start.36 = (bf16[2560,512]{1,0:T(8,128)(2,1)S(1)}, bf16[2560,512]{1,0:T(8,128)(2,1)S(1)}, u32[]{:S(2)}, u32[]{:S(2)}) collective-permute-start(bf16[2560,512]{1,0:T(8,128)(2,1)S(1)} %get-tuple-element.177.h0.refs_1_), channel_id=1, source_target_pairs={{0,1},{1,0},{2,3},{3,2},{4,5},{5,4},{6,7},{7,6},{8,9},{9,8},{10,11... | collective-permute-start | bytes 7864328 | tf_op jit(solution)/shard_map/ppermute | solution.py:332
  775.0 93.8 %collective-permute-start.39 = (bf16[1024,2048]{1,0:T(8,128)(2,1)}, bf16[1024,2048]{1,0:T(8,128)(2,1)}, u32[]{:S(2)}, u32[]{:S(2)}) collective-permute-start(bf16[1024,2048]{1,0:T(8,128)(2,1)} %gate_grad_other.1), channel_id=1, source_target_pairs={{0,16},{16,0},{8,24},{24,8},{1,17},{17,1},{9,25},{25,9},{2,18},{18... | collective-permute-start | bytes 12582920 | tf_op jit(solution)/shard_map/ppermute | solution.py:328
  776.4 57.8 %collective-permute-start.37 = (bf16[2560,512]{1,0:T(8,128)(2,1)S(1)}, bf16[2560,512]{1,0:T(8,128)(2,1)}, u32[]{:S(2)}, u32[]{:S(2)}) collective-permute-start(bf16[2560,512]{1,0:T(8,128)(2,1)S(1)} %get-tuple-element.177.h0.refs_1_), channel_id=1, source_target_pairs={{0,8},{8,0},{16,24},{24,16},{1,9},{9,1},{17,25},{25,17},{2,10},{10... | collective-permute-start | bytes 7864328 | tf_op jit(solution)/shard_map/ppermute | solution.py:324
  832.5 124.2 %collective-permute-start.43 = (bf16[1024,2048]{1,0:T(8,128)(2,1)}, bf16[1024,2048]{1,0:T(8,128)(2,1)}, u32[]{:S(2)}, u32[]{:S(2)}) collective-permute-start(bf16[1024,2048]{1,0:T(8,128)(2,1)} %up_grad_other.1), channel_id=1, source_target_pairs={{0,16},{16,0},{8,24},{24,8},{1,17},{17,1},{9,25},{25,9},{2,18},{18... | collective-permute-start | bytes 12582920 | tf_op jit(solution)/shard_map/ppermute | solution.py:328
  834.2 102.0 %collective-permute-start.41 = (bf16[2560,512]{1,0:T(8,128)(2,1)}, bf16[2560,512]{1,0:T(8,128)(2,1)}, u32[]{:S(2)}, u32[]{:S(2)}) collective-permute-start(bf16[2560,512]{1,0:T(8,128)(2,1)} %get-tuple-element.168), channel_id=1, source_target_pairs={{0,8},{8,0},{16,24},{24,16},{1,9},{9,1},{17,25},{25,17},{2,10},{10... | collective-permute-start | bytes 7864328 | tf_op jit(solution)/shard_map/ppermute | solution.py:324
  880.4 261.1 %reduce-scatter.9.cloned.1.call-start = ((), (), s32[]{:S(2)}) async-start(), calls=%async_computation.13 | async-start | bytes 5242880 | tf_op jit(solution)/shard_map/reduce_scatter | solution.py:1097
  991.0 59.2 %collective-permute-start.46 = (bf16[2560,512]{1,0:T(8,128)(2,1)}, bf16[2560,512]{1,0:T(8,128)(2,1)}, u32[]{:S(2)}, u32[]{:S(2)}) collective-permute-start(bf16[2560,512]{1,0:T(8,128)(2,1)} %add_convert_fusion.4), channel_id=1, source_target_pairs={{0,1},{1,0},{2,3},{3,2},{4,5},{5,4},{6,7},{7,6},{8,9},{9,8},{10,11... | collective-permute-start | bytes 7864328 | tf_op jit(solution)/shard_map/ppermute | solution.py:332
  993.0 125.6 %all-to-all-start.2 = ((bf16[4,640,512]{2,1,0:T(8,128)(2,1)}), bf16[4,640,512]{2,1,0:T(8,128)(2,1)S(1)}, u32[]{:S(2)}, u32[]{:S(2)}) async-start(bf16[4,640,512]{2,1,0:T(8,128)(2,1)} %bitcast.207), calls=%async_computation.2 | async-start | bytes 5242880 | tf_op jit(solution)/shard_map/all_to_all | solution.py:1180
  996.7 215.4 %reduce-scatter.11.cloned.1.call-start = ((), (), s32[]{:S(2)}) async-start(), calls=%async_computation.14 | async-start | bytes 3932160 | tf_op jit(solution)/shard_map/reduce_scatter | solution.py:1218
  1056.8 70.3 %collective-permute-start.51 = (bf16[2,2,2,384,512]{4,3,2,1,0:T(8,128)(2,1)}, bf16[2,2,2,384,512]{4,3,2,1,0:T(8,128)(2,1)}, u32[]{:S(2)}, u32[]{:S(2)}) collective-permute-start(bf16[2,2,2,384,512]{4,3,2,1,0:T(8,128)(2,1)} %pad_maximum_fusion), channel_id=1, source_target_pairs={{0,16},{16,0},{8,24},{24,8},{1,17},{17,1},{9,25},{25,9},{2,18},{18... | collective-permute-start | bytes 9437192 | tf_op jit(solution)/shard_map/ppermute | solution.py:328
  1184.0 66.2 %all-to-all-start.3 = ((bf16[4,640,512]{2,1,0:T(8,128)(2,1)}), bf16[4,640,512]{2,1,0:T(8,128)(2,1)}, u32[]{:S(2)}, u32[]{:S(2)}) async-start(bf16[4,640,512]{2,1,0:T(8,128)(2,1)} %bitcast.203), calls=%async_computation.5 | async-start | bytes 5242880 | tf_op jit(solution)/shard_map/all_to_all | solution.py:1208
  (109 other events, 1786.6 us)
Sparse Core Ops, SparseCore 0:
  62.7 79.0 all-gather.13
  153.2 28.3 all-gather.15
  183.8 108.1 all-gather.7
  301.0 86.9 all-gather.9
  391.6 78.8 all-gather.11
  762.3 75.3 reduce-scatter.4
  880.5 75.2 reduce-scatter.6
  993.1 121.9 reduce-scatter.8
  1135.9 58.8 reduce-scatter.10

commit v6 on v5

--- a/solution.py
+++ b/solution.py
@@ -1166,17 +1166,18 @@
         TRUNK, LEAF_BEGIN, block,
     )
     output = low(after(middle, qkv_grad) + collect_col(out_own, out_got, out_outgoing))
-    up_total = low(wide(after(up_own, output)) + wide(swap_x(up_other)))
-    up_sum = to_row(up_total)
     parts = rows_call(
         project_back_kernel,
         2 * block,
-        [after(qkv_grad, up_total)],
+        [after(qkv_grad, output)],
         [w_near, w_far],
         [(quarter, jnp.bfloat16)] * 4,
         2 * rows * features * groups * 4 * HEAD,
         "project_back",
     )
+    up_total = low(wide(after(up_own, parts[0])) + wide(swap_x(up_other)))
+    up_sum = to_row(up_total)
+    parts[1] = after(parts[1], up_total)
     output_tree = lax.all_to_all(output, "row", 0, 0, tiled=True)
     own, got, outgoing = collect_core(parts)
     project_grad = weight_grad(

time: 1300 us -> 1290 us (level)
  transfers between devices with their start and end apart: 82 -> 82, of which waited for: 36 -> 35; matrix products, arithmetic and copies ran while one was open for 14% -> 15% of each run, Pallas kernels for 29% -> 29%
where the time goes in v6:
time: 1290 us; the launch traced here: 1280 us
  waiting for transfers between devices  496 us (38%)
  Pallas kernels  485 us (38%)
  other arithmetic  142 us (11%)
  local copies, waits for them, and re-layouts  73.6 us (6%)
  starting transfers between devices  70.5 us (5%)
  between operations  15.2 us (1%)
    ppermute x18, waiting for transfers between devices, swap_col(): return lax.ppermute(a, 'col', COL_SWAP)  241 us
    pallas_call x8, Pallas kernels, rows_call(): pl.pallas_call(fn, grid=(rows // block,), in_specs=in_specs, out_specs=[p...  226 us
    ppermute x13, waiting for transfers between devices, swap_x(): return lax.ppermute(a, 'dp', X_SWAP)  120 us
    pallas_call x5, Pallas kernels, weight_grad(): pl.pallas_call(functools.partial(weight_grad_kernel, len(bs), split), gri...  79.5 us
    convert_element_type x12, other arithmetic, low(): return a.astype(jnp.bfloat16)  59.7 us
    pallas_call x1, Pallas kernels, attend_back(): pl.pallas_call(functools.partial(attend_back_kernel, trunk, leaf_begin, b...  56.3 us
    pallas_call x3, Pallas kernels, turned_grad(): pl.pallas_call(functools.partial(turned_grad_kernel, len(bs)), grid_spec=...  51.8 us
    all_to_all x1, waiting for transfers between devices, tree_body(): output_tree = lax.all_to_all(output, 'row', 0, 0, tiled=True)  43.6 us
  transfers between devices with their start and end apart: 82, of which 35 were waited for; matrix products, arithmetic and copies ran while one was open for 15% of the time, Pallas kernels for 29%

profile of v6, /device:TPU:0, one launch (start us, length us, event | category | flops | bytes accessed | tf_op | source)
XLA Modules:
  0.0 1282.0 jit_solution(2201329288700672333)
XLA Ops:
  62.3 13.1 %collective-permute-done.2 = bf16[896,1024]{1,0:T(8,128)(2,1)} collective-permute-done((bf16[896,1024]{1,0:T(8,128)(2,1)}, bf16[896,1024]{1,0:T(8,128)(2,1)}, u32[]{:S(2)}, u32[]{:S(2)}) %collective-permute-start.2) | collective-permute-done | bytes 1835040 | tf_op jit(solution)/shard_map/ppermute | solution.py:332
  95.0 18.0 %collective-permute-done.3 = bf16[768,1024]{1,0:T(8,128)(2,1)} collective-permute-done((bf16[768,1024]{1,0:T(8,128)(2,1)}, bf16[768,1024]{1,0:T(8,128)(2,1)}, u32[]{:S(2)}, u32[]{:S(2)}) %collective-permute-start.3) | collective-permute-done | bytes 1572896 | tf_op jit(solution)/shard_map/ppermute | solution.py:332
  117.9 23.9 %all-gather.14.cloned.1.call-done = bf16[8,256,512]{2,1,0:T(8,128)(2,1)} async-done(((bf16[2,256,512]{2,1,0:T(8,128)(2,1)}), bf16[8,256,512]{2,1,0:T(8,128)(2,1)}) %all-gather.14.cloned.1.call-update) | async-done | bytes 2097168 | tf_op jit(solution)/shard_map/all_gather | solution.py:970
  141.8 11.3 all-to-all-done
  155.8 55.8 %collective-permute-done.6.x1 = bf16[2560,512]{1,0:T(8,128)(2,1)} collective-permute-done((bf16[2560,512]{1,0:T(8,128)(2,1)S(1)}, bf16[2560,512]{1,0:T(8,128)(2,1)}, u32[]{:S(2)}, u32[]{:S(2)}) %collective-permute-start.6) | collective-permute-done | bytes 2621472 | tf_op jit(solution)/shard_map/ppermute | solution.py:332
  231.7 20.2 %project.1 = (bf16[2560,2048]{1,0:T(8,128)(2,1)}, bf16[2560,1024]{1,0:T(8,128)(2,1)}, f32[2560,1]{1,0:T(8,128)}) custom-call(bf16[2560,512]{1,0:T(8,128)(2,1)} %bitcast.192, bf16[2560,512]{1,0:T(8,128)(2,1)} %collective-permute-done.6.x1, bf16[2560,512]{1,0:T(8,128)(2,1)} %collective-permute-done.7.x2, bf16[2560,512]{1,0:T(8,128)(2,1)} %collective-permute-done.8.x3, ...), custom_call_target="tpu_custom_call" | custom-call | flops 1342177280 | bytes 4131072 | tf_op jit(solution)/shard_map/project/pallas_call | solution.py:372
  256.4 34.4 %attend.1 = (bf16[2560,512]{1,0:T(8,128)(2,1)}, f32[2,10,1,512]{3,2,1,0:T(1,128)}) custom-call(bf16[2560,1024]{1,0:T(8,128)(2,1)} %get-tuple-element.112.q_ref.k_ref.v_ref, bf16[2560,1024]{1,0:T(8,128)(2,1)} %get-tuple-element.112.q_ref.k_ref.v_ref, bf16[2560,1024]{1,0:T(8,128)(2,1)} %get-tuple-element.112.q_ref.k_ref.v_ref, s32[2560,1]{1,0:T(8,128)} %copy.90.lab_ref, ...), custom_call_target="tpu_custom_call" | custom-call | flops 3355443200 | bytes 1638400 | tf_op jit(solution)/shard_map/attend/pallas_call | solution.py:585
  305.9 17.6 %all-to-all-done.1 = bf16[4,640,512]{2,1,0:T(8,128)(2,1)} async-done(((bf16[4,640,512]{2,1,0:T(8,128)(2,1)}), bf16[4,640,512]{2,1,0:T(8,128)(2,1)}, u32[]{:S(2)}, u32[]{:S(2)}) %all-to-all-start.1) | async-done | bytes 2621472 | tf_op jit(solution)/shard_map/all_to_all | solution.py:1055
  330.1 55.5 %collective-permute-done.16 = bf16[2560,512]{1,0:T(8,128)(2,1)S(1)} collective-permute-done((bf16[2560,512]{1,0:T(8,128)(2,1)S(1)}, bf16[2560,512]{1,0:T(8,128)(2,1)S(1)}, u32[]{:S(2)}, u32[]{:S(2)}) %collective-permute-start.16) | collective-permute-done | bytes 2621472 | tf_op jit(solution)/shard_map/ppermute | solution.py:332
  401.1 56.3 %collective-permute-done.21.refs_1_.refs_2_ = bf16[2560,512]{1,0:T(8,128)(2,1)S(1)} collective-permute-done((bf16[2560,512]{1,0:T(8,128)(2,1)}, bf16[2560,512]{1,0:T(8,128)(2,1)S(1)}, u32[]{:S(2)}, u32[]{:S(2)}) %collective-permute-start.21) | collective-permute-done | bytes 2621472 | tf_op jit(solution)/shard_map/ppermute | solution.py:332
  459.2 11.4 all-gather.12.cloned.1.call-done.in_ref.refs_8_.refs_2_
  476.4 53.0 %gate_up.1 = (bf16[2560,1024]{1,0:T(8,128)(2,1)}, bf16[2560,1024]{1,0:T(8,128)(2,1)}, bf16[2560,1024]{1,0:T(8,128)(2,1)}, bf16[2560,1024]{1,0:T(8,128)(2,1)}) custom-call(bf16[2560,512]{1,0:T(8,128)(2,1)} %multiply_convert_fusion.refs_0_.refs_1_, bf16[2560,512]{1,0:T(8,128)(2,1)} %copy-done.4, bf16[2560,512]{1,0:T(8,128)(2,1)} %collective-permute-done.25.refs_2_.refs_3_, ...), custom_call_target="tpu_custom_call" | custom-call | flops 5368709120 | bytes 6029312 | tf_op jit(solution)/shard_map/gate_up/pallas_call | solution.py:372
  530.0 15.1 %collective-permute-done.28.refs_10_.refs_4_ = bf16[768,2048]{1,0:T(8,128)(2,1)} collective-permute-done((bf16[768,2048]{1,0:T(8,128)(2,1)}, bf16[768,2048]{1,0:T(8,128)(2,1)}, u32[]{:S(2)}, u32[]{:S(2)}) %collective-permute-start.28) | collective-permute-done | bytes 3145760 | tf_op jit(solution)/shard_map/ppermute | solution.py:328
  547.4 37.0 %hidden.1 = (bf16[2560,1024]{1,0:T(8,128)(2,1)}, bf16[2560,1024]{1,0:T(8,128)(2,1)}, bf16[2560,1024]{1,0:T(8,128)(2,1)}, bf16[2560,1024]{1,0:T(8,128)(2,1)}, bf1...) custom-call(bf16[2560,512]{1,0:T(8,128)(2,1)} %bitcast.39.refs_0_.refs_1_, ...), custom_call_target="tpu_custom_call" | custom-call | flops 2684354560 | bytes 8912896 | tf_op jit(solution)/shard_map/hidden/pallas_call | solution.py:372
  584.4 17.1 %down_grad_other.1 = bf16[1024,2048]{1,0:T(8,128)(2,1)} custom-call(s32[1]{0:T(128)} %bitcast.40.where_ref, bf16[2560,1024]{1,0:T(8,128)(2,1)} %get-tuple-element.141.refs_0_.refs_1_, bf16[2560,512]{1,0:T(8,128)(2,1)} %bitcast.39.refs_0_.refs_1_, bf16[2560,512]{1,0:T(8,128)(2,1)} %collective-permute-done.22.refs_1_.refs_2_, bf16[2560,512]{1,0:T(8,128)(2,1)} %copy-done.5, ...), custom_call_target="tpu_custom_call" | custom-call | flops 1342177280 | bytes 2490368 | tf_op jit(solution)/shard_map/down_grad_other/pallas_call | solution.py:761
  601.6 52.8 %pair_back.1 = (bf16[2560,512]{1,0:T(8,128)(2,1)}, bf16[2560,512]{1,0:T(8,128)(2,1)}, bf16[2560,512]{1,0:T(8,128)(2,1)}, bf16[2560,512]{1,0:T(8,128)(2,1)}) custom-call(bf16[2560,1024]{1,0:T(8,128)(2,1)} %get-tuple-element.154.refs_0_, bf16[2560,1024]{1,0:T(8,128)(2,1)} %get-tuple-element.158.refs_1_.refs_0_, ...), custom_call_target="tpu_custom_call" | custom-call | flops 5368709120 | bytes 6029312 | tf_op jit(solution)/shard_map/pair_back/pallas_call | solution.py:372
  656.0 17.1 %gate_grad_other.1 = bf16[1024,2048]{1,0:T(8,128)(2,1)} custom-call(s32[1]{0:T(128)} %bitcast.40.where_ref, bf16[2560,1024]{1,0:T(8,128)(2,1)} %get-tuple-element.148.refs_2_.refs_0_, bf16[2560,512]{1,0:T(8,128)(2,1)} %multiply_convert_fusion.refs_0_.refs_1_, bf16[2560,512]{1,0:T(8,128)(2,1)} %copy-done.4, ...), custom_call_target="tpu_custom_call" | custom-call | flops 1342177280 | bytes 2490368 | tf_op jit(solution)/shard_map/gate_grad_other/pallas_call | solution.py:761
  673.1 17.5 %down_grad_mine.1 = bf16[1024,2048]{1,0:T(8,128)(2,1)} custom-call(bf16[2560,1024]{1,0:T(8,128)(2,1)} %get-tuple-element.159.refs_0_, bf16[2560,512]{1,0:T(8,128)(2,1)} %bitcast.39.refs_0_.refs_1_, bf16[2560,512]{1,0:T(8,128)(2,1)} %collective-permute-done.22.refs_1_.refs_2_, bf16[2560,512]{1,0:T(8,128)(2,1)} %copy-done.5, bf16[2560,512]{1,0:T(8,128)(2,1)} %copy-done.6), custom_call_target="tpu_custom_call" | custom-call | flops 1342177280 | bytes 2490368 | tf_op jit(solution)/shard_map/down_grad_mine/pallas_call | solution.py:848
  694.4 17.5 %up_grad_other.1 = bf16[1024,2048]{1,0:T(8,128)(2,1)} custom-call(s32[1]{0:T(128)} %bitcast.40.where_ref, bf16[2560,1024]{1,0:T(8,128)(2,1)} %get-tuple-element.153.refs_3_.refs_0_, bf16[2560,512]{1,0:T(8,128)(2,1)} %multiply_convert_fusion.refs_0_.refs_1_, bf16[2560,512]{1,0:T(8,128)(2,1)} %copy-done.4, ...), custom_call_target="tpu_custom_call" | custom-call | flops 1342177280 | bytes 2490368 | tf_op jit(solution)/shard_map/up_grad_other/pallas_call | solution.py:761
  712.0 17.6 %gate_grad_mine.1 = bf16[1024,2048]{1,0:T(8,128)(2,1)} custom-call(bf16[2560,1024]{1,0:T(8,128)(2,1)} %get-tuple-element.154.refs_0_, bf16[2560,512]{1,0:T(8,128)(2,1)} %multiply_convert_fusion.refs_0_.refs_1_, bf16[2560,512]{1,0:T(8,128)(2,1)} %copy-done.4, bf16[2560,512]{1,0:T(8,128)(2,1)} %collective-permute-done.25.refs_2_.refs_3_, ...), custom_call_target="tpu_custom_call" | custom-call | flops 1342177280 | bytes 2490368 | tf_op jit(solution)/shard_map/gate_grad_mine/pallas_call | solution.py:848
  729.5 18.2 %collective-permute-done.30 = bf16[1024,2048]{1,0:T(8,128)(2,1)} collective-permute-done((bf16[1024,2048]{1,0:T(8,128)(2,1)}, bf16[1024,2048]{1,0:T(8,128)(2,1)}, u32[]{:S(2)}, u32[]{:S(2)}) %collective-permute-start.30) | collective-permute-done | bytes 4194336 | tf_op jit(solution)/shard_map/ppermute | solution.py:328
  776.4 17.4 %up_grad_mine.1 = bf16[1024,2048]{1,0:T(8,128)(2,1)} custom-call(bf16[2560,1024]{1,0:T(8,128)(2,1)} %get-tuple-element.158.refs_1_.refs_0_, bf16[2560,512]{1,0:T(8,128)(2,1)} %multiply_convert_fusion.refs_0_.refs_1_, bf16[2560,512]{1,0:T(8,128)(2,1)} %copy-done.4, bf16[2560,512]{1,0:T(8,128)(2,1)} %collective-permute-done.25.refs_2_.refs_3_, ...), custom_call_target="tpu_custom_call" | custom-call | flops 1342177280 | bytes 2490368 | tf_op jit(solution)/shard_map/up_grad_mine/pallas_call | solution.py:848
  793.8 27.7 %down.1 = (bf16[2560,512]{1,0:T(8,128)(2,1)}, bf16[2560,512]{1,0:T(8,128)(2,1)}, bf16[2560,512]{1,0:T(8,128)(2,1)}, bf16[2560,512]{1,0:T(8,128)(2,1)}) custom-call(bf16[2560,1024]{1,0:T(8,128)(2,1)} %get-tuple-element.159.refs_0_, bf16[2560,1024]{1,0:T(8,128)(2,1)} %get-tuple-element.141.refs_0_.refs_1_, ...), custom_call_target="tpu_custom_call" | custom-call | flops 2684354560 | bytes 3670016 | tf_op jit(solution)/shard_map/down/pallas_call | solution.py:372
  851.3 15.5 %collective-permute-done.39 = bf16[1024,2048]{1,0:T(8,128)(2,1)} collective-permute-done((bf16[1024,2048]{1,0:T(8,128)(2,1)}, bf16[1024,2048]{1,0:T(8,128)(2,1)}, u32[]{:S(2)}, u32[]{:S(2)}) %collective-permute-start.39) | collective-permute-done | bytes 4194336 | tf_op jit(solution)/shard_map/ppermute | solution.py:328
  880.8 56.3 %attend_back.1.d_ref.refs_1_ = bf16[2560,1024]{1,0:T(8,128)(2,1)} custom-call(bf16[2560,1024]{1,0:T(8,128)(2,1)} %get-tuple-element.112.q_ref.k_ref.v_ref, bf16[2560,1024]{1,0:T(8,128)(2,1)} %get-tuple-element.112.q_ref.k_ref.v_ref, bf16[2560,1024]{1,0:T(8,128)(2,1)} %get-tuple-element.112.q_ref.k_ref.v_ref, ...), custom_call_target="tpu_custom_call" | custom-call | flops 8388608000 | bytes 3276800 | tf_op jit(solution)/shard_map/attend_back/pallas_call | solution.py:608
  943.5 15.9 %project_back.1 = (bf16[2560,512]{1,0:T(8,128)(2,1)}, bf16[2560,512]{1,0:T(8,128)(2,1)}, bf16[2560,512]{1,0:T(8,128)(2,1)}, bf16[2560,512]{1,0:T(8,128)(2,1)}) custom-call(bf16[2560,1024]{1,0:T(8,128)(2,1)} %attend_back.1.d_ref.refs_1_, bf16[2,1024,512]{2,1,0:T(8,128)(2,1)} %bitcast.199, bf16[2,1024,512]{2,1,0:T(8,128)(2,1)} %bitcast.29.far_ref), custom_call_target="tpu_custom_call" | custom-call | flops 1342177280 | bytes 2490368 | tf_op jit(solution)/shard_map/project_back/pallas_call | solution.py:372
  959.5 11.2 collective-permute-done.43
  987.9 15.9 %project_grad.1 = bf16[2,2048,512]{2,1,0:T(8,128)(2,1)} custom-call(bf16[2560,2048]{1,0:T(8,128)(2,1)} %get-tuple-element.173.refs_0_, bf16[2560,1024]{1,0:T(8,128)(2,1)} %attend_back.1.d_ref.refs_1_), custom_call_target="tpu_custom_call" | custom-call | flops 1342177280 | bytes 2490368 | tf_op jit(solution)/shard_map/project_grad/pallas_call | solution.py:848
  1003.8 11.2 mix_grad.1
  1025.7 15.9 %collective-permute-done.46 = bf16[2560,512]{1,0:T(8,128)(2,1)} collective-permute-done((bf16[2560,512]{1,0:T(8,128)(2,1)}, bf16[2560,512]{1,0:T(8,128)(2,1)}, u32[]{:S(2)}, u32[]{:S(2)}) %collective-permute-start.46) | collective-permute-done | bytes 2621472 | tf_op jit(solution)/shard_map/ppermute | solution.py:332
  1065.1 43.6 %all-to-all-done.2 = bf16[4,640,512]{2,1,0:T(8,128)(2,1)S(1)} async-done(((bf16[4,640,512]{2,1,0:T(8,128)(2,1)}), bf16[4,640,512]{2,1,0:T(8,128)(2,1)S(1)}, u32[]{:S(2)}, u32[]{:S(2)}) %all-to-all-start.2) | async-done | bytes 2621472 | tf_op jit(solution)/shard_map/all_to_all | solution.py:1181
  1134.3 41.1 %collective-permute-done.56.refs_2_ = bf16[2,512,1024]{2,1,0:T(8,128)(2,1)} collective-permute-done((bf16[2,512,1024]{2,1,0:T(8,128)(2,1)S(1)}, bf16[2,512,1024]{2,1,0:T(8,128)(2,1)}, u32[]{:S(2)}, u32[]{:S(2)}) %collective-permute-start.56) | collective-permute-done | bytes 2097184 | tf_op jit(solution)/shard_map/ppermute | solution.py:328
  (438 shorter events, 414.6 us)
Async XLA Ops:
  54.8 98.2 %all-to-all-start = ((bf16[4,640,512]{2,1,0:T(8,128)(2,1)}), bf16[4,640,512]{2,1,0:T(8,128)(2,1)S(1)}, u32[]{:S(2)}, u32[]{:S(2)}) async-start(bf16[4,640,512]{2,1,0:T(8,128)(2,1)} %bitcast.205), calls=%async_computation | async-start | bytes 5242880 | tf_op jit(solution)/shard_map/all_to_all | solution.py:959
  59.7 82.1 %all-gather.14.cloned.1.call-start = ((), (), s32[]{:S(2)}) async-start(), calls=%async_computation.15 | async-start | bytes 2621440 | tf_op jit(solution)/shard_map/all_gather | solution.py:970
  62.2 156.5 %all-gather.16.cloned.1.call-start = ((), (), s32[]{:S(2)}) async-start(), calls=%async_computation.16 | async-start | bytes 1310720 | tf_op jit(solution)/shard_map/all_gather | solution.py:1015
  153.1 148.4 %all-gather.8.cloned.1.call-start = ((), (), s32[]{:S(2)}) async-start(), calls=%async_computation.8 | async-start | bytes 5242880 | tf_op jit(solution)/shard_map/all_gather | solution.py:1016
  153.6 58.0 %collective-permute-start.6 = (bf16[2560,512]{1,0:T(8,128)(2,1)S(1)}, bf16[2560,512]{1,0:T(8,128)(2,1)}, u32[]{:S(2)}, u32[]{:S(2)}) collective-permute-start(bf16[2560,512]{1,0:T(8,128)(2,1)S(1)} %bitcast.190), channel_id=1, source_target_pairs={{0,1},{1,0},{2,3},{3,2},{4,5},{5,4},{6,7},{7,6},{8,9},{9,8},{10,11... | collective-permute-start | bytes 7864328 | tf_op jit(solution)/shard_map/ppermute | solution.py:332
  155.7 76.0 %collective-permute-start.7 = (bf16[2560,512]{1,0:T(8,128)(2,1)S(1)}, bf16[2560,512]{1,0:T(8,128)(2,1)}, u32[]{:S(2)}, u32[]{:S(2)}) collective-permute-start(bf16[2560,512]{1,0:T(8,128)(2,1)S(1)} %bitcast.191), channel_id=1, source_target_pairs={{0,8},{8,0},{16,24},{24,16},{1,9},{9,1},{17,25},{25,17},{2,10},{10... | collective-permute-start | bytes 7864328 | tf_op jit(solution)/shard_map/ppermute | solution.py:324
  227.0 96.5 %all-to-all-start.1 = ((bf16[4,640,512]{2,1,0:T(8,128)(2,1)}), bf16[4,640,512]{2,1,0:T(8,128)(2,1)}, u32[]{:S(2)}, u32[]{:S(2)}) async-start(bf16[4,640,512]{2,1,0:T(8,128)(2,1)} %bitcast.206), calls=%async_computation.1 | async-start | bytes 5242880 | tf_op jit(solution)/shard_map/all_to_all | solution.py:1055
  231.7 159.9 %all-gather.10.cloned.1.call-start = ((), (), s32[]{:S(2)}) async-start(), calls=%async_computation.9 | async-start | bytes 5242880 | tf_op jit(solution)/shard_map/all_gather | solution.py:1017
  300.9 169.6 %all-gather.12.cloned.1.call-start = ((), (), s32[]{:S(2)}) async-start(), calls=%async_computation.10 | async-start | bytes 5242880 | tf_op jit(solution)/shard_map/all_gather | solution.py:1018
  327.0 58.6 %collective-permute-start.16 = (bf16[2560,512]{1,0:T(8,128)(2,1)S(1)}, bf16[2560,512]{1,0:T(8,128)(2,1)S(1)}, u32[]{:S(2)}, u32[]{:S(2)}) collective-permute-start(bf16[2560,512]{1,0:T(8,128)(2,1)S(1)} %add_convert_fusion.8), channel_id=1, source_target_pairs={{0,1},{1,0},{2,3},{3,2},{4,5},{5,4},{6,7},{7,6},{8,9},{9,8},{10,11... | collective-permute-start | bytes 7864328 | tf_op jit(solution)/shard_map/ppermute | solution.py:332
  328.6 69.8 %collective-permute-start.20 = (bf16[768,2048]{1,0:T(8,128)(2,1)}, bf16[768,2048]{1,0:T(8,128)(2,1)}, u32[]{:S(2)}, u32[]{:S(2)}) collective-permute-start(bf16[768,2048]{1,0:T(8,128)(2,1)} %next_blocks.3), channel_id=1, source_target_pairs={{0,16},{16,0},{8,24},{24,8},{1,17},{17,1},{9,25},{25,9},{2,18},{18... | collective-permute-start | bytes 9437192 | tf_op jit(solution)/shard_map/ppermute | solution.py:328
  391.5 664.1 %reduce-scatter.5.cloned.1.call-start = ((), (), s32[]{:S(2)}) async-start(), calls=%async_computation.11 | async-start | bytes 5242880 | tf_op jit(solution)/shard_map/reduce_scatter | solution.py:1097
  398.4 59.0 %collective-permute-start.21 = (bf16[2560,512]{1,0:T(8,128)(2,1)}, bf16[2560,512]{1,0:T(8,128)(2,1)S(1)}, u32[]{:S(2)}, u32[]{:S(2)}) collective-permute-start(bf16[2560,512]{1,0:T(8,128)(2,1)} %multiply_convert_fusion.refs_0_.refs_1_), channel_id=1, source_target_pairs={{0,1},{1,0},{2,3},{3,2},{4,5},{5,4},{6,7},{7,6},{8,9},{9,8},{10,11... | collective-permute-start | bytes 7864328 | tf_op jit(solution)/shard_map/ppermute | solution.py:332
  399.7 76.8 %collective-permute-start.26 = (bf16[768,2048]{1,0:T(8,128)(2,1)}, bf16[768,2048]{1,0:T(8,128)(2,1)}, u32[]{:S(2)}, u32[]{:S(2)}) collective-permute-start(bf16[768,2048]{1,0:T(8,128)(2,1)} %next_blocks.4), channel_id=1, source_target_pairs={{0,16},{16,0},{8,24},{24,8},{1,17},{17,1},{9,25},{25,9},{2,18},{18... | collective-permute-start | bytes 9437192 | tf_op jit(solution)/shard_map/ppermute | solution.py:328
  457.9 71.5 %collective-permute-start.22 = (bf16[2560,512]{1,0:T(8,128)(2,1)}, bf16[2560,512]{1,0:T(8,128)(2,1)}, u32[]{:S(2)}, u32[]{:S(2)}) collective-permute-start(bf16[2560,512]{1,0:T(8,128)(2,1)} %bitcast.39.refs_0_.refs_1_), channel_id=1, source_target_pairs={{0,1},{1,0},{2,3},{3,2},{4,5},{5,4},{6,7},{7,6},{8,9},{9,8},{10,11... | collective-permute-start | bytes 7864328 | tf_op jit(solution)/shard_map/ppermute | solution.py:332
  474.9 70.2 %collective-permute-start.28 = (bf16[768,2048]{1,0:T(8,128)(2,1)}, bf16[768,2048]{1,0:T(8,128)(2,1)}, u32[]{:S(2)}, u32[]{:S(2)}) collective-permute-start(bf16[768,2048]{1,0:T(8,128)(2,1)} %next_blocks.5), channel_id=1, source_target_pairs={{0,16},{16,0},{8,24},{24,8},{1,17},{17,1},{9,25},{25,9},{2,18},{18... | collective-permute-start | bytes 9437192 | tf_op jit(solution)/shard_map/ppermute | solution.py:328
  476.4 68.7 %collective-permute-start.24 = (bf16[2560,512]{1,0:T(8,128)(2,1)}, bf16[2560,512]{1,0:T(8,128)(2,1)S(1)}, u32[]{:S(2)}, u32[]{:S(2)}) collective-permute-start(bf16[2560,512]{1,0:T(8,128)(2,1)} %bitcast.39.refs_0_.refs_1_), channel_id=1, source_target_pairs={{0,8},{8,0},{16,24},{24,16},{1,9},{9,1},{17,25},{25,17},{2,10},{10... | collective-permute-start | bytes 7864328 | tf_op jit(solution)/shard_map/ppermute | solution.py:324
  654.5 93.3 %collective-permute-start.30 = (bf16[1024,2048]{1,0:T(8,128)(2,1)}, bf16[1024,2048]{1,0:T(8,128)(2,1)}, u32[]{:S(2)}, u32[]{:S(2)}) collective-permute-start(bf16[1024,2048]{1,0:T(8,128)(2,1)} %down_grad_other.1), channel_id=1, source_target_pairs={{0,16},{16,0},{8,24},{24,8},{1,17},{17,1},{9,25},{25,9},{2,18},{18... | collective-permute-start | bytes 12582920 | tf_op jit(solution)/shard_map/ppermute | solution.py:328
  690.6 63.6 %collective-permute-start.31 = (bf16[2560,512]{1,0:T(8,128)(2,1)}, bf16[2560,512]{1,0:T(8,128)(2,1)}, u32[]{:S(2)}, u32[]{:S(2)}) collective-permute-start(bf16[2560,512]{1,0:T(8,128)(2,1)} %get-tuple-element.157), channel_id=1, source_target_pairs={{0,8},{8,0},{16,24},{24,16},{1,9},{9,1},{17,25},{25,17},{2,10},{10... | collective-permute-start | bytes 7864328 | tf_op jit(solution)/shard_map/ppermute | solution.py:324
  693.0 61.2 %collective-permute-start.32 = (bf16[2560,512]{1,0:T(8,128)(2,1)}, bf16[2560,512]{1,0:T(8,128)(2,1)}, u32[]{:S(2)}, u32[]{:S(2)}) collective-permute-start(bf16[2560,512]{1,0:T(8,128)(2,1)} %add_convert_fusion.7), channel_id=1, source_target_pairs={{0,1},{1,0},{2,3},{3,2},{4,5},{5,4},{6,7},{7,6},{8,9},{9,8},{10,11... | collective-permute-start | bytes 7864328 | tf_op jit(solution)/shard_map/ppermute | solution.py:332
  762.2 295.8 %reduce-scatter.7.cloned.1.call-start = ((), (), s32[]{:S(2)}) async-start(), calls=%async_computation.12 | async-start | bytes 5242880 | tf_op jit(solution)/shard_map/reduce_scatter | solution.py:1097
  773.2 58.8 %collective-permute-start.36 = (bf16[2560,512]{1,0:T(8,128)(2,1)S(1)}, bf16[2560,512]{1,0:T(8,128)(2,1)S(1)}, u32[]{:S(2)}, u32[]{:S(2)}) collective-permute-start(bf16[2560,512]{1,0:T(8,128)(2,1)S(1)} %get-tuple-element.179.h0.refs_1_), channel_id=1, source_target_pairs={{0,1},{1,0},{2,3},{3,2},{4,5},{5,4},{6,7},{7,6},{8,9},{9,8},{10,11... | collective-permute-start | bytes 7864328 | tf_op jit(solution)/shard_map/ppermute | solution.py:332
  775.0 91.8 %collective-permute-start.39 = (bf16[1024,2048]{1,0:T(8,128)(2,1)}, bf16[1024,2048]{1,0:T(8,128)(2,1)}, u32[]{:S(2)}, u32[]{:S(2)}) collective-permute-start(bf16[1024,2048]{1,0:T(8,128)(2,1)} %gate_grad_other.1), channel_id=1, source_target_pairs={{0,16},{16,0},{8,24},{24,8},{1,17},{17,1},{9,25},{25,9},{2,18},{18... | collective-permute-start | bytes 12582920 | tf_op jit(solution)/shard_map/ppermute | solution.py:328
  832.5 104.7 %collective-permute-start.41 = (bf16[2560,512]{1,0:T(8,128)(2,1)}, bf16[2560,512]{1,0:T(8,128)(2,1)}, u32[]{:S(2)}, u32[]{:S(2)}) collective-permute-start(bf16[2560,512]{1,0:T(8,128)(2,1)} %get-tuple-element.169), channel_id=1, source_target_pairs={{0,8},{8,0},{16,24},{24,16},{1,9},{9,1},{17,25},{25,17},{2,10},{10... | collective-permute-start | bytes 7864328 | tf_op jit(solution)/shard_map/ppermute | solution.py:324
  878.1 59.1 %collective-permute-start.42 = (bf16[2560,512]{1,0:T(8,128)(2,1)}, bf16[2560,512]{1,0:T(8,128)(2,1)}, u32[]{:S(2)}, u32[]{:S(2)}) collective-permute-start(bf16[2560,512]{1,0:T(8,128)(2,1)} %add_convert_fusion.6), channel_id=1, source_target_pairs={{0,1},{1,0},{2,3},{3,2},{4,5},{5,4},{6,7},{7,6},{8,9},{9,8},{10,11... | collective-permute-start | bytes 7864328 | tf_op jit(solution)/shard_map/ppermute | solution.py:332
  879.0 91.7 %collective-permute-start.43 = (bf16[1024,2048]{1,0:T(8,128)(2,1)}, bf16[1024,2048]{1,0:T(8,128)(2,1)}, u32[]{:S(2)}, u32[]{:S(2)}) collective-permute-start(bf16[1024,2048]{1,0:T(8,128)(2,1)} %up_grad_other.1), channel_id=1, source_target_pairs={{0,16},{16,0},{8,24},{24,8},{1,17},{17,1},{9,25},{25,9},{2,18},{18... | collective-permute-start | bytes 12582920 | tf_op jit(solution)/shard_map/ppermute | solution.py:328
  982.0 59.5 %collective-permute-start.46 = (bf16[2560,512]{1,0:T(8,128)(2,1)}, bf16[2560,512]{1,0:T(8,128)(2,1)}, u32[]{:S(2)}, u32[]{:S(2)}) collective-permute-start(bf16[2560,512]{1,0:T(8,128)(2,1)} %add_convert_fusion.4), channel_id=1, source_target_pairs={{0,1},{1,0},{2,3},{3,2},{4,5},{5,4},{6,7},{7,6},{8,9},{9,8},{10,11... | collective-permute-start | bytes 7864328 | tf_op jit(solution)/shard_map/ppermute | solution.py:332
  983.4 125.2 %all-to-all-start.2 = ((bf16[4,640,512]{2,1,0:T(8,128)(2,1)}), bf16[4,640,512]{2,1,0:T(8,128)(2,1)S(1)}, u32[]{:S(2)}, u32[]{:S(2)}) async-start(bf16[4,640,512]{2,1,0:T(8,128)(2,1)} %bitcast.207), calls=%async_computation.2 | async-start | bytes 5242880 | tf_op jit(solution)/shard_map/all_to_all | solution.py:1181
  987.1 145.9 %reduce-scatter.9.cloned.1.call-start = ((), (), s32[]{:S(2)}) async-start(), calls=%async_computation.13 | async-start | bytes 5242880 | tf_op jit(solution)/shard_map/reduce_scatter | solution.py:1097
  987.8 215.9 %reduce-scatter.11.cloned.1.call-start = ((), (), s32[]{:S(2)}) async-start(), calls=%async_computation.14 | async-start | bytes 3932160 | tf_op jit(solution)/shard_map/reduce_scatter | solution.py:1219
  1048.2 70.3 %collective-permute-start.51 = (bf16[2,2,2,384,512]{4,3,2,1,0:T(8,128)(2,1)}, bf16[2,2,2,384,512]{4,3,2,1,0:T(8,128)(2,1)}, u32[]{:S(2)}, u32[]{:S(2)}) collective-permute-start(bf16[2,2,2,384,512]{4,3,2,1,0:T(8,128)(2,1)} %pad_maximum_fusion), channel_id=1, source_target_pairs={{0,16},{16,0},{8,24},{24,8},{1,17},{17,1},{9,25},{25,9},{2,18},{18... | collective-permute-start | bytes 9437192 | tf_op jit(solution)/shard_map/ppermute | solution.py:328
  1175.4 65.4 %all-to-all-start.3 = ((bf16[4,640,512]{2,1,0:T(8,128)(2,1)}), bf16[4,640,512]{2,1,0:T(8,128)(2,1)}, u32[]{:S(2)}, u32[]{:S(2)}) async-start(bf16[4,640,512]{2,1,0:T(8,128)(2,1)} %bitcast.203), calls=%async_computation.5 | async-start | bytes 5242880 | tf_op jit(solution)/shard_map/all_to_all | solution.py:1209
  (109 other events, 1794.0 us)
Sparse Core Ops, SparseCore 0:
  62.7 79.0 all-gather.13
  153.2 28.3 all-gather.15
  183.8 108.1 all-gather.7
  301.0 86.9 all-gather.9
  391.6 78.8 all-gather.11
  762.3 75.3 reduce-scatter.4
  879.1 74.8 reduce-scatter.6
  990.8 120.9 reduce-scatter.8
  1127.3 57.9 reduce-scatter.10
